TPU v7x, 32 devices: a whole 2x2x4 slice. The times are simulated.
32 devices in a mesh: section: 4 (over x, core), expert: 8 (over z, y).
Axes of the slice: x: 2, y: 2, z: 4, core: 2. Of those that a mesh axis runs over, the one named last changes fastest.
Arguments:
- inputs: bfloat16 [4, 2, 512, 2048], P('section', None, 'expert'), may hold values from -6 to 6
- routes: int32 [4, 2, 512, 10], P('section', None, 'expert'), may hold values from 0 to 15, all different within a row; in each aligned block of 64 rows (0 to 63, 64 to 127, ..., all dimensions but the last counted through in order) at most 48 rows name the same one
- gates: float32 [4, 2, 512, 10], P('section', None, 'expert'), may hold values from 0.1 to 0.6
- cot_early: bfloat16 [4, 512, 2048], P('section', 'expert'), may hold values from -6 to 6
- head_grad: bfloat16 [512, 2048], P('expert'), may hold values from -6 to 6
- w_gate: bfloat16 [4, 16, 2048, 512], P('section', 'expert'), may hold values from -0.125 to 0.125
- w_up: bfloat16 [4, 16, 2048, 512], P('section', 'expert'), may hold values from -0.125 to 0.125
- w_down: bfloat16 [4, 16, 512, 2048], P('section', 'expert'), may hold values from -0.25 to 0.25
Outputs:
- grad_early: bfloat16 [4, 512, 2048], P('section', 'expert')
- grad_late: bfloat16 [4, 512, 2048], P('section', 'expert')
- grad_gate: bfloat16 [4, 16, 2048, 512], P('section', 'expert')
- grad_up: bfloat16 [4, 16, 2048, 512], P('section', 'expert')
- grad_down: bfloat16 [4, 16, 512, 2048], P('section', 'expert')
Inputs may be any that keep to these rules, and one draw needn't show every extreme that they name: `routes`: each row names 10 different experts. In each aligned block of 64 rows (one device's tokens of one micro-batch at one section) no expert is named by more than 48 rows, a bound that some block reaches.
All inputs are finite; a program needn't handle non-finite values.
Results may differ from a plain program's by a relative error of at most 0.008.
Values may be sent and summed in bfloat16 or wider, within the bound.
No kernel may reach another device: no remote copies, remote signals or barrier semaphores. Data moves between devices by JAX's collectives and lax.ppermute only.
A program may use at most 128 MiB of HBM per device.

v0:
```python
import jax
import jax.numpy as jnp
from jax import lax
from jax.sharding import PartitionSpec as P

TOPK = 10
CAP = 48


def shifted(x, axis, by):
    peers = lax.axis_size(axis)
    pairs = [(i, i + by) for i in range(peers) if 0 <= i + by < peers]
    return lax.ppermute(x, axis, pairs)


def swish_parts(gate_value):
    sigmoid_value = jax.nn.sigmoid(gate_value)
    swished = gate_value * sigmoid_value
    derivative = sigmoid_value * (1.0 + gate_value * (1.0 - sigmoid_value))
    return (swished, derivative)


def route_slots(route_ids, experts):
    flat_ids = route_ids.reshape(-1)
    row_count = flat_ids.shape[0]
    one_hot = (flat_ids[:, None] == jnp.arange(experts, dtype=jnp.int32)[None, :]).astype(jnp.int32)
    position = jnp.sum((jnp.cumsum(one_hot, axis=0) - 1) * one_hot, axis=1)
    slot_of = flat_ids * CAP + position
    source = (
        jnp.zeros((experts * CAP,), jnp.int32)
        .at[slot_of]
        .set(jnp.arange(row_count, dtype=jnp.int32))
    )
    marks = jnp.zeros((experts * CAP,), jnp.int32).at[slot_of].set(1)
    return (slot_of, source, marks > 0)


def pack_inputs(tokens_in, source, filled, owners):
    rows_out = jnp.where(filled[:, None], tokens_in[source // TOPK], jnp.zeros((), jnp.bfloat16))
    return rows_out.reshape(owners, -1, tokens_in.shape[-1])


def pack_grads(cotangent, gate_weights, source, filled, owners):
    weight_of = gate_weights.reshape(-1)[source]
    scaled = weight_of[:, None] * cotangent[source // TOPK].astype(jnp.float32)
    scaled = jnp.where(filled[:, None], scaled, jnp.zeros((), jnp.float32)).astype(jnp.bfloat16)
    return scaled.reshape(owners, -1, cotangent.shape[-1])


def send_pair(row_inputs, row_grads):
    return (
        lax.all_to_all(row_inputs, "expert", split_axis=0, concat_axis=0, tiled=True),
        lax.all_to_all(row_grads, "expert", split_axis=0, concat_axis=0, tiled=True),
    )


def expert_rows(row_inputs, row_grads, weight_gate, weight_up, weight_down):
    owners = row_inputs.shape[0]
    local = weight_gate.shape[0]
    width = row_inputs.shape[-1]
    row_inputs = row_inputs.reshape(owners, local, -1, width)
    row_grads = row_grads.reshape(owners, local, -1, width)
    gate_value = jnp.einsum(
        "sekd,edf->sekf", row_inputs, weight_gate, preferred_element_type=jnp.float32
    )
    up_value = jnp.einsum(
        "sekd,edf->sekf", row_inputs, weight_up, preferred_element_type=jnp.float32
    )
    swished, derivative = swish_parts(gate_value)
    hidden = (swished * up_value).astype(jnp.bfloat16)
    grad_hidden = jnp.einsum(
        "sekd,efd->sekf", row_grads, weight_down, preferred_element_type=jnp.float32
    )
    grad_gate_value = (grad_hidden * up_value * derivative).astype(jnp.bfloat16)
    grad_up_value = (grad_hidden * swished).astype(jnp.bfloat16)
    back_rows = jnp.einsum(
        "sekf,edf->sekd", grad_gate_value, weight_gate, preferred_element_type=jnp.float32
    ) + jnp.einsum("sekf,edf->sekd", grad_up_value, weight_up, preferred_element_type=jnp.float32)
    back_rows = back_rows.astype(jnp.bfloat16).reshape(owners, -1, width)
    return (back_rows, (row_inputs, row_grads, hidden, grad_gate_value, grad_up_value))


def weight_terms(saved):
    row_inputs, row_grads, hidden, grad_gate_value, grad_up_value = saved
    term_gate = jnp.einsum(
        "sekd,sekf->edf", row_inputs, grad_gate_value, preferred_element_type=jnp.float32
    )
    term_up = jnp.einsum(
        "sekd,sekf->edf", row_inputs, grad_up_value, preferred_element_type=jnp.float32
    )
    term_down = jnp.einsum("sekf,sekd->efd", hidden, row_grads, preferred_element_type=jnp.float32)
    return (term_gate, term_up, term_down)


def combine_rows(cotangent, back_rows, slot_of):
    returned = lax.all_to_all(back_rows, "expert", split_axis=0, concat_axis=0, tiled=True)
    flat_rows = returned.reshape(-1, cotangent.shape[-1])
    picked = (
        flat_rows[slot_of]
        .reshape(cotangent.shape[0], TOPK, cotangent.shape[-1])
        .astype(jnp.float32)
    )
    return (cotangent.astype(jnp.float32) + jnp.sum(picked, axis=1)).astype(jnp.bfloat16)


def on_device(inputs, routes, gates, cot_early, head_grad, w_gate, w_up, w_down):
    weight_gate, weight_up, weight_down = (w_gate[0], w_up[0], w_down[0])
    owners = lax.axis_size("expert")
    experts = weight_gate.shape[0] * owners
    section_index = lax.axis_index("section")
    top_section = lax.axis_size("section") - 1
    first_in, second_in = (inputs[0, 0], inputs[0, 1])
    first_gates, second_gates = (gates[0, 0], gates[0, 1])
    first_cot = cot_early[0]
    first_slot, first_source, first_filled = route_slots(routes[0, 0], experts)
    second_slot, second_source, second_filled = route_slots(routes[0, 1], experts)
    first_send = pack_inputs(first_in, first_source, first_filled, owners)
    second_send = pack_inputs(second_in, second_source, second_filled, owners)
    first_rows, first_grads = send_pair(
        first_send, pack_grads(first_cot, first_gates, first_source, first_filled, owners)
    )
    first_back, first_saved = expert_rows(
        first_rows, first_grads, weight_gate, weight_up, weight_down
    )
    first_terms = weight_terms(first_saved)
    grad_early = combine_rows(first_cot, first_back, first_slot)
    received = shifted(grad_early, "section", -1)
    second_cot = jnp.where(section_index == top_section, head_grad, received)
    second_pack = pack_grads(second_cot, second_gates, second_source, second_filled, owners)
    second_rows, second_grads = send_pair(second_send, second_pack)
    second_back, second_saved = expert_rows(
        second_rows, second_grads, weight_gate, weight_up, weight_down
    )
    second_terms = weight_terms(second_saved)
    grad_late = combine_rows(second_cot, second_back, second_slot)
    grad_gate = (first_terms[0] + second_terms[0]).astype(jnp.bfloat16)
    grad_up = (first_terms[1] + second_terms[1]).astype(jnp.bfloat16)
    grad_down = (first_terms[2] + second_terms[2]).astype(jnp.bfloat16)
    return (grad_early[None], grad_late[None], grad_gate[None], grad_up[None], grad_down[None])


def solution(mesh):
    in_specs = (
        P("section", None, "expert", None),
        P("section", None, "expert", None),
        P("section", None, "expert", None),
        P("section", "expert", None),
        P("expert", None),
        P("section", "expert", None, None),
        P("section", "expert", None, None),
        P("section", "expert", None, None),
    )
    out_specs = (
        P("section", "expert", None),
        P("section", "expert", None),
        P("section", "expert", None, None),
        P("section", "expert", None, None),
        P("section", "expert", None, None),
    )
    return jax.shard_map(
        on_device, mesh=mesh, in_specs=in_specs, out_specs=out_specs, check_vma=False
    )
```

profile of v0, /device:TPU:0, one launch (start us, length us, event | category | flops | bytes accessed | tf_op | source)
XLA Modules:
  0.0 518.0 jit_solution(12904323642616741064)
XLA Ops:
  21.4 7.4 %all-to-all-start.1 = ((bf16[8,96,2048]{2,1,0:T(8,128)(2,1)}), bf16[8,96,2048]{2,1,0:T(8,128)(2,1)}, u32[]{:S(2)}, u32[]{:S(2)}) async-start(bf16[8,96,2048]{2,1,0:T(8,128)(2,1)} %broadcast_select_fusion.1), calls=%async_computation.1 | async-start | bytes 6291456 | tf_op jit(solution)/shard_map/all_to_all | solution.py:52
  40.9 58.7 %all-to-all-done.1 = bf16[8,96,2048]{2,1,0:T(8,128)(2,1)} async-done(((bf16[8,96,2048]{2,1,0:T(8,128)(2,1)}), bf16[8,96,2048]{2,1,0:T(8,128)(2,1)}, u32[]{:S(2)}, u32[]{:S(2)}) %all-to-all-start.1) | async-done | bytes 3145760 | tf_op jit(solution)/shard_map/all_to_all | solution.py:52
  104.3 5.1 fusion.13
  109.4 5.4 %fusion.25 = f32[2,8,48,512]{3,2,1,0:T(8,128)} fusion(bf16[1,2,2048,512]{3,2,1,0:T(8,128)(2,1)S(1)} %copy-done.1, bf16[8,2,48,2048]{3,2,1,0:T(8,128)(2,1)} %bitcast.10), kind=kOutput, calls=%fused_computation.44 | convolution fusion | flops 1610612736 | bytes 8912896 | tf_op jit(solution)/shard_map/sekd,edf->sekf/dot_general | solution.py:66
  114.8 59.7 %all-to-all-done = bf16[8,96,2048]{2,1,0:T(8,128)(2,1)} async-done(((bf16[8,96,2048]{2,1,0:T(8,128)(2,1)}), bf16[8,96,2048]{2,1,0:T(8,128)(2,1)}, u32[]{:S(2)}, u32[]{:S(2)}) %all-to-all-start) | async-done | bytes 3145760 | tf_op jit(solution)/shard_map/all_to_all | solution.py:53
  174.5 6.1 %fusion.66 = (bf16[8,2,48,512]{3,2,0,1:T(8,128)(2,1)S(1)}, bf16[8,2,48,512]{3,2,0,1:T(8,128)(2,1)S(1)}) fusion(f32[2,8,48,512]{3,2,1,0:T(8,128)S(1)} %fusion.13, f32[2,8,48,512]{3,2,1,0:T(8,128)} %fusion.25, bf16[1,2,512,2048]{3,2,1,0:T(8,128)(2,1)} %param.15, bf16[8,2,48,2048]{3,2,1,0:T(8,128)(2,1)} %bitcast.3), kind=kOutput, calls=%fused_computation.91 | convolution fusion | flops 1615724544 | bytes 12058624 | tf_op jit(solution)/shard_map/sekd,efd->sekf/dot_general | solution.py:71
  210.6 51.3 %all-to-all-done.2 = bf16[8,96,2048]{2,1,0:T(8,128)(2,1)} async-done(((bf16[8,96,2048]{2,1,0:T(8,128)(2,1)}), bf16[8,96,2048]{2,1,0:T(8,128)(2,1)}, u32[]{:S(2)}, u32[]{:S(2)}) %all-to-all-start.2) | async-done | bytes 3145760 | tf_op jit(solution)/shard_map/all_to_all | solution.py:96
  266.6 8.6 %gather_fusion.3 = bf16[640,2048]{1,0:T(8,128)(2,1)S(1)} fusion(bf16[768,2048]{1,0:T(8,128)(2,1)} %bitcast.22, s32[1024]{0:T(1024)S(1)} %pad_clamp_fusion.3), kind=kCustom, calls=%fused_computation.3 | custom fusion | bytes 5245440 | tf_op jit(solution)/shard_map/gather | solution.py:99
  278.9 5.3 %reduce_sum.44 = f32[64,2048]{1,0:T(8,128)S(1)} reduce(f32[64,10,2048]{2,1,0:T(8,128)} %reshape.190, f32[]{:T(128)} %constant.47.clone.1), dimensions={1}, to_apply=%region_5.6 | reduce | flops 1179648 | bytes 5767172 | tf_op jit(solution)/shard_map/reduce_sum | solution.py:103
  297.9 38.9 %all-to-all-done.4 = bf16[8,96,2048]{2,1,0:T(8,128)(2,1)} async-done(((bf16[8,96,2048]{2,1,0:T(8,128)(2,1)}), bf16[8,96,2048]{2,1,0:T(8,128)(2,1)}, u32[]{:S(2)}, u32[]{:S(2)}) %all-to-all-start.4) | async-done | bytes 3145760 | tf_op jit(solution)/shard_map/all_to_all | solution.py:52
  336.8 4.9 all-to-all-start.3
  341.7 6.2 %fusion.21 = f32[2,8,48,512]{3,2,1,0:T(8,128)} fusion(bf16[1,2,2048,512]{3,2,1,0:T(8,128)(2,1)} %param.14, bf16[8,2,48,2048]{3,2,1,0:T(8,128)(2,1)} %bitcast.31), kind=kOutput, calls=%fused_computation.40 | convolution fusion | flops 1610612736 | bytes 8912896 | tf_op jit(solution)/shard_map/sekd,edf->sekf/dot_general | solution.py:66
  348.0 4.9 fusion.9
  352.8 7.5 %fusion.70 = f32[2,2048,512,1]{2,1,0,3:T(8,128)} fusion(bf16[8,2,48,2048]{3,2,1,0:T(8,128)(2,1)} %bitcast.10, bf16[8,2,48,512]{3,2,0,1:T(8,128)(2,1)S(1)} %copy-done.8), kind=kOutput, calls=%fused_computation.93 | convolution fusion | flops 1610612736 | bytes 12320768 | tf_op jit(solution)/shard_map/sekd,sekf->edf/dot_general | solution.py:88
  360.3 51.5 %all-to-all-done.3 = bf16[8,96,2048]{2,1,0:T(8,128)(2,1)} async-done(((bf16[8,96,2048]{2,1,0:T(8,128)(2,1)}), bf16[8,96,2048]{2,1,0:T(8,128)(2,1)}, u32[]{:S(2)}, u32[]{:S(2)}) %all-to-all-start.3) | async-done | bytes 3145760 | tf_op jit(solution)/shard_map/all_to_all | solution.py:53
  411.9 6.5 %fusion.57 = (bf16[8,2,48,512]{3,2,0,1:T(8,128)(2,1)S(1)}, bf16[8,2,48,512]{3,2,0,1:T(8,128)(2,1)S(1)}) fusion(f32[2,8,48,512]{3,2,1,0:T(8,128)} %fusion.9, f32[2,8,48,512]{3,2,1,0:T(8,128)} %fusion.21, bf16[1,2,512,2048]{3,2,1,0:T(8,128)(2,1)} %param.15, bf16[8,2,48,2048]{3,2,1,0:T(8,128)(2,1)} %bitcast.26), kind=kOutput, calls=%fused_computation.76 | convolution fusion | flops 1615724544 | bytes 12058624 | tf_op jit(solution)/shard_map/sekd,efd->sekf/dot_general | solution.py:71
  424.5 4.8 all-to-all-start.5
  429.3 7.6 %fusion.73 = f32[2,2048,512,1]{2,1,0,3:T(8,128)} fusion(bf16[8,2,48,2048]{3,2,1,0:T(8,128)(2,1)} %bitcast.10, bf16[8,2,48,512]{3,2,0,1:T(8,128)(2,1)S(1)} %copy-done.10), kind=kOutput, calls=%fused_computation.96 | convolution fusion | flops 1610612736 | bytes 12320768 | tf_op jit(solution)/shard_map/sekd,sekf->edf/dot_general | solution.py:85
  442.2 6.6 %fusion.27 = bf16[1,2,512,2048]{3,2,1,0:T(8,128)(2,1)} fusion(f32[2,512,2048,1]{2,1,3,0:T(8,128)S(1)} %fusion.46, bf16[8,2,48,2048]{3,2,1,0:T(8,128)(2,1)} %bitcast.26, f32[2,8,48,512]{3,2,1,0:T(8,128)S(1)} %copy-done.16, f32[2,8,48,512]{3,2,1,0:T(8,128)S(1)} %copy-done.17), kind=kOutput, calls=%fused_computation.46 | convolution fusion | flops 1617166336 | bytes 18874368 | tf_op jit(solution)/shard_map/sekf,sekd->efd/dot_general | solution.py:91
  448.8 8.7 %fusion.29 = bf16[1,2,2048,512]{3,2,1,0:T(8,128)(2,1)} fusion(bf16[8,2,48,2048]{3,2,1,0:T(8,128)(2,1)} %bitcast.31, f32[2,2048,512,1]{2,1,0,3:T(8,128)} %fusion.70, bf16[8,2,48,512]{3,2,0,1:T(8,128)(2,1)S(1)} %get-tuple-element.5), kind=kOutput, calls=%fused_computation.48 | convolution fusion | flops 1614807040 | bytes 16515072 | tf_op jit(solution)/shard_map/sekd,sekf->edf/dot_general | solution.py:88
  457.6 8.7 %fusion.28 = bf16[1,2,2048,512]{3,2,1,0:T(8,128)(2,1)} fusion(bf16[8,2,48,2048]{3,2,1,0:T(8,128)(2,1)} %bitcast.31, f32[2,2048,512,1]{2,1,0,3:T(8,128)} %fusion.73, bf16[8,2,48,512]{3,2,0,1:T(8,128)(2,1)S(1)} %get-tuple-element.6), kind=kOutput, calls=%fused_computation.47 | convolution fusion | flops 1614807040 | bytes 16515072 | tf_op jit(solution)/shard_map/sekd,sekf->edf/dot_general | solution.py:85
  466.3 32.9 %all-to-all-done.5 = bf16[8,96,2048]{2,1,0:T(8,128)(2,1)} async-done(((bf16[8,96,2048]{2,1,0:T(8,128)(2,1)}), bf16[8,96,2048]{2,1,0:T(8,128)(2,1)}, u32[]{:S(2)}, u32[]{:S(2)}) %all-to-all-start.5) | async-done | bytes 3145760 | tf_op jit(solution)/shard_map/all_to_all | solution.py:96
  499.2 8.8 %gather_fusion.7 = bf16[640,2048]{1,0:T(8,128)(2,1)S(1)} fusion(bf16[768,2048]{1,0:T(8,128)(2,1)} %bitcast.37, s32[1024]{0:T(1024)S(1)} %pad_clamp_fusion), kind=kCustom, calls=%fused_computation.7 | custom fusion | bytes 5245440 | tf_op jit(solution)/shard_map/gather | solution.py:99
  511.7 5.3 %reduce_sum.48 = f32[64,2048]{1,0:T(8,128)S(1)} reduce(f32[64,10,2048]{2,1,0:T(8,128)} %reshape.192, f32[]{:T(128)} %constant.47.clone.1), dimensions={1}, to_apply=%region_11.12 | reduce | flops 1179648 | bytes 5767172 | tf_op jit(solution)/shard_map/reduce_sum | solution.py:103
  (115 shorter events, 105.1 us)
Async XLA Ops:
  21.4 7.4 %copy-start = (bf16[1,64,2048]{2,1,0:T(8,128)(2,1)S(1)}, bf16[1,64,2048]{2,1,0:T(8,128)(2,1)}, u32[]{:S(2)}) copy-start(bf16[1,64,2048]{2,1,0:T(8,128)(2,1)} %param.11) | copy-start | bytes 786436
  21.4 78.2 %all-to-all-start.1 = ((bf16[8,96,2048]{2,1,0:T(8,128)(2,1)}), bf16[8,96,2048]{2,1,0:T(8,128)(2,1)}, u32[]{:S(2)}, u32[]{:S(2)}) async-start(bf16[8,96,2048]{2,1,0:T(8,128)(2,1)} %broadcast_select_fusion.1), calls=%async_computation.1 | async-start | bytes 6291456 | tf_op jit(solution)/shard_map/all_to_all | solution.py:52
  28.8 4.2 copy-start.12
  99.6 74.9 %all-to-all-start = ((bf16[8,96,2048]{2,1,0:T(8,128)(2,1)}), bf16[8,96,2048]{2,1,0:T(8,128)(2,1)}, u32[]{:S(2)}, u32[]{:S(2)}) async-start(bf16[8,96,2048]{2,1,0:T(8,128)(2,1)} %fusion.6), calls=%async_computation | async-start | bytes 6291456 | tf_op jit(solution)/shard_map/all_to_all | solution.py:53
  104.3 5.1 copy-start.1
  109.4 65.1 %copy-start.13 = (f32[2,8,48,512]{3,2,1,0:T(8,128)}, f32[2,8,48,512]{3,2,1,0:T(8,128)S(1)}, u32[]{:S(2)}) copy-start(f32[2,8,48,512]{3,2,1,0:T(8,128)S(1)} %fusion.13) | copy-start | bytes 4718596
  174.5 6.1 %copy-start.4 = (bf16[1,2,2048,512]{3,2,1,0:T(8,128)(2,1)S(1)}, bf16[1,2,2048,512]{3,2,1,0:T(8,128)(2,1)}, u32[]{:S(2)}) copy-start(bf16[1,2,2048,512]{3,2,1,0:T(8,128)(2,1)} %param.13) | copy-start | bytes 12582916
  180.6 1.9 copy-start.9
  180.6 2.7 copy-start.2
  187.3 74.6 %all-to-all-start.2 = ((bf16[8,96,2048]{2,1,0:T(8,128)(2,1)}), bf16[8,96,2048]{2,1,0:T(8,128)(2,1)}, u32[]{:S(2)}, u32[]{:S(2)}) async-start(bf16[8,96,2048]{2,1,0:T(8,128)(2,1)} %bitcast.249), calls=%async_computation.2 | async-start | bytes 6291456 | tf_op jit(solution)/shard_map/all_to_all | solution.py:96
  261.9 74.9 %all-to-all-start.4 = ((bf16[8,96,2048]{2,1,0:T(8,128)(2,1)}), bf16[8,96,2048]{2,1,0:T(8,128)(2,1)}, u32[]{:S(2)}, u32[]{:S(2)}) async-start(bf16[8,96,2048]{2,1,0:T(8,128)(2,1)} %broadcast_select_fusion), calls=%async_computation.4 | async-start | bytes 6291456 | tf_op jit(solution)/shard_map/all_to_all | solution.py:52
  284.2 5.0 copy-start.11
  284.3 5.0 collective-permute-start
  336.8 75.1 %all-to-all-start.3 = ((bf16[8,96,2048]{2,1,0:T(8,128)(2,1)}), bf16[8,96,2048]{2,1,0:T(8,128)(2,1)}, u32[]{:S(2)}, u32[]{:S(2)}) async-start(bf16[8,96,2048]{2,1,0:T(8,128)(2,1)} %fusion.4), calls=%async_computation.3 | async-start | bytes 6291456 | tf_op jit(solution)/shard_map/all_to_all | solution.py:53
  341.7 6.2 %copy-start.5 = (bf16[1,2,2048,512]{3,2,1,0:T(8,128)(2,1)S(1)}, bf16[1,2,2048,512]{3,2,1,0:T(8,128)(2,1)}, u32[]{:S(2)}) copy-start(bf16[1,2,2048,512]{3,2,1,0:T(8,128)(2,1)} %param.13) | copy-start | bytes 12582916
  348.0 4.9 copy-start.8
  411.9 6.5 %copy-start.6 = (bf16[1,2,2048,512]{3,2,1,0:T(8,128)(2,1)S(1)}, bf16[1,2,2048,512]{3,2,1,0:T(8,128)(2,1)}, u32[]{:S(2)}) copy-start(bf16[1,2,2048,512]{3,2,1,0:T(8,128)(2,1)} %param.13) | copy-start | bytes 12582916
  418.4 2.2 copy-start.3
  424.5 4.8 copy-start.10
  424.5 74.8 %all-to-all-start.5 = ((bf16[8,96,2048]{2,1,0:T(8,128)(2,1)}), bf16[8,96,2048]{2,1,0:T(8,128)(2,1)}, u32[]{:S(2)}, u32[]{:S(2)}) async-start(bf16[8,96,2048]{2,1,0:T(8,128)(2,1)} %bitcast.250), calls=%async_computation.5 | async-start | bytes 6291456 | tf_op jit(solution)/shard_map/all_to_all | solution.py:96
  429.3 7.7 %copy-start.14 = (f32[2,8,48,512]{3,2,1,0:T(8,128)S(1)}, f32[2,8,48,512]{3,2,1,0:T(8,128)}, u32[]{:S(2)}) copy-start(f32[2,8,48,512]{3,2,1,0:T(8,128)} %copy-done.13) | copy-start | bytes 4718596
  429.3 7.6 %copy-start.15 = (f32[2,8,48,512]{3,2,1,0:T(8,128)S(1)}, f32[2,8,48,512]{3,2,1,0:T(8,128)}, u32[]{:S(2)}) copy-start(f32[2,8,48,512]{3,2,1,0:T(8,128)} %fusion.25) | copy-start | bytes 4718596
  436.9 5.3 %copy-start.16 = (f32[2,8,48,512]{3,2,1,0:T(8,128)S(1)}, f32[2,8,48,512]{3,2,1,0:T(8,128)}, u32[]{:S(2)}) copy-start(f32[2,8,48,512]{3,2,1,0:T(8,128)} %fusion.21) | copy-start | bytes 4718596
  436.9 5.3 %copy-start.17 = (f32[2,8,48,512]{3,2,1,0:T(8,128)S(1)}, f32[2,8,48,512]{3,2,1,0:T(8,128)}, u32[]{:S(2)}) copy-start(f32[2,8,48,512]{3,2,1,0:T(8,128)} %fusion.9) | copy-start | bytes 4718596
  (1 other events, 1.9 us)
where the time goes:
time: 525 us; the launch traced here: 518 us
  waiting for transfers between devices  293 us (56%)
  matrix products  85.2 us (16%)
  local copies, waits for them, and re-layouts  74.2 us (14%)
  starting transfers between devices  32.3 us (6%)
  other arithmetic  31.7 us (6%)
    all_to_all x2, waiting for transfers between devices, send_pair(): lax.all_to_all(row_grads, 'expert', split_axis=0, concat_axis=0, tiled=True)  111 us
    all_to_all x2, waiting for transfers between devices, send_pair(): lax.all_to_all(row_inputs, 'expert', split_axis=0, concat_axis=0, tiled=T...  97.6 us
    all_to_all x2, waiting for transfers between devices, combine_rows(): lax.all_to_all(back_rows, 'expert', split_axis=0, concat_axis=0, tiled=True)  84.2 us
    gather x2, local copies, waits for them, and re-layouts, combine_rows(): flat_rows[slot_of].reshape(cotangent.shape[0], TOPK, cotangent.shape[-1])  17.5 us
    dot_general x2, matrix products, weight_terms(): jnp.einsum('sekd,sekf->edf', row_inputs, grad_gate_value, preferred_eleme...  16.4 us
    dot_general x2, matrix products, weight_terms(): jnp.einsum('sekd,sekf->edf', row_inputs, grad_up_value, preferred_element...  16.2 us
    dot_general x2, matrix products, expert_rows(): jnp.einsum('sekd,efd->sekf', row_grads, weight_down, preferred_element_ty...  12.6 us
    all_to_all x2, starting transfers between devices, send_pair(): lax.all_to_all(row_inputs, 'expert', split_axis=0, concat_axis=0, tiled=T...  12.1 us
  transfers between devices with their start and end apart: 7, of which 6 were waited for; matrix products, arithmetic and copies ran while one was open for 24% of the time, Pallas kernels for 0%

commit v1 on v0

v1 whole, which is shorter than its diff:
```python
import functools

import jax
import jax.numpy as jnp
from jax import lax
from jax.experimental import pallas as pl
from jax.experimental.pallas import tpu as pltpu
from jax.sharding import PartitionSpec as P

LANES = 128
VMEM_BYTES = 48 * 1024 * 1024
NT = (((1,), (1,)), ((), ()))
TN = (((0,), (0,)), ((), ()))
BF16 = jnp.bfloat16
F32 = jnp.float32


def dot(a, b, dims=(((1,), (0,)), ((), ()))):
    return lax.dot_general(a, b, dims, preferred_element_type=F32)


def params():
    return pltpu.CompilerParams(vmem_limit_bytes=VMEM_BYTES)


def cost(flops, moved):
    return pl.CostEstimate(flops=int(flops), bytes_accessed=int(moved), transcendentals=0)


class Grid:
    def __init__(self, count):
        self.ny = max(d for d in range(1, count + 1) if count % d == 0 and d * d <= count)
        self.nz = count // self.ny
        self.far = sorted(range(1, self.nz), key=lambda k: -min(k, self.nz - k))
        self.offsets = [(k, j) for k in [0] + self.far for j in range(self.ny)]

    def pairs(self, dz, dy):
        return [
            (z * self.ny + y, (z + dz) % self.nz * self.ny + (y + dy) % self.ny)
            for z in range(self.nz)
            for y in range(self.ny)
        ]

    def move(self, x, dz, dy):
        return lax.ppermute(x, "expert", self.pairs(dz, dy))

    def move_down(self, x, dz):
        sections, count = lax.axis_size("section"), lax.axis_size("expert")
        pairs = [
            (s * count + a, (s - 1) % sections * count + b)
            for s in range(sections)
            for a, b in self.pairs(dz, 0)
        ]
        return lax.ppermute(x, ("section", "expert"), pairs)

    def spread(self, along_z):
        found = {(k, 0): block for k, block in along_z.items()}
        for k in [0] + self.far:
            for j in range(1, self.ny):
                found[k, j] = self.move(along_z[k], 0, j)
        return [found[offset] for offset in self.offsets]

    def gather(self, x):
        along_z = {0: x}
        for k in self.far:
            along_z[k] = self.move(x, k, 0)
        return self.spread(along_z)

    def reduce(self, blocks):
        part = dict(zip(self.offsets, blocks))
        total = None
        for k in self.far + [0]:
            summed = part[k, 0].astype(F32)
            for j in range(1, self.ny):
                summed = summed + self.move(part[k, j], 0, -j).astype(F32)
            if k:
                summed = self.move(summed.astype(BF16), -k, 0).astype(F32)
            total = summed if total is None else total + summed
        return total


def join(refs, whole):
    rows = refs[0].shape[0]
    for i, ref in enumerate(refs):
        whole[i * rows : (i + 1) * rows, :] = ref[...]


def hidden_kernel(count, *refs):
    x_refs, (gate_w, up_w, x_out, gate_out, up_out) = refs[:count], refs[count:]

    @pl.when((pl.program_id(0) == 0) & (pl.program_id(1) == 0))
    def _():
        join(x_refs, x_out)

    x = x_out[...]
    gate_out[...] = dot(x, gate_w[0])
    up_out[...] = dot(x, up_w[0])


def hidden_values(blocks, w_gate, w_up):
    local, depth, width = w_gate.shape
    rows = blocks[0].shape[0]
    tokens = rows * len(blocks)
    tile = min(256, width)
    steps = width // tile
    whole = lambda e, f: (0, 0)
    at = lambda e, f: (0, e * steps + f)
    out = jax.ShapeDtypeStruct((tokens, local * width), F32)
    return pl.pallas_call(
        functools.partial(hidden_kernel, len(blocks)),
        grid=(local, steps),
        in_specs=[pl.BlockSpec((rows, depth), whole)] * len(blocks)
        + [pl.BlockSpec((1, depth, tile), lambda e, f: (e, 0, f))] * 2,
        out_specs=[
            pl.BlockSpec((tokens, depth), whole),
            pl.BlockSpec((tokens, tile), at),
            pl.BlockSpec((tokens, tile), at),
        ],
        out_shape=[jax.ShapeDtypeStruct((tokens, depth), BF16), out, out],
        compiler_params=params(),
        cost_estimate=cost(4 * tokens * depth * local * width, 4 * local * depth * width),
        name="hidden_values",
    )(*blocks, w_gate, w_up)


def grads_kernel(count, *refs):
    c_refs, g_refs = refs[:count], refs[count : 2 * count]
    pick, gate, up, down_w, c_out, grad_gate, grad_up, hidden, gates = refs[2 * count :]

    @pl.when((pl.program_id(0) == 0) & (pl.program_id(1) == 0))
    def _():
        join(c_refs, c_out)
        join(g_refs, gates)

    weight = dot(gates[...], pick[0])
    grad_hidden = dot(c_out[...], down_w[0], NT) * weight
    gate_value, up_value = gate[...], up[...]
    sigmoid_value = jax.nn.sigmoid(gate_value)
    swished = gate_value * sigmoid_value
    derivative = sigmoid_value * (1.0 + gate_value * (1.0 - sigmoid_value))
    hidden[...] = (swished * up_value * weight).astype(BF16)
    grad_gate[...] = (grad_hidden * up_value * derivative).astype(BF16)
    grad_up[...] = (grad_hidden * swished).astype(BF16)


def hidden_grads(blocks, gate_blocks, pick, gate, up, w_down):
    local, width, depth = w_down.shape
    rows = blocks[0].shape[0]
    tokens = rows * len(blocks)
    tile = pick.shape[-1]
    steps = width // tile
    whole = lambda e, f: (0, 0)
    at = lambda e, f: (0, e * steps + f)
    columns = gate_blocks[0].shape[1]
    out = jax.ShapeDtypeStruct((tokens, local * width), BF16)
    return pl.pallas_call(
        functools.partial(grads_kernel, len(blocks)),
        grid=(local, steps),
        in_specs=[pl.BlockSpec((rows, depth), whole)] * len(blocks)
        + [pl.BlockSpec((rows, columns), whole)] * len(blocks)
        + [
            pl.BlockSpec((1, columns, tile), lambda e, f: (e, 0, 0)),
            pl.BlockSpec((tokens, tile), at),
            pl.BlockSpec((tokens, tile), at),
            pl.BlockSpec((1, tile, depth), lambda e, f: (e, f, 0)),
        ],
        out_specs=[pl.BlockSpec((tokens, depth), whole)] + [pl.BlockSpec((tokens, tile), at)] * 3,
        out_shape=[jax.ShapeDtypeStruct((tokens, depth), BF16), out, out, out],
        scratch_shapes=[pltpu.VMEM((tokens, columns), BF16)],
        compiler_params=params(),
        cost_estimate=cost(2 * tokens * depth * local * width, 2 * local * depth * width),
        name="hidden_grads",
    )(*blocks, *gate_blocks, pick, gate, up, w_down)


def back_kernel(count, grad_gate, grad_up, gate_w, up_w, *outs):
    local, _, width = gate_w.shape
    total = None
    for e in range(local):
        columns = slice(e * width, (e + 1) * width)
        for grad, weight in ((grad_gate, gate_w), (grad_up, up_w)):
            term = dot(grad[:, columns], weight[e], NT)
            total = term if total is None else total + term
    total = total.astype(BF16)
    rows = outs[0].shape[0]
    for i in range(count):
        outs[i][...] = total[i * rows : (i + 1) * rows]


def back_rows(grad_gate, grad_up, w_gate, w_up, count):
    local, depth, width = w_gate.shape
    tokens = grad_gate.shape[0]
    rows = tokens // count
    tile = min(256, depth)
    whole = pl.BlockSpec(grad_gate.shape, lambda d: (0, 0))
    weight = pl.BlockSpec((local, tile, width), lambda d: (0, d, 0))
    return pl.pallas_call(
        functools.partial(back_kernel, count),
        grid=(depth // tile,),
        in_specs=[whole, whole, weight, weight],
        out_specs=[pl.BlockSpec((rows, tile), lambda d: (0, d))] * count,
        out_shape=[jax.ShapeDtypeStruct((rows, depth), BF16)] * count,
        compiler_params=params(),
        cost_estimate=cost(4 * tokens * depth * local * width, 4 * local * depth * width),
        name="back_rows",
    )(grad_gate, grad_up, w_gate, w_up)


def outer_kernel(lefts, rights, out):
    left = jnp.concatenate([ref[...] for ref in lefts], axis=0)
    right = jnp.concatenate([ref[...] for ref in rights], axis=0)
    out[0] = dot(left, right, TN).astype(BF16)


def outer_input_kernel(first_x, second_x, first, second, out):
    outer_kernel((first_x, second_x), (first, second), out)


def outer_input(first_x, second_x, first, second, local):
    tokens, depth = first_x.shape
    width = first.shape[1] // local
    tile = min(512, depth)
    x_spec = pl.BlockSpec((tokens, tile), lambda e, d: (0, d))
    g_spec = pl.BlockSpec((tokens, width), lambda e, d: (0, e))
    return pl.pallas_call(
        outer_input_kernel,
        grid=(local, depth // tile),
        in_specs=[x_spec, x_spec, g_spec, g_spec],
        out_specs=pl.BlockSpec((1, tile, width), lambda e, d: (e, d, 0)),
        out_shape=jax.ShapeDtypeStruct((local, depth, width), BF16),
        compiler_params=params(),
        cost_estimate=cost(4 * tokens * depth * local * width, 2 * local * depth * width),
        name="outer_input",
    )(first_x, second_x, first, second)


def outer_hidden(first_hidden, second_hidden, first_c, second_c, local):
    tokens, depth = first_c.shape
    width = first_hidden.shape[1] // local
    tile = min(256, width)
    steps = width // tile
    h_spec = pl.BlockSpec((tokens, tile), lambda e, f: (0, e * steps + f))
    c_spec = pl.BlockSpec((tokens, depth), lambda e, f: (0, 0))
    return pl.pallas_call(
        outer_input_kernel,
        grid=(local, steps),
        in_specs=[h_spec, h_spec, c_spec, c_spec],
        out_specs=pl.BlockSpec((1, tile, depth), lambda e, f: (e, f, 0)),
        out_shape=jax.ShapeDtypeStruct((local, width, depth), BF16),
        compiler_params=params(),
        cost_estimate=cost(4 * tokens * depth * local * width, 2 * local * depth * width),
        name="outer_hidden",
    )(first_hidden, second_hidden, first_c, second_c)


def gate_columns(routes, gates, experts):
    chosen = routes[:, :, None] == jnp.arange(experts, dtype=jnp.int32)[None, None, :]
    dense = jnp.sum(jnp.where(chosen, gates[:, :, None], 0.0), axis=1)
    high = lax.reduce_precision(dense, 8, 7)
    middle = lax.reduce_precision(dense - high, 8, 7)
    low = dense - high - middle
    columns = jnp.concatenate([high, middle, low], axis=1).astype(BF16)
    return jnp.pad(columns, ((0, 0), (0, -columns.shape[1] % LANES)))


def on_device(inputs, routes, gates, cot_early, head_grad, w_gate, w_up, w_down):
    w_gate, w_up, w_down = w_gate[0], w_up[0], w_down[0]
    grid = Grid(lax.axis_size("expert"))
    me = lax.axis_index("expert")
    local, depth, width = w_gate.shape
    experts = local * lax.axis_size("expert")
    first_in, second_in = inputs[0, 0], inputs[0, 1]
    first_cot = cot_early[0]
    first_g = gate_columns(routes[0, 0], gates[0, 0], experts)
    second_g = gate_columns(routes[0, 1], gates[0, 1], experts)
    columns = first_g.shape[1]
    own = me * local + jnp.arange(local, dtype=jnp.int32)
    lane = jnp.arange(columns, dtype=jnp.int32)
    mine = (lane[None, :] % experts == own[:, None]) & (lane[None, :] < 3 * experts)
    pick = jnp.broadcast_to(
        mine[:, :, None], (local, columns, min(256, width))
    ).astype(BF16)

    first_blocks = grid.gather(first_in)
    first_x, first_gate, first_up = hidden_values(first_blocks, w_gate, w_up)
    joined = grid.gather(jnp.concatenate([first_cot, first_g], axis=1))
    first_c, first_dg, first_du, first_h = hidden_grads(
        [b[:, :depth] for b in joined],
        [b[:, depth:] for b in joined],
        pick, first_gate, first_up, w_down,
    )
    first_back = back_rows(first_dg, first_du, w_gate, w_up, len(joined))
    grad_early = (first_cot.astype(F32) + grid.reduce(first_back)).astype(BF16)

    sent = jnp.where(lax.axis_index("section") == 0, head_grad, grad_early)
    joined = grid.gather(jnp.concatenate([second_in, second_g], axis=1))
    second_x, second_gate, second_up = hidden_values(
        [b[:, :depth] for b in joined], w_gate, w_up
    )
    along_z = {k: grid.move_down(sent, k) for k in grid.far + [0]}
    second_cot = along_z[0]
    second_c, second_dg, second_du, second_h = hidden_grads(
        grid.spread(along_z),
        [b[:, depth:] for b in joined],
        pick, second_gate, second_up, w_down,
    )
    second_back = back_rows(second_dg, second_du, w_gate, w_up, len(joined))
    grad_late = (second_cot.astype(F32) + grid.reduce(second_back)).astype(BF16)
    grad_gate = outer_input(first_x, second_x, first_dg, second_dg, local)
    grad_up = outer_input(first_x, second_x, first_du, second_du, local)
    grad_down = outer_hidden(first_h, second_h, first_c, second_c, local)
    return (grad_early[None], grad_late[None], grad_gate[None], grad_up[None], grad_down[None])


def solution(mesh):
    in_specs = (
        P("section", None, "expert", None),
        P("section", None, "expert", None),
        P("section", None, "expert", None),
        P("section", "expert", None),
        P("expert", None),
        P("section", "expert", None, None),
        P("section", "expert", None, None),
        P("section", "expert", None, None),
    )
    out_specs = (
        P("section", "expert", None),
        P("section", "expert", None),
        P("section", "expert", None, None),
        P("section", "expert", None, None),
        P("section", "expert", None, None),
    )
    return jax.shard_map(
        on_device, mesh=mesh, in_specs=in_specs, out_specs=out_specs, check_vma=False
    )
```

time: 525 us -> 269 us (0.51)
  waiting for transfers between devices: 293 us -> 107 us
  matrix products: 85.2 us -> 0 us
  Pallas kernels: 0 us -> 77.1 us
  local copies, waits for them, and re-layouts: 74.2 us -> 9.71 us
  starting transfers between devices: 32.3 us -> 62.6 us
  other arithmetic: 31.7 us -> 7.7 us
    all_to_all x6 -> x0, waiting for transfers between devices: 293 us -> none  [the longest x2 111 us: send_pair(): lax.all_to_all(row_grads, 'expert', split_axis=0, concat_axis=0, tiled=True)]
    ppermute x1 -> x43, waiting for transfers between devices: 0.01 us -> 107 us  [the longest x39 95.1 us: move(): return lax.ppermute(x, 'expert', self.pairs(dz, dy))]
    dot_general x16 -> x0, matrix products: 85.2 us -> none  [the longest x2 16.4 us: weight_terms(): jnp.einsum('sekd,sekf->edf', row_inputs, grad_gate_value, preferred_eleme...]
    pallas_call x0 -> x9, Pallas kernels: none -> 77.1 us  [the longest x2 19 us: outer_input(): pl.pallas_call(outer_input_kernel, grid=(local, depth // tile), in_specs=...]
    ppermute x1 -> x43, starting transfers between devices: 1.42 us -> 62.6 us  [the longest x39 60 us: move(): return lax.ppermute(x, 'expert', self.pairs(dz, dy))]
    gather x8 -> x0, local copies, waits for them, and re-layouts: 40.8 us -> none  [the longest x2 17.5 us: combine_rows(): flat_rows[slot_of].reshape(cotangent.shape[0], TOPK, cotangent.shape[-1])]
    all_to_all x6 -> x0, starting transfers between devices: 30.9 us -> none  [the longest x2 12.1 us: send_pair(): lax.all_to_all(row_inputs, 'expert', split_axis=0, concat_axis=0, tiled=T...]
    scatter x4 -> x0, local copies, waits for them, and re-layouts: 16.4 us -> none  [the longest x2 8.19 us: route_slots(): source = jnp.zeros((experts * CAP,), jnp.int32).at[slot_of].set(jnp.arang...]
  transfers between devices with their start and end apart: 7 -> 43, of which waited for: 6 -> 18; matrix products, arithmetic and copies ran while one was open for 24% -> 5% of each run, Pallas kernels for 0% -> 17%
where the time goes in v1:
time: 269 us; the launch traced here: 266 us
  waiting for transfers between devices  107 us (40%)
  Pallas kernels  77.1 us (29%)
  starting transfers between devices  62.6 us (23%)
  local copies, waits for them, and re-layouts  9.71 us (4%)
  other arithmetic  7.7 us (3%)
    ppermute x39, waiting for transfers between devices, move(): return lax.ppermute(x, 'expert', self.pairs(dz, dy))  95.1 us
    ppermute x39, starting transfers between devices, move(): return lax.ppermute(x, 'expert', self.pairs(dz, dy))  60 us
    pallas_call x2, Pallas kernels, outer_input(): pl.pallas_call(outer_input_kernel, grid=(local, depth // tile), in_specs=...  19 us
    pallas_call x2, Pallas kernels, back_rows(): pl.pallas_call(functools.partial(back_kernel, count), grid=(depth // tile...  18.5 us
    pallas_call x2, Pallas kernels, hidden_values(): pl.pallas_call(functools.partial(hidden_kernel, len(blocks)), grid=(local...  17.1 us
    pallas_call x2, Pallas kernels, hidden_grads(): pl.pallas_call(functools.partial(grads_kernel, len(blocks)), grid=(local,...  14.5 us
    ppermute x4, waiting for transfers between devices, move_down(): return lax.ppermute(x, ('section', 'expert'), pairs)  12.3 us
    pallas_call x1, Pallas kernels, outer_hidden(): pl.pallas_call(outer_input_kernel, grid=(local, steps), in_specs=[h_spec,...  8.03 us
  transfers between devices with their start and end apart: 43, of which 18 were waited for; matrix products, arithmetic and copies ran while one was open for 5% of the time, Pallas kernels for 17%

profile of v1, /device:TPU:0, one launch (start us, length us, event | category | flops | bytes accessed | tf_op | source)
XLA Modules:
  0.0 265.6 jit_solution(14560816301050116694)
XLA Ops:
  3.5 5.1 %collective-permute-start.5 = (bf16[64,2176]{1,0:T(8,128)(2,1)S(1)}, bf16[64,2176]{1,0:T(8,128)(2,1)S(1)}, u32[]{:S(2)}, u32[]{:S(2)}) collective-permute-start(bf16[64,2176]{1,0:T(8,128)(2,1)S(1)} %pad_maximum_fusion), channel_id=1, source_target_pairs={{0,6},{1,7},{2,0},{3,1},{4,2},{5,3},{6,4},{7,5},{8,14},{9,15},{10,... | collective-permute-start | bytes 835592 | tf_op jit(solution)/shard_map/ppermute | solution.py:45
  14.4 18.9 %collective-permute-done.12.refs_6_ = bf16[64,2048]{1,0:T(8,128)(2,1)S(1)} collective-permute-done((bf16[64,2048]{1,0:T(8,128)(2,1)S(1)}, bf16[64,2048]{1,0:T(8,128)(2,1)S(1)}, u32[]{:S(2)}, u32[]{:S(2)}) %collective-permute-start.12) | collective-permute-done | bytes 262176 | tf_op jit(solution)/shard_map/ppermute | solution.py:45
  33.3 10.4 %collective-permute-start.8 = (bf16[64,2048]{1,0:T(8,128)(2,1)S(1)}, bf16[64,2048]{1,0:T(8,128)(2,1)S(1)}, u32[]{:S(2)}, u32[]{:S(2)}) collective-permute-start(bf16[64,2048]{1,0:T(8,128)(2,1)S(1)} %get-tuple-element.68.refs_0_), channel_id=1, source_target_pairs={{0,4},{1,5},{2,6},{3,7},{4,0},{5,1},{6,2},{7,3},{8,12},{9,13},{10,... | collective-permute-start | bytes 786440 | tf_op jit(solution)/shard_map/ppermute | solution.py:45
  45.4 9.4 %collective-permute-done.8.refs_2_ = bf16[64,2048]{1,0:T(8,128)(2,1)S(1)} collective-permute-done((bf16[64,2048]{1,0:T(8,128)(2,1)S(1)}, bf16[64,2048]{1,0:T(8,128)(2,1)S(1)}, u32[]{:S(2)}, u32[]{:S(2)}) %collective-permute-start.8) | collective-permute-done | bytes 262176 | tf_op jit(solution)/shard_map/ppermute | solution.py:45
  65.6 4.1 %collective-permute-done.13.refs_7_ = bf16[64,2048]{1,0:T(8,128)(2,1)S(1)} collective-permute-done((bf16[64,2048]{1,0:T(8,128)(2,1)S(1)}, bf16[64,2048]{1,0:T(8,128)(2,1)S(1)}, u32[]{:S(2)}, u32[]{:S(2)}) %collective-permute-start.13) | collective-permute-done | bytes 262176 | tf_op jit(solution)/shard_map/ppermute | solution.py:45
  71.2 4.1 %collective-permute-done.11.refs_5_ = bf16[64,2048]{1,0:T(8,128)(2,1)S(1)} collective-permute-done((bf16[64,2048]{1,0:T(8,128)(2,1)S(1)}, bf16[64,2048]{1,0:T(8,128)(2,1)S(1)}, u32[]{:S(2)}, u32[]{:S(2)}) %collective-permute-start.11) | collective-permute-done | bytes 262176 | tf_op jit(solution)/shard_map/ppermute | solution.py:45
  75.3 5.6 %collective-permute-done.9.refs_3_ = bf16[64,2048]{1,0:T(8,128)(2,1)S(1)} collective-permute-done((bf16[64,2048]{1,0:T(8,128)(2,1)S(1)}, bf16[64,2048]{1,0:T(8,128)(2,1)S(1)}, u32[]{:S(2)}, u32[]{:S(2)}) %collective-permute-start.9) | collective-permute-done | bytes 262176 | tf_op jit(solution)/shard_map/ppermute | solution.py:45
  80.9 8.6 %hidden_values.2 = (bf16[512,2048]{1,0:T(8,128)(2,1)S(1)}, f32[512,1024]{1,0:T(8,128)}, f32[512,1024]{1,0:T(8,128)}) custom-call(bf16[64,2048]{1,0:T(8,128)(2,1)S(1)} %get-tuple-element.68.refs_0_, bf16[64,2048]{1,0:T(8,128)(2,1)S(1)} %collective-permute-done.7.refs_1_, bf16[64,2048]{1,0:T(8,128)(2,1)S(1)} %collective-permute-done.8.refs_2_, ...), custom_call_target="tpu_custom_call" | custom-call | flops 4294967296 | bytes 8388608 | tf_op jit(solution)/shard_map/hidden_values/pallas_call | solution.py:109
  96.3 7.2 %hidden_grads.2 = (bf16[512,2048]{1,0:T(8,128)(2,1)}, bf16[512,1024]{1,0:T(8,128)(2,1)S(1)}, bf16[512,1024]{1,0:T(8,128)(2,1)S(1)}, bf16[512,1024]{1,0:T(8,128)(2,1)S(1)}) custom-call(bf16[64,2048]{1,0:T(8,128)(2,1)S(1)} %bitcast.25, bf16[64,2048]{1,0:T(8,128)(2,1)S(1)} %slice.136.refs_1_, bf16[64,2048]{1,0:T(8,128)(2,1)S(1)} %slice.137.refs_2_, ...), custom_call_target="tpu_custom_call" | custom-call | flops 2147483648 | bytes 4194304 | tf_op jit(solution)/shard_map/hidden_grads/pallas_call | solution.py:156
  103.6 9.4 %back_rows.2 = (bf16[64,2048]{1,0:T(8,128)(2,1)S(1)}, bf16[64,2048]{1,0:T(8,128)(2,1)S(1)}, bf16[64,2048]{1,0:T(8,128)(2,1)S(1)}, bf16[64,2048]{1,0:T(8,128)(2,1...) custom-call(bf16[512,1024]{1,0:T(8,128)(2,1)S(1)} %get-tuple-element, ...), custom_call_target="tpu_custom_call" | custom-call | flops 4294967296 | bytes 8388608 | tf_op jit(solution)/shard_map/back_rows/pallas_call | solution.py:197
  115.3 4.2 %collective-permute-start.34 = (bf16[64,2176]{1,0:T(8,128)(2,1)}, bf16[64,2176]{1,0:T(8,128)(2,1)}, u32[]{:S(2)}, u32[]{:S(2)}) collective-permute-start(bf16[64,2176]{1,0:T(8,128)(2,1)} %pad_maximum_fusion.1), channel_id=1, source_target_pairs={{0,6},{1,7},{2,0},{3,1},{4,2},{5,3},{6,4},{7,5},{8,14},{9,15},{10,... | collective-permute-start | bytes 835592 | tf_op jit(solution)/shard_map/ppermute | solution.py:45
  122.8 6.4 %collective-permute-done.16 = bf16[64,2048]{1,0:T(8,128)(2,1)S(1)} collective-permute-done((bf16[64,2048]{1,0:T(8,128)(2,1)S(1)}, bf16[64,2048]{1,0:T(8,128)(2,1)S(1)}, u32[]{:S(2)}, u32[]{:S(2)}) %collective-permute-start.16) | collective-permute-done | bytes 262176 | tf_op jit(solution)/shard_map/ppermute | solution.py:45
  130.5 4.2 %collective-permute-done.18 = bf16[64,2048]{1,0:T(8,128)(2,1)S(1)} collective-permute-done((bf16[64,2048]{1,0:T(8,128)(2,1)S(1)}, bf16[64,2048]{1,0:T(8,128)(2,1)S(1)}, u32[]{:S(2)}, u32[]{:S(2)}) %collective-permute-start.18) | collective-permute-done | bytes 262176 | tf_op jit(solution)/shard_map/ppermute | solution.py:45
  141.5 13.3 %collective-permute-done.30 = bf16[64,2176]{1,0:T(8,128)(2,1)} collective-permute-done((bf16[64,2176]{1,0:T(8,128)(2,1)}, bf16[64,2176]{1,0:T(8,128)(2,1)}, u32[]{:S(2)}, u32[]{:S(2)}) %collective-permute-start.30) | collective-permute-done | bytes 278560 | tf_op jit(solution)/shard_map/ppermute | solution.py:45
  169.6 3.9 %collective-permute-done.33 = bf16[64,2176]{1,0:T(8,128)(2,1)S(1)} collective-permute-done((bf16[64,2176]{1,0:T(8,128)(2,1)}, bf16[64,2176]{1,0:T(8,128)(2,1)S(1)}, u32[]{:S(2)}, u32[]{:S(2)}) %collective-permute-start.33) | collective-permute-done | bytes 278560 | tf_op jit(solution)/shard_map/ppermute | solution.py:45
  182.3 9.8 %collective-permute-done.23.refs_2_ = bf16[64,2048]{1,0:T(8,128)(2,1)S(1)} collective-permute-done((bf16[64,2048]{1,0:T(8,128)(2,1)S(1)}, bf16[64,2048]{1,0:T(8,128)(2,1)S(1)}, u32[]{:S(2)}, u32[]{:S(2)}) %collective-permute-start.23) | collective-permute-done | bytes 262176 | tf_op jit(solution)/shard_map/ppermute | solution.py:54
  194.1 8.5 %hidden_values.3 = (bf16[512,2048]{1,0:T(8,128)(2,1)S(1)}, f32[512,1024]{1,0:T(8,128)}, f32[512,1024]{1,0:T(8,128)}) custom-call(bf16[64,2048]{1,0:T(8,128)(2,1)S(1)} %get-tuple-element.67.refs_0_, bf16[64,2048]{1,0:T(8,128)(2,1)S(1)} %slice.157.refs_1_, bf16[64,2048]{1,0:T(8,128)(2,1)S(1)} %slice.158.refs_2_, bf16[64,2048]{1,0:T(8,128)(2,1)S(1)} %slice.159.refs_3_, ...), custom_call_target="tpu_custom_call" | custom-call | flops 4294967296 | bytes 8388608 | tf_op jit(solution)/shard_map/hidden_values/pallas_call | solution.py:109
  202.7 3.7 %collective-permute-done.22.refs_1_ = bf16[64,2048]{1,0:T(8,128)(2,1)S(1)} collective-permute-done((bf16[64,2048]{1,0:T(8,128)(2,1)S(1)}, bf16[64,2048]{1,0:T(8,128)(2,1)S(1)}, u32[]{:S(2)}, u32[]{:S(2)}) %collective-permute-start.22) | collective-permute-done | bytes 262176 | tf_op jit(solution)/shard_map/ppermute | solution.py:45
  206.4 7.2 %hidden_grads.3 = (bf16[512,2048]{1,0:T(8,128)(2,1)}, bf16[512,1024]{1,0:T(8,128)(2,1)S(1)}, bf16[512,1024]{1,0:T(8,128)(2,1)S(1)}, bf16[512,1024]{1,0:T(8,128)(2,1)S(1)}) custom-call(bf16[64,2048]{1,0:T(8,128)(2,1)S(1)} %collective-permute-done.21.refs_0_, bf16[64,2048]{1,0:T(8,128)(2,1)S(1)} %collective-permute-done.22.refs_1_, ...), custom_call_target="tpu_custom_call" | custom-call | flops 2147483648 | bytes 4194304 | tf_op jit(solution)/shard_map/hidden_grads/pallas_call | solution.py:156
  213.6 9.2 %back_rows.3 = (bf16[64,2048]{1,0:T(8,128)(2,1)S(1)}, bf16[64,2048]{1,0:T(8,128)(2,1)S(1)}, bf16[64,2048]{1,0:T(8,128)(2,1)S(1)}, bf16[64,2048]{1,0:T(8,128)(2,1...) custom-call(bf16[512,1024]{1,0:T(8,128)(2,1)S(1)} %get-tuple-element, ...), custom_call_target="tpu_custom_call" | custom-call | flops 4294967296 | bytes 8388608 | tf_op jit(solution)/shard_map/back_rows/pallas_call | solution.py:197
  226.9 9.5 %outer_input.3 = bf16[2,2048,512]{2,1,0:T(8,128)(2,1)} custom-call(bf16[512,2048]{1,0:T(8,128)(2,1)S(1)} %copy-done.5, bf16[512,2048]{1,0:T(8,128)(2,1)} %copy-done.6, bf16[512,1024]{1,0:T(8,128)(2,1)S(1)} %copy-done.3, bf16[512,1024]{1,0:T(8,128)(2,1)S(1)} %get-tuple-element.50.grad_up.second), custom_call_target="tpu_custom_call" | custom-call | flops 4294967296 | bytes 4194304 | tf_op jit(solution)/shard_map/outer_input/pallas_call | solution.py:225
  236.4 9.5 %outer_input.2 = bf16[2,2048,512]{2,1,0:T(8,128)(2,1)} custom-call(bf16[512,2048]{1,0:T(8,128)(2,1)S(1)} %copy-done.5, bf16[512,2048]{1,0:T(8,128)(2,1)} %copy-done.6, bf16[512,1024]{1,0:T(8,128)(2,1)S(1)} %get-tuple-element.37.grad_gate.first, bf16[512,1024]{1,0:T(8,128)(2,1)S(1)} %get-tuple-element.49.grad_gate.second), custom_call_target="tpu_custom_call" | custom-call | flops 4294967296 | bytes 4194304 | tf_op jit(solution)/shard_map/outer_input/pallas_call | solution.py:225
  249.9 8.0 %outer_hidden.1 = bf16[2,512,2048]{2,1,0:T(8,128)(2,1)} custom-call(bf16[512,1024]{1,0:T(8,128)(2,1)S(1)} %get-tuple-element.61.first_x, bf16[512,1024]{1,0:T(8,128)(2,1)S(1)} %get-tuple-element.62.second_x, bf16[512,2048]{1,0:T(8,128)(2,1)S(1)} %copy-done.1, bf16[512,2048]{1,0:T(8,128)(2,1)} %get-tuple-element.64.second), custom_call_target="tpu_custom_call" | custom-call | flops 4294967296 | bytes 4194304 | tf_op jit(solution)/shard_map/outer_hidden/pallas_call | solution.py:244
  257.9 6.7 %collective-permute-done.37 = bf16[64,2048]{1,0:T(8,128)(2,1)S(1)} collective-permute-done((bf16[64,2048]{1,0:T(8,128)(2,1)S(1)}, bf16[64,2048]{1,0:T(8,128)(2,1)S(1)}, u32[]{:S(2)}, u32[]{:S(2)}) %collective-permute-start.37) | collective-permute-done | bytes 262176 | tf_op jit(solution)/shard_map/ppermute | solution.py:45
  (145 shorter events, 77.6 us)
Async XLA Ops:
  3.5 52.8 %collective-permute-start.5 = (bf16[64,2176]{1,0:T(8,128)(2,1)S(1)}, bf16[64,2176]{1,0:T(8,128)(2,1)S(1)}, u32[]{:S(2)}, u32[]{:S(2)}) collective-permute-start(bf16[64,2176]{1,0:T(8,128)(2,1)S(1)} %pad_maximum_fusion), channel_id=1, source_target_pairs={{0,6},{1,7},{2,0},{3,1},{4,2},{5,3},{6,4},{7,5},{8,14},{9,15},{10,... | collective-permute-start | bytes 835592 | tf_op jit(solution)/shard_map/ppermute | solution.py:45
  8.6 48.2 %collective-permute-start.3 = (bf16[64,2176]{1,0:T(8,128)(2,1)S(1)}, bf16[64,2176]{1,0:T(8,128)(2,1)S(1)}, u32[]{:S(2)}, u32[]{:S(2)}) collective-permute-start(bf16[64,2176]{1,0:T(8,128)(2,1)S(1)} %pad_maximum_fusion), channel_id=1, source_target_pairs={{0,2},{1,3},{2,4},{3,5},{4,6},{5,7},{6,0},{7,1},{8,10},{9,11},{10,... | collective-permute-start | bytes 835592 | tf_op jit(solution)/shard_map/ppermute | solution.py:45
  8.6 49.7 %collective-permute-start.1 = (bf16[64,2176]{1,0:T(8,128)(2,1)S(1)}, bf16[64,2176]{1,0:T(8,128)(2,1)S(1)}, u32[]{:S(2)}, u32[]{:S(2)}) collective-permute-start(bf16[64,2176]{1,0:T(8,128)(2,1)S(1)} %pad_maximum_fusion), channel_id=1, source_target_pairs={{0,4},{1,5},{2,6},{3,7},{4,0},{5,1},{6,2},{7,3},{8,12},{9,13},{10,... | collective-permute-start | bytes 835592 | tf_op jit(solution)/shard_map/ppermute | solution.py:45
  10.7 22.6 %collective-permute-start.12 = (bf16[64,2048]{1,0:T(8,128)(2,1)S(1)}, bf16[64,2048]{1,0:T(8,128)(2,1)S(1)}, u32[]{:S(2)}, u32[]{:S(2)}) collective-permute-start(bf16[64,2048]{1,0:T(8,128)(2,1)S(1)} %get-tuple-element.68.refs_0_), channel_id=1, source_target_pairs={{0,6},{1,7},{2,0},{3,1},{4,2},{5,3},{6,4},{7,5},{8,14},{9,15},{10,... | collective-permute-start | bytes 786440 | tf_op jit(solution)/shard_map/ppermute | solution.py:45
  13.6 30.2 %collective-permute-start.10 = (bf16[64,2048]{1,0:T(8,128)(2,1)S(1)}, bf16[64,2048]{1,0:T(8,128)(2,1)S(1)}, u32[]{:S(2)}, u32[]{:S(2)}) collective-permute-start(bf16[64,2048]{1,0:T(8,128)(2,1)S(1)} %get-tuple-element.68.refs_0_), channel_id=1, source_target_pairs={{0,2},{1,3},{2,4},{3,5},{4,6},{5,7},{6,0},{7,1},{8,10},{9,11},{10,... | collective-permute-start | bytes 786440 | tf_op jit(solution)/shard_map/ppermute | solution.py:45
  33.3 21.5 %collective-permute-start.8 = (bf16[64,2048]{1,0:T(8,128)(2,1)S(1)}, bf16[64,2048]{1,0:T(8,128)(2,1)S(1)}, u32[]{:S(2)}, u32[]{:S(2)}) collective-permute-start(bf16[64,2048]{1,0:T(8,128)(2,1)S(1)} %get-tuple-element.68.refs_0_), channel_id=1, source_target_pairs={{0,4},{1,5},{2,6},{3,7},{4,0},{5,1},{6,2},{7,3},{8,12},{9,13},{10,... | collective-permute-start | bytes 786440 | tf_op jit(solution)/shard_map/ppermute | solution.py:45
  58.4 22.5 %collective-permute-start.9 = (bf16[64,2048]{1,0:T(8,128)(2,1)S(1)}, bf16[64,2048]{1,0:T(8,128)(2,1)S(1)}, u32[]{:S(2)}, u32[]{:S(2)}) collective-permute-start(bf16[64,2048]{1,0:T(8,128)(2,1)S(1)} %collective-permute-done.8.refs_2_), channel_id=1, source_target_pairs={{0,1},{1,0},{2,3},{3,2},{4,5},{5,4},{6,7},{7,6},{8,9},{9,8},{10,11... | collective-permute-start | bytes 786440 | tf_op jit(solution)/shard_map/ppermute | solution.py:45
  59.1 31.7 %collective-permute-start.6 = (bf16[64,2176]{1,0:T(8,128)(2,1)S(1)}, bf16[64,2176]{1,0:T(8,128)(2,1)S(1)}, u32[]{:S(2)}, u32[]{:S(2)}) collective-permute-start(bf16[64,2176]{1,0:T(8,128)(2,1)S(1)} %collective-permute-done.5), channel_id=1, source_target_pairs={{0,1},{1,0},{2,3},{3,2},{4,5},{5,4},{6,7},{7,6},{8,9},{9,8},{10,11... | collective-permute-start | bytes 835592 | tf_op jit(solution)/shard_map/ppermute | solution.py:45
  64.1 28.8 %collective-permute-start.4 = (bf16[64,2176]{1,0:T(8,128)(2,1)S(1)}, bf16[64,2176]{1,0:T(8,128)(2,1)S(1)}, u32[]{:S(2)}, u32[]{:S(2)}) collective-permute-start(bf16[64,2176]{1,0:T(8,128)(2,1)S(1)} %collective-permute-done.3), channel_id=1, source_target_pairs={{0,1},{1,0},{2,3},{3,2},{4,5},{5,4},{6,7},{7,6},{8,9},{9,8},{10,11... | collective-permute-start | bytes 835592 | tf_op jit(solution)/shard_map/ppermute | solution.py:45
  69.7 26.5 %collective-permute-start.2 = (bf16[64,2176]{1,0:T(8,128)(2,1)S(1)}, bf16[64,2176]{1,0:T(8,128)(2,1)S(1)}, u32[]{:S(2)}, u32[]{:S(2)}) collective-permute-start(bf16[64,2176]{1,0:T(8,128)(2,1)S(1)} %collective-permute-done.1), channel_id=1, source_target_pairs={{0,1},{1,0},{2,3},{3,2},{4,5},{5,4},{6,7},{7,6},{8,9},{9,8},{10,11... | collective-permute-start | bytes 835592 | tf_op jit(solution)/shard_map/ppermute | solution.py:45
  115.3 22.7 %collective-permute-start.34 = (bf16[64,2176]{1,0:T(8,128)(2,1)}, bf16[64,2176]{1,0:T(8,128)(2,1)}, u32[]{:S(2)}, u32[]{:S(2)}) collective-permute-start(bf16[64,2176]{1,0:T(8,128)(2,1)} %pad_maximum_fusion.1), channel_id=1, source_target_pairs={{0,6},{1,7},{2,0},{3,1},{4,2},{5,3},{6,4},{7,5},{8,14},{9,15},{10,... | collective-permute-start | bytes 835592 | tf_op jit(solution)/shard_map/ppermute | solution.py:45
  119.4 22.0 %collective-permute-start.32 = (bf16[64,2176]{1,0:T(8,128)(2,1)}, bf16[64,2176]{1,0:T(8,128)(2,1)}, u32[]{:S(2)}, u32[]{:S(2)}) collective-permute-start(bf16[64,2176]{1,0:T(8,128)(2,1)} %pad_maximum_fusion.1), channel_id=1, source_target_pairs={{0,2},{1,3},{2,4},{3,5},{4,6},{5,7},{6,0},{7,1},{8,10},{9,11},{10,... | collective-permute-start | bytes 835592 | tf_op jit(solution)/shard_map/ppermute | solution.py:45
  119.5 35.3 %collective-permute-start.30 = (bf16[64,2176]{1,0:T(8,128)(2,1)}, bf16[64,2176]{1,0:T(8,128)(2,1)}, u32[]{:S(2)}, u32[]{:S(2)}) collective-permute-start(bf16[64,2176]{1,0:T(8,128)(2,1)} %pad_maximum_fusion.1), channel_id=1, source_target_pairs={{0,4},{1,5},{2,6},{3,7},{4,0},{5,1},{6,2},{7,3},{8,12},{9,13},{10,... | collective-permute-start | bytes 835592 | tf_op jit(solution)/shard_map/ppermute | solution.py:45
  129.3 26.0 %collective-permute-start.20 = (bf16[64,2048]{1,0:T(8,128)(2,1)S(1)}, bf16[64,2048]{1,0:T(8,128)(2,1)}, u32[]{:S(2)}, u32[]{:S(2)}) collective-permute-start(bf16[64,2048]{1,0:T(8,128)(2,1)S(1)} %get-tuple-element.46), channel_id=1, source_target_pairs={{0,1},{1,0},{2,3},{3,2},{4,5},{5,4},{6,7},{7,6},{8,9},{9,8},{10,11... | collective-permute-start | bytes 786440 | tf_op jit(solution)/shard_map/ppermute | solution.py:45
  134.8 25.5 %collective-permute-start.15 = (bf16[64,2048]{1,0:T(8,128)(2,1)}, bf16[64,2048]{1,0:T(8,128)(2,1)}, u32[]{:S(2)}, u32[]{:S(2)}) collective-permute-start(bf16[64,2048]{1,0:T(8,128)(2,1)} %add_convert_fusion.7), channel_id=1, source_target_pairs={{0,4},{1,5},{2,6},{3,7},{4,0},{5,1},{6,2},{7,3},{8,12},{9,13},{10,... | collective-permute-start | bytes 786440 | tf_op jit(solution)/shard_map/ppermute | solution.py:45
  137.9 22.9 %collective-permute-start.17 = (bf16[64,2048]{1,0:T(8,128)(2,1)}, bf16[64,2048]{1,0:T(8,128)(2,1)}, u32[]{:S(2)}, u32[]{:S(2)}) collective-permute-start(bf16[64,2048]{1,0:T(8,128)(2,1)} %add_convert_fusion.6), channel_id=1, source_target_pairs={{0,6},{1,7},{2,0},{3,1},{4,2},{5,3},{6,4},{7,5},{8,14},{9,15},{10,... | collective-permute-start | bytes 786440 | tf_op jit(solution)/shard_map/ppermute | solution.py:45
  141.5 20.9 %collective-permute-start.19 = (bf16[64,2048]{1,0:T(8,128)(2,1)}, bf16[64,2048]{1,0:T(8,128)(2,1)}, u32[]{:S(2)}, u32[]{:S(2)}) collective-permute-start(bf16[64,2048]{1,0:T(8,128)(2,1)} %add_convert_fusion.5), channel_id=1, source_target_pairs={{0,2},{1,3},{2,4},{3,5},{4,6},{5,7},{6,0},{7,1},{8,10},{9,11},{10,... | collective-permute-start | bytes 786440 | tf_op jit(solution)/shard_map/ppermute | solution.py:45
  169.6 22.5 %collective-permute-start.23 = (bf16[64,2048]{1,0:T(8,128)(2,1)S(1)}, bf16[64,2048]{1,0:T(8,128)(2,1)S(1)}, u32[]{:S(2)}, u32[]{:S(2)}) collective-permute-start(bf16[64,2048]{1,0:T(8,128)(2,1)S(1)} %get-tuple-element.65), channel_id=1, source_target_pairs={{0,28},{1,29},{2,30},{3,31},{4,24},{5,25},{6,26},{7,27},{8,4},{9,5... | collective-permute-start | bytes 786440 | tf_op jit(solution)/shard_map/ppermute | solution.py:54
  178.7 24.0 %collective-permute-start.28 = (bf16[64,2048]{1,0:T(8,128)(2,1)S(1)}, bf16[64,2048]{1,0:T(8,128)(2,1)S(1)}, u32[]{:S(2)}, u32[]{:S(2)}) collective-permute-start(bf16[64,2048]{1,0:T(8,128)(2,1)S(1)} %collective-permute-done.27.refs_6_), channel_id=1, source_target_pairs={{0,1},{1,0},{2,3},{3,2},{4,5},{5,4},{6,7},{7,6},{8,9},{9,8},{10,11... | collective-permute-start | bytes 786440 | tf_op jit(solution)/shard_map/ppermute | solution.py:45
  181.8 20.8 %collective-permute-start.26 = (bf16[64,2048]{1,0:T(8,128)(2,1)S(1)}, bf16[64,2048]{1,0:T(8,128)(2,1)S(1)}, u32[]{:S(2)}, u32[]{:S(2)}) collective-permute-start(bf16[64,2048]{1,0:T(8,128)(2,1)S(1)} %collective-permute-done.25.refs_4_), channel_id=1, source_target_pairs={{0,1},{1,0},{2,3},{3,2},{4,5},{5,4},{6,7},{7,6},{8,9},{9,8},{10,11... | collective-permute-start | bytes 786440 | tf_op jit(solution)/shard_map/ppermute | solution.py:45
  222.8 23.1 %collective-permute-start.36 = (bf16[64,2048]{1,0:T(8,128)(2,1)S(1)}, bf16[64,2048]{1,0:T(8,128)(2,1)S(1)}, u32[]{:S(2)}, u32[]{:S(2)}) collective-permute-start(bf16[64,2048]{1,0:T(8,128)(2,1)S(1)} %get-tuple-element.52), channel_id=1, source_target_pairs={{0,1},{1,0},{2,3},{3,2},{4,5},{5,4},{6,7},{7,6},{8,9},{9,8},{10,11... | collective-permute-start | bytes 786440 | tf_op jit(solution)/shard_map/ppermute | solution.py:45
  223.1 23.0 %collective-permute-start.38 = (bf16[64,2048]{1,0:T(8,128)(2,1)S(1)}, bf16[64,2048]{1,0:T(8,128)(2,1)S(1)}, u32[]{:S(2)}, u32[]{:S(2)}) collective-permute-start(bf16[64,2048]{1,0:T(8,128)(2,1)S(1)} %get-tuple-element.54), channel_id=1, source_target_pairs={{0,1},{1,0},{2,3},{3,2},{4,5},{5,4},{6,7},{7,6},{8,9},{9,8},{10,11... | collective-permute-start | bytes 786440 | tf_op jit(solution)/shard_map/ppermute | solution.py:45
  224.9 24.9 %collective-permute-start.40 = (bf16[64,2048]{1,0:T(8,128)(2,1)S(1)}, bf16[64,2048]{1,0:T(8,128)(2,1)S(1)}, u32[]{:S(2)}, u32[]{:S(2)}) collective-permute-start(bf16[64,2048]{1,0:T(8,128)(2,1)S(1)} %get-tuple-element.56), channel_id=1, source_target_pairs={{0,1},{1,0},{2,3},{3,2},{4,5},{5,4},{6,7},{7,6},{8,9},{9,8},{10,11... | collective-permute-start | bytes 786440 | tf_op jit(solution)/shard_map/ppermute | solution.py:45
  225.2 32.8 %collective-permute-start.42 = (bf16[64,2048]{1,0:T(8,128)(2,1)S(1)}, bf16[64,2048]{1,0:T(8,128)(2,1)S(1)}, u32[]{:S(2)}, u32[]{:S(2)}) collective-permute-start(bf16[64,2048]{1,0:T(8,128)(2,1)S(1)} %get-tuple-element.58), channel_id=1, source_target_pairs={{0,1},{1,0},{2,3},{3,2},{4,5},{5,4},{6,7},{7,6},{8,9},{9,8},{10,11... | collective-permute-start | bytes 786440 | tf_op jit(solution)/shard_map/ppermute | solution.py:45
  (26 other events, 336.9 us)

commit v2 on v0

v2 whole, which is shorter than its diff:
```python
import functools

import jax
import jax.numpy as jnp
from jax import lax
from jax.experimental import pallas as pl
from jax.experimental.pallas import tpu as pltpu
from jax.sharding import PartitionSpec as P

LANES = 128
VMEM_BYTES = 60 * 1024 * 1024
OUTER_VMEM_BYTES = 20 * 1024 * 1024
NT = (((1,), (1,)), ((), ()))
TN = (((0,), (0,)), ((), ()))
BF16 = jnp.bfloat16
F32 = jnp.float32


def dot(a, b, dims=(((1,), (0,)), ((), ()))):
    return lax.dot_general(a, b, dims, preferred_element_type=F32)


class Grid:
    def __init__(self, count):
        self.ny = max(d for d in range(1, count + 1) if count % d == 0 and d * d <= count)
        self.nz = count // self.ny
        self.far = sorted(range(1, self.nz), key=lambda k: (min(k, self.nz - k), -k))
        self.along = [0] + self.far

    def pairs(self, dz, dy):
        return [
            (z * self.ny + y, (z + dz) % self.nz * self.ny + (y + dy) % self.ny)
            for z in range(self.nz)
            for y in range(self.ny)
        ]

    def move(self, x, dz, dy):
        with jax.named_scope(f"z{dz}y{dy}"):
            return lax.ppermute(x, "expert", self.pairs(dz, dy))

    def move_down(self, x, dz):
        sections, count = lax.axis_size("section"), lax.axis_size("expert")
        pairs = [
            (s * count + a, (s - 1) % sections * count + b)
            for s in range(sections)
            for a, b in self.pairs(dz, 0)
        ]
        with jax.named_scope(f"down_z{dz}"):
            return lax.ppermute(x, ("section", "expert"), pairs)

    def along_z(self, x):
        return [x] + [self.move(x, k, 0) for k in self.far]

    def near(self, x):
        return [self.move(x, 0, j) for j in range(1, self.ny)]

    def reduce_y(self, parts):
        move = lambda *x: [self.move(part, 0, -j) for j, part in enumerate(x, 1)]
        summed = parts[0].astype(F32)
        for moved in move(*parts[1:]):
            summed = summed + moved.astype(F32)
        rows = summed.shape[0] // self.nz
        own = summed[:rows]
        return own, [summed[i * rows : (i + 1) * rows].astype(BF16) for i in range(1, self.nz)]

    def reduce_z(self, own, blocks, turn):
        move = lambda *x: [self.move(block, -k, 0) for k, block in zip(self.far, x)]
        for moved in turn("z", move, *blocks):
            own = own + moved.astype(F32)
        return own


def on_core(kernel, name, flops, index, operands, out_shape, scratch):
    hbm = pl.BlockSpec(memory_space=pltpu.HBM)
    return pl.pallas_call(
        kernel,
        in_specs=[pl.BlockSpec(memory_space=pltpu.SMEM)] * len(index) + [hbm] * len(operands),
        out_specs=[hbm] * len(out_shape),
        out_shape=out_shape,
        scratch_shapes=scratch,
        compiler_params=pltpu.CompilerParams(vmem_limit_bytes=VMEM_BYTES),
        cost_estimate=pl.CostEstimate(flops=int(flops), bytes_accessed=0, transcendentals=0),
        name=name,
    )(*index, *operands)


def join(refs, whole, place, sem):
    rows, block, at = place
    copies, start = [], 0
    for ref in refs:
        for first in range(at[0], ref.shape[0], block):
            copies.append(
                pltpu.make_async_copy(
                    ref.at[first : first + rows, at[1] : at[1] + whole.shape[1]],
                    whole.at[start : start + rows, :],
                    sem.at[len(copies)],
                )
            )
            start += rows
    return copies


def tiles(size):
    tile = min(256, size)
    return [slice(i, i + tile) for i in range(0, size, tile)]


def rows_kernel(counts, places, lane, count, me, *refs):
    refs = list(refs)
    take = lambda n: [refs.pop(0) for _ in range(n)]
    x_refs, c_refs, g_refs = (take(n) for n in counts)
    weights_hbm = take(3)
    x_hbm, c_hbm = take(2)
    values_hbm, outs = take(3), take(count)
    weights, values = take(3), take(3)
    x, c, g, gate, up, back, total_out, x_sem, c_sem, g_sem, w_sem, v_sem, out_sem = refs
    gate_w, up_w, down_w = weights
    grad_gate, grad_up, hidden = values
    local, depth, width = gate_w.shape
    rows = outs[0].shape[0]
    x_copies = join(x_refs, x, places[0], x_sem)
    c_copies = join(c_refs, c, places[1], c_sem)
    g_copies = join(g_refs, g, places[2], g_sem)
    queue = [
        pltpu.make_async_copy(weights_hbm[i].at[e], weights[i].at[e], w_sem.at[i * local + e])
        for e in range(local)
        for i in (2, 0, 1)
    ]

    def arrived(position):
        if position + 2 < len(queue):
            queue[position + 2].start()
        queue[position].wait()

    for copy in c_copies + g_copies + queue[:1] + x_copies + queue[1:2]:
        copy.start()
    for copy in c_copies + g_copies:
        copy.wait()
    writes = []

    def write(*copy):
        writes.append(pltpu.make_async_copy(*copy))
        writes[-1].start()

    experts = lane[1]
    at_lane = lax.broadcasted_iota(jnp.int32, (g.shape[1], tiles(width)[0].stop), 0)
    for e in range(local):
        arrived(3 * e)
        first = lane[0] + me[0] * local + e
        mine = (at_lane == first) | (at_lane == first + experts) | (at_lane == first + 2 * experts)
        weight = dot(g[...], mine.astype(F32).astype(BF16))
        grads = [dot(c[...], down_w[e, f, :], NT) * weight for f in tiles(width)]
        if e == 0:
            for copy in x_copies:
                copy.wait()
        arrived(3 * e + 1)
        if e == local - 1:
            write(x, x_hbm, v_sem.at[3])
            write(c, c_hbm, v_sem.at[4])
        for f in tiles(width):
            gate[:, f] = dot(x[...], gate_w[e, :, f])
        arrived(3 * e + 2)
        for f in tiles(width):
            up[:, f] = dot(x[...], up_w[e, :, f])
        for f, grad_hidden in zip(tiles(width), grads):
            at = slice(e * width + f.start, e * width + f.stop)
            gate_value, up_value = gate[:, f], up[:, f]
            sigmoid_value = jax.nn.sigmoid(gate_value)
            swished = gate_value * sigmoid_value
            derivative = sigmoid_value * (1.0 + gate_value * (1.0 - sigmoid_value))
            hidden[:, at] = (swished * up_value * weight).astype(BF16)
            grad_gate[:, at] = (grad_hidden * up_value * derivative).astype(BF16)
            grad_up[:, at] = (grad_hidden * swished).astype(BF16)
        columns = slice(e * width, (e + 1) * width)
        if e == local - 1:
            for i in range(3):
                write(values[i], values_hbm[i], v_sem.at[i])
        for d in tiles(depth):
            total = dot(grad_gate[:, columns], gate_w[e, d, :], NT)
            total = total + dot(grad_up[:, columns], up_w[e, d, :], NT)
            if e:
                total = total + back[:, d]
            if e < local - 1:
                back[:, d] = total
                continue
            total_out[:, d] = total.astype(BF16)
            if d.stop in (depth // 2, depth):
                side = slice(d.stop - depth // 2, d.stop)
                for j, out in enumerate(outs):
                    sem = out_sem.at[j, d.stop // depth]
                    write(total_out.at[j * rows : (j + 1) * rows, side], out.at[:, side], sem)
    for copy in writes:
        copy.wait()


def expert_rows(tokens, blocks, places, lane, lanes, me, weights, count):
    local, depth, width = weights[0].shape
    value = (tokens, local * width)
    return on_core(
        functools.partial(rows_kernel, [len(x) for x in blocks], places, lane, count),
        "expert_rows",
        10 * tokens * depth * local * width,
        [me],
        [*blocks[0], *blocks[1], *blocks[2], *weights],
        [jax.ShapeDtypeStruct((tokens, depth), BF16)] * 2
        + [jax.ShapeDtypeStruct(value, BF16)] * 3
        + [jax.ShapeDtypeStruct((tokens // count, depth), BF16)] * count,
        [pltpu.VMEM(w.shape, BF16) for w in weights]
        + [pltpu.VMEM(value, BF16)] * 3
        + [pltpu.VMEM((tokens, depth), BF16)] * 2
        + [pltpu.VMEM((tokens, lanes), BF16)]
        + [pltpu.VMEM((tokens, width), F32)] * 2
        + [pltpu.VMEM((tokens, depth), F32), pltpu.VMEM((tokens, depth), BF16)]
        + [pltpu.SemaphoreType.DMA((tokens // place[0],)) for place in places]
        + [pltpu.SemaphoreType.DMA((3 * local,)), pltpu.SemaphoreType.DMA((5,))]
        + [pltpu.SemaphoreType.DMA((count, 2))],
    )


def outer_kernel(pieces, *refs):
    lefts, rights = refs[:pieces], refs[pieces : 2 * pieces]
    out, right = refs[2 * pieces :]
    local, rows, columns = out.shape
    start = 0
    for ref in rights:
        right[start : start + ref.shape[0], :] = ref[...]
        start += ref.shape[0]
    for m in tiles(lefts[0].shape[1]):
        left = jnp.concatenate([ref[:, m] for ref in lefts], axis=0)
        product = dot(left, right[...], TN).astype(BF16)
        if lefts[0].shape[1] == rows:
            for e in range(local):
                out[e, m, :] = product[:, e * columns : (e + 1) * columns]
        else:
            at = m.start % rows
            out[m.start // rows, at : at + m.stop - m.start, :] = product


def outer(lefts, rights, local, rows, columns, name):
    tokens = sum(x.shape[0] for x in lefts)
    spec = pl.BlockSpec(memory_space=pltpu.VMEM)
    return pl.pallas_call(
        functools.partial(outer_kernel, len(lefts)),
        in_specs=[spec] * (2 * len(lefts)),
        out_specs=spec,
        out_shape=jax.ShapeDtypeStruct((local, rows, columns), BF16),
        scratch_shapes=[pltpu.VMEM((tokens, rights[0].shape[1]), BF16)],
        compiler_params=pltpu.CompilerParams(vmem_limit_bytes=OUTER_VMEM_BYTES),
        cost_estimate=pl.CostEstimate(
            flops=2 * tokens * local * rows * columns, bytes_accessed=0, transcendentals=0
        ),
        name=name,
    )(*lefts, *rights)


def payload_kernel(experts, half, routes, gates, x_in, c_in, *refs):
    *outs, columns, sems = refs
    rows, depth = half, x_in.shape[-1]
    copies = []
    for i, out in enumerate(outs):
        from_rows = slice(i * rows, (i + 1) * rows)
        for j, source in enumerate((x_in.at[0, 0], c_in.at[0])):
            copies.append(
                pltpu.make_async_copy(
                    source.at[from_rows, :],
                    out.at[:, j * depth : (j + 1) * depth],
                    sems.at[len(copies)],
                )
            )
    for copy in copies:
        copy.start()
    lanes = columns.shape[1]
    lane = lax.broadcasted_iota(jnp.int32, (lanes, rows), 0)
    group = lane // (3 * experts)
    part = lane // experts % 3
    expert = lane % experts
    dense = jnp.zeros((lanes, rows), F32)
    for m in range(routes.shape[2]):
        for i in range(len(outs)):
            here = group == m * len(outs) + i
            chosen = routes[0, :, m, i * rows : (i + 1) * rows]
            weight = gates[0, :, m, i * rows : (i + 1) * rows]
            for k in range(chosen.shape[0]):
                named = here & (chosen[k : k + 1, :] == expert)
                dense = dense + jnp.where(named, weight[k : k + 1, :], 0.0)
    high = dense.astype(BF16)
    rest = dense - high.astype(F32)
    middle = rest.astype(BF16)
    low = (rest - middle.astype(F32)).astype(BF16)
    pieces = [x.astype(F32) for x in (high, middle, low)]
    chosen = jnp.where(part == 0, pieces[0], jnp.where(part == 1, pieces[1], pieces[2]))
    columns[...] = jnp.transpose(chosen).astype(BF16)
    outs[0][:, 2 * depth :] = columns[...]
    for copy in copies:
        copy.wait()


def payloads(routes, gates, inputs, cot_early, experts):
    half, depth = inputs.shape[2] // 2, inputs.shape[3]
    lanes = 2 * 2 * 3 * experts
    lanes += -lanes % LANES
    small = pl.BlockSpec(memory_space=pltpu.VMEM)
    large = pl.BlockSpec(memory_space=pltpu.HBM)
    return pl.pallas_call(
        functools.partial(payload_kernel, experts, half),
        in_specs=[small, small, large, large],
        out_specs=[small, small],
        out_shape=[
            jax.ShapeDtypeStruct((half, 2 * depth + lanes), BF16),
            jax.ShapeDtypeStruct((half, 2 * depth), BF16),
        ],
        scratch_shapes=[pltpu.VMEM((half, lanes), BF16), pltpu.SemaphoreType.DMA((4,))],
        compiler_params=pltpu.CompilerParams(vmem_limit_bytes=VMEM_BYTES),
        name="payloads",
    )(jnp.moveaxis(routes, 3, 1), jnp.moveaxis(gates, 3, 1), inputs, cot_early)


def after(x, *done):
    return lax.optimization_barrier((x, done))[0]


def on_device(inputs, routes, gates, cot_early, head_grad, w_gate, w_up, w_down):
    w_gate, w_up, w_down = w_gate[0], w_up[0], w_down[0]
    grid = Grid(lax.axis_size("expert"))
    me = lax.axis_index("expert")
    local, depth, width = w_gate.shape
    experts = local * lax.axis_size("expert")
    first_in, second_in = inputs[0, 0], inputs[0, 1]
    first_cot = cot_early[0]
    tokens = first_in.shape[0]
    half = tokens // 2
    halves = [slice(0, half), slice(half, tokens)]
    is_first = lax.axis_index("section") == 0
    everyone = half * grid.nz * grid.ny
    a0, b0 = payloads(routes, gates, inputs, cot_early, experts)
    lanes = a0.shape[1] - 2 * depth
    me = jnp.full((1,), lax.axis_index("expert"), jnp.int32)
    weights = (w_gate, w_up, w_down)

    def fuse(blocks):
        return jnp.concatenate(blocks, axis=0)

    def mix(*values):
        return [part for group in zip(*values) for part in group]

    def rows_of(m, part, x, c):
        results = expert_rows(
            everyone, (x[0], c[0], gate_blocks), (x[1], c[1], (half, half, (0, 2 * depth))),
            ((2 * m + part) * 3 * experts, experts), lanes, me, weights, grid.ny,
        )
        for kept, value in zip((xs, cs, dgs, dus, hs), results):
            kept.append(value)
        return results[5:]

    xs, cs, dgs, dus, hs = [], [], [], [], []

    def early_rows(part, blocks):
        return rows_of(0, part, (blocks, (half, half, (0, 0))), (blocks, (half, half, (0, depth))))

    def late_rows(part, blocks):
        x = (second_blocks, (half, tokens, (halves[part].start, 0)))
        return rows_of(1, part, x, (blocks, (half, half, (0, 0))))

    def early_grad(part, total):
        rows = halves[part]
        grad = (first_cot[rows].astype(F32) + total).astype(BF16)
        return grad, jnp.where(is_first, head_grad[rows], grad)

    last = {"z": (), "y": ()}

    def turn(link, move, *x):
        x = after(x, last[link])
        last[link] = move(*x)
        return last[link]

    straight = lambda link, move, *x: move(*x)
    a, b = halves
    along_z = lambda x: grid.along_z(x)[1:]
    ya, yb, yx = grid.near(a0), grid.near(b0), grid.near(second_in)
    za = turn("z", along_z, a0)
    fa = grid.near(after(fuse(za), ya, yb, yx))
    zb = turn("z", along_z, b0)
    gate_blocks = [a0] + za + mix(ya, fa)
    fb = grid.near(fuse(zb))
    zx = turn("z", along_z, second_in)
    back_a = early_rows(0, gate_blocks)
    own_a, sums_a = grid.reduce_y(back_a)
    back_b = early_rows(1, after([b0] + zb + mix(yb, fb), zx))
    total_a = grid.reduce_z(own_a, sums_a, turn)
    own_b, sums_b = grid.reduce_y(back_b)
    early_a, sent_a = early_grad(0, total_a)
    move_down = lambda *x: [grid.move_down(x[0], k) for k in grid.along]
    down_a = turn("z", move_down, sent_a)
    fx = grid.near(fuse(zx))
    second_blocks = [second_in] + zx + mix(yx, fx)
    total_b = grid.reduce_z(own_b, sums_b, straight)
    fa = grid.near(fuse(down_a))
    early_b, sent_b = early_grad(1, total_b)
    down_b = turn("z", move_down, sent_b)
    late_back_a = late_rows(0, down_a + fa)
    fb = grid.near(fuse(down_b))
    own_a, sums_a = grid.reduce_y(late_back_a)
    late_back_b = late_rows(1, down_b + fb)
    total_a = grid.reduce_z(own_a, sums_a, turn)
    own_b, sums_b = grid.reduce_y(late_back_b)
    total_b = grid.reduce_z(own_b, sums_b, turn)
    grad_late_a = (down_a[0].astype(F32) + total_a).astype(BF16)
    grad_late_b = (down_b[0].astype(F32) + total_b).astype(BF16)
    grad_gate = outer(after(xs, late_back_b, sums_a), dgs, local, depth, width, "outer_gate")
    grad_up = outer(after(xs, sums_b), dus, local, depth, width, "outer_up")
    grad_down = outer(after(hs, sums_b), cs, local, width, depth, "outer_down")
    grad_early = jnp.concatenate([early_a, early_b], axis=0)
    grad_late = jnp.concatenate([grad_late_a, grad_late_b], axis=0)
    return (grad_early[None], grad_late[None], grad_gate[None], grad_up[None], grad_down[None])


def solution(mesh):
    in_specs = (
        P("section", None, "expert", None),
        P("section", None, "expert", None),
        P("section", None, "expert", None),
        P("section", "expert", None),
        P("expert", None),
        P("section", "expert", None, None),
        P("section", "expert", None, None),
        P("section", "expert", None, None),
    )
    out_specs = (
        P("section", "expert", None),
        P("section", "expert", None),
        P("section", "expert", None, None),
        P("section", "expert", None, None),
        P("section", "expert", None, None),
    )
    return jax.shard_map(
        on_device, mesh=mesh, in_specs=in_specs, out_specs=out_specs, check_vma=False
    )
```

time: 525 us -> 221 us (0.42)
  waiting for transfers between devices: 293 us -> 56.5 us
  matrix products: 85.2 us -> 0 us
  local copies, waits for them, and re-layouts: 74.2 us -> 5.71 us
  Pallas kernels: 0 us -> 64.7 us
  starting transfers between devices: 32.3 us -> 86 us
  other arithmetic: 31.7 us -> 3.78 us
    all_to_all x6 -> x0, waiting for transfers between devices: 293 us -> none  [the longest x2 111 us: send_pair(): lax.all_to_all(row_grads, 'expert', split_axis=0, concat_axis=0, tiled=True)]
    dot_general x16 -> x0, matrix products: 85.2 us -> none  [the longest x2 16.4 us: weight_terms(): jnp.einsum('sekd,sekf->edf', row_inputs, grad_gate_value, preferred_eleme...]
    ppermute x1 -> x41, starting transfers between devices: 1.42 us -> 86 us  [the longest x33 68.8 us: move(): return lax.ppermute(x, 'expert', self.pairs(dz, dy))]
    pallas_call x0 -> x8, Pallas kernels: none -> 64.7 us  [the longest x4 42.4 us: on_core(): pl.pallas_call(kernel, in_specs=[pl.BlockSpec(memory_space=pltpu.SMEM)] *...]
    ppermute x1 -> x41, waiting for transfers between devices: 0.01 us -> 56.5 us  [the longest x33 44.4 us: move(): return lax.ppermute(x, 'expert', self.pairs(dz, dy))]
    gather x8 -> x0, local copies, waits for them, and re-layouts: 40.8 us -> none  [the longest x2 17.5 us: combine_rows(): flat_rows[slot_of].reshape(cotangent.shape[0], TOPK, cotangent.shape[-1])]
    all_to_all x6 -> x0, starting transfers between devices: 30.9 us -> none  [the longest x2 12.1 us: send_pair(): lax.all_to_all(row_inputs, 'expert', split_axis=0, concat_axis=0, tiled=T...]
    scatter x4 -> x0, local copies, waits for them, and re-layouts: 16.4 us -> none  [the longest x2 8.19 us: route_slots(): source = jnp.zeros((experts * CAP,), jnp.int32).at[slot_of].set(jnp.arang...]
  transfers between devices with their start and end apart: 7 -> 41, of which waited for: 6 -> 13; matrix products, arithmetic and copies ran while one was open for 24% -> 2% of each run, Pallas kernels for 0% -> 28%
where the time goes in v2:
time: 221 us; the launch traced here: 219 us
  starting transfers between devices  86 us (39%)
  Pallas kernels  64.7 us (29%)
  waiting for transfers between devices  56.5 us (26%)
  local copies, waits for them, and re-layouts  5.71 us (3%)
  other arithmetic  3.78 us (2%)
    ppermute x33, starting transfers between devices, move(): return lax.ppermute(x, 'expert', self.pairs(dz, dy))  68.8 us
    ppermute x33, waiting for transfers between devices, move(): return lax.ppermute(x, 'expert', self.pairs(dz, dy))  44.4 us
    pallas_call x4, Pallas kernels, on_core(): pl.pallas_call(kernel, in_specs=[pl.BlockSpec(memory_space=pltpu.SMEM)] *...  42.4 us
    pallas_call x3, Pallas kernels, outer(): pl.pallas_call(functools.partial(outer_kernel, len(lefts)), in_specs=[spe...  19.7 us
    ppermute x8, starting transfers between devices, move_down(): return lax.ppermute(x, ('section', 'expert'), pairs)  17.2 us
    ppermute x8, waiting for transfers between devices, move_down(): return lax.ppermute(x, ('section', 'expert'), pairs)  12.1 us
  transfers between devices with their start and end apart: 41, of which 13 were waited for; matrix products, arithmetic and copies ran while one was open for 2% of the time, Pallas kernels for 28%

profile of v2, /device:TPU:0, one launch (start us, length us, event | category | flops | bytes accessed | tf_op | source)
XLA Modules:
  0.0 218.5 jit_solution(9041621041540757839)
XLA Ops:
  3.3 4.1 %collective-permute-start.2 = (bf16[32,4352]{1,0:T(8,128)(2,1)}, bf16[32,4352]{1,0:T(8,128)(2,1)S(1)}, u32[]{:S(2)}, u32[]{:S(2)}) collective-permute-start(bf16[32,4352]{1,0:T(8,128)(2,1)} %get-tuple-element.67.refs_0_.refs_6_.refs_12_.refs_11_), channel_id=1, source_target_pairs={{0,4},{1,5},{2,6},{3,7},{4,0},{5,1},{6,2},{7,3},{8,12},{9,13},{10,... | collective-permute-start | bytes 835592 | tf_op jit(solution)/shard_map/z2y0/ppermute | solution.py:39
  14.3 12.8 %collective-permute-done.2.refs_3_.refs_9_.refs_15_.refs_14_ = bf16[32,4352]{1,0:T(8,128)(2,1)S(1)} collective-permute-done((bf16[32,4352]{1,0:T(8,128)(2,1)}, bf16[32,4352]{1,0:T(8,128)(2,1)S(1)}, u32[]{:S(2)}, u32[]{:S(2)}) %collective-permute-start.2) | collective-permute-done | bytes 278560 | tf_op jit(solution)/shard_map/z2y0/ppermute | solution.py:39
  29.0 5.9 %collective-permute-start.10 = (bf16[32,4096]{1,0:T(8,128)(2,1)}, bf16[32,4096]{1,0:T(8,128)(2,1)S(1)}, u32[]{:S(2)}, u32[]{:S(2)}) collective-permute-start(bf16[32,4096]{1,0:T(8,128)(2,1)} %get-tuple-element.77.refs_0_.refs_6_), channel_id=1, source_target_pairs={{0,4},{1,5},{2,6},{3,7},{4,0},{5,1},{6,2},{7,3},{8,12},{9,13},{10,... | collective-permute-start | bytes 786440 | tf_op jit(solution)/shard_map/z2y0/ppermute | solution.py:39
  34.9 3.8 %collective-permute-start.8 = (bf16[32,4096]{1,0:T(8,128)(2,1)}, bf16[32,4096]{1,0:T(8,128)(2,1)S(1)}, u32[]{:S(2)}, u32[]{:S(2)}) collective-permute-start(bf16[32,4096]{1,0:T(8,128)(2,1)} %get-tuple-element.77.refs_0_.refs_6_), channel_id=1, source_target_pairs={{0,6},{1,7},{2,0},{3,1},{4,2},{5,3},{6,4},{7,5},{8,14},{9,15},{10,... | collective-permute-start | bytes 786440 | tf_op jit(solution)/shard_map/z3y0/ppermute | solution.py:39
  40.4 12.8 %collective-permute-done.10.refs_3_.refs_9_ = bf16[32,4096]{1,0:T(8,128)(2,1)S(1)} collective-permute-done((bf16[32,4096]{1,0:T(8,128)(2,1)}, bf16[32,4096]{1,0:T(8,128)(2,1)S(1)}, u32[]{:S(2)}, u32[]{:S(2)}) %collective-permute-start.10) | collective-permute-done | bytes 262176 | tf_op jit(solution)/shard_map/z2y0/ppermute | solution.py:39
  55.7 4.1 %collective-permute-start.13 = (bf16[64,2048]{1,0:T(8,128)(2,1)S(1)}, bf16[64,2048]{1,0:T(8,128)(2,1)}, u32[]{:S(2)}, u32[]{:S(2)}) collective-permute-start(bf16[64,2048]{1,0:T(8,128)(2,1)S(1)} %slice_bitcast_fusion.refs_0_), channel_id=1, source_target_pairs={{0,4},{1,5},{2,6},{3,7},{4,0},{5,1},{6,2},{7,3},{8,12},{9,13},{10,... | collective-permute-start | bytes 786440 | tf_op jit(solution)/shard_map/z2y0/ppermute | solution.py:39
  60.7 3.1 %collective-permute-start.11 = (bf16[64,2048]{1,0:T(8,128)(2,1)S(1)}, bf16[64,2048]{1,0:T(8,128)(2,1)}, u32[]{:S(2)}, u32[]{:S(2)}) collective-permute-start(bf16[64,2048]{1,0:T(8,128)(2,1)S(1)} %slice_bitcast_fusion.refs_0_), channel_id=1, source_target_pairs={{0,6},{1,7},{2,0},{3,1},{4,2},{5,3},{6,4},{7,5},{8,14},{9,15},{10,... | collective-permute-start | bytes 786440 | tf_op jit(solution)/shard_map/z3y0/ppermute | solution.py:39
  63.8 10.6 %expert_rows.4 = (bf16[256,2048]{1,0:T(8,128)(2,1)}, bf16[256,2048]{1,0:T(8,128)(2,1)}, bf16[256,1024]{1,0:T(8,128)(2,1)}, bf16[256,1024]{1,0:T(8,128)(2,1)}, bf...) custom-call(s32[1]{0:T(128)} %bitcast.1.me, ...), custom_call_target="tpu_custom_call" | custom-call | flops 5368709120 | tf_op jit(solution)/shard_map/expert_rows/pallas_call | solution.py:75
  75.0 3.3 %collective-permute-done.13.refs_3_ = bf16[64,2048]{1,0:T(8,128)(2,1)} collective-permute-done((bf16[64,2048]{1,0:T(8,128)(2,1)S(1)}, bf16[64,2048]{1,0:T(8,128)(2,1)}, u32[]{:S(2)}, u32[]{:S(2)}) %collective-permute-start.13) | collective-permute-done | bytes 262176 | tf_op jit(solution)/shard_map/z2y0/ppermute | solution.py:39
  78.3 10.5 %expert_rows.5 = (bf16[256,2048]{1,0:T(8,128)(2,1)}, bf16[256,2048]{1,0:T(8,128)(2,1)}, bf16[256,1024]{1,0:T(8,128)(2,1)}, bf16[256,1024]{1,0:T(8,128)(2,1)}, bf...) custom-call(s32[1]{0:T(128)} %bitcast.1.me, ...), custom_call_target="tpu_custom_call" | custom-call | flops 5368709120 | tf_op jit(solution)/shard_map/expert_rows/pallas_call | solution.py:75
  90.3 5.3 %collective-permute-start.14 = (bf16[32,2048]{1,0:T(8,128)(2,1)S(1)}, bf16[32,2048]{1,0:T(8,128)(2,1)S(1)}, u32[]{:S(2)}, u32[]{:S(2)}) collective-permute-start(bf16[32,2048]{1,0:T(8,128)(2,1)S(1)} %get-tuple-element.74), channel_id=1, source_target_pairs={{0,2},{1,3},{2,4},{3,5},{4,6},{5,7},{6,0},{7,1},{8,10},{9,11},{10,... | collective-permute-start | bytes 393224 | tf_op jit(solution)/shard_map/z-3y0/ppermute | solution.py:39
  95.6 3.9 %collective-permute-start.16 = (bf16[32,2048]{1,0:T(8,128)(2,1)S(1)}, bf16[32,2048]{1,0:T(8,128)(2,1)S(1)}, u32[]{:S(2)}, u32[]{:S(2)}) collective-permute-start(bf16[32,2048]{1,0:T(8,128)(2,1)S(1)} %get-tuple-element.76), channel_id=1, source_target_pairs={{0,4},{1,5},{2,6},{3,7},{4,0},{5,1},{6,2},{7,3},{8,12},{9,13},{10,... | collective-permute-start | bytes 393224 | tf_op jit(solution)/shard_map/z-2y0/ppermute | solution.py:39
  101.6 6.9 %collective-permute-start.19 = (bf16[32,2048]{1,0:T(8,128)(2,1)}, bf16[32,2048]{1,0:T(8,128)(2,1)S(1)}, u32[]{:S(2)}, u32[]{:S(2)}) collective-permute-start(bf16[32,2048]{1,0:T(8,128)(2,1)} %get-tuple-element.152), channel_id=1, source_target_pairs={{0,2},{1,3},{2,4},{3,5},{4,6},{5,7},{6,0},{7,1},{8,10},{9,11},{10,... | collective-permute-start | bytes 393224 | tf_op jit(solution)/shard_map/z-3y0/ppermute | solution.py:39
  110.5 2.9 %collective-permute-start.20 = (bf16[32,2048]{1,0:T(8,128)(2,1)}, bf16[32,2048]{1,0:T(8,128)(2,1)S(1)}, u32[]{:S(2)}, u32[]{:S(2)}) collective-permute-start(bf16[32,2048]{1,0:T(8,128)(2,1)} %get-tuple-element.154), channel_id=1, source_target_pairs={{0,6},{1,7},{2,0},{3,1},{4,2},{5,3},{6,4},{7,5},{8,14},{9,15},{10,... | collective-permute-start | bytes 393224 | tf_op jit(solution)/shard_map/z-1y0/ppermute | solution.py:39
  113.4 4.3 %collective-permute-done.21 = bf16[32,2048]{1,0:T(8,128)(2,1)S(1)} collective-permute-done((bf16[32,2048]{1,0:T(8,128)(2,1)}, bf16[32,2048]{1,0:T(8,128)(2,1)S(1)}, u32[]{:S(2)}, u32[]{:S(2)}) %collective-permute-start.21) | collective-permute-done | bytes 131104 | tf_op jit(solution)/shard_map/z-2y0/ppermute | solution.py:39
  118.0 9.1 %collective-permute-start.25 = (bf16[32,2048]{1,0:T(8,128)(2,1)S(1)}, bf16[32,2048]{1,0:T(8,128)(2,1)S(1)}, u32[]{:S(2)}, u32[]{:S(2)}) collective-permute-start(bf16[32,2048]{1,0:T(8,128)(2,1)S(1)} %get-tuple-element.85), channel_id=1, source_target_pairs={{0,26},{1,27},{2,28},{3,29},{4,30},{5,31},{6,24},{7,25},{8,2},{9,3... | collective-permute-start | bytes 393224 | tf_op jit(solution)/shard_map/down_z1/ppermute | solution.py:49
  141.1 5.7 %collective-permute-done.32.refs_9_ = bf16[32,2048]{1,0:T(8,128)(2,1)S(1)} collective-permute-done((bf16[32,2048]{1,0:T(8,128)(2,1)S(1)}, bf16[32,2048]{1,0:T(8,128)(2,1)S(1)}, u32[]{:S(2)}, u32[]{:S(2)}) %collective-permute-start.32) | collective-permute-done | bytes 131104 | tf_op jit(solution)/shard_map/down_z2/ppermute | solution.py:49
  151.8 8.5 %collective-permute-done.27.refs_10_ = bf16[128,2048]{1,0:T(8,128)(2,1)S(1)} collective-permute-done((bf16[128,2048]{1,0:T(8,128)(2,1)S(1)}, bf16[128,2048]{1,0:T(8,128)(2,1)S(1)}, u32[]{:S(2)}, u32[]{:S(2)}) %collective-permute-start.27) | collective-permute-done | bytes 524320 | tf_op jit(solution)/shard_map/z0y1/ppermute | solution.py:39
  161.1 10.4 %expert_rows.6 = (bf16[256,2048]{1,0:T(8,128)(2,1)}, bf16[256,2048]{1,0:T(8,128)(2,1)}, bf16[256,1024]{1,0:T(8,128)(2,1)}, bf16[256,1024]{1,0:T(8,128)(2,1)}, bf...) custom-call(s32[1]{0:T(128)} %bitcast.1.me, bf16[64,2048]{1,0:T(8,128)(2,1)} %copy-done.34, ...), custom_call_target="tpu_custom_call" | custom-call | flops 5368709120 | tf_op jit(solution)/shard_map/expert_rows/pallas_call | solution.py:75
  173.3 10.9 %expert_rows.7 = (bf16[256,2048]{1,0:T(8,128)(2,1)}, bf16[256,2048]{1,0:T(8,128)(2,1)}, bf16[256,1024]{1,0:T(8,128)(2,1)}, bf16[256,1024]{1,0:T(8,128)(2,1)}, bf...) custom-call(s32[1]{0:T(128)} %bitcast.1.me, bf16[64,2048]{1,0:T(8,128)(2,1)} %copy-done.34, ...), custom_call_target="tpu_custom_call" | custom-call | flops 5368709120 | tf_op jit(solution)/shard_map/expert_rows/pallas_call | solution.py:75
  192.1 6.6 %outer_gate.1 = bf16[2,2048,512]{2,1,0:T(8,128)(2,1)} custom-call(bf16[256,2048]{1,0:T(8,128)(2,1)S(1)} %copy-done, bf16[256,2048]{1,0:T(8,128)(2,1)S(1)} %copy-done.5, bf16[256,2048]{1,0:T(8,128)(2,1)S(1)} %copy-done.10, bf16[256,2048]{1,0:T(8,128)(2,1)S(1)} %copy-done.12, bf16[256,1024]{1,0:T(8,128)(2,1)S(1)} %copy-done.4, ...), custom_call_target="tpu_custom_call" | custom-call | flops 4294967296 | tf_op jit(solution)/shard_map/outer_gate/pallas_call | solution.py:242
  199.6 3.8 %collective-permute-start.39 = (bf16[32,2048]{1,0:T(8,128)(2,1)S(1)}, bf16[32,2048]{1,0:T(8,128)(2,1)S(1)}, u32[]{:S(2)}, u32[]{:S(2)}) collective-permute-start(bf16[32,2048]{1,0:T(8,128)(2,1)S(1)} %get-tuple-element.95), channel_id=1, source_target_pairs={{0,6},{1,7},{2,0},{3,1},{4,2},{5,3},{6,4},{7,5},{8,14},{9,15},{10,... | collective-permute-start | bytes 393224 | tf_op jit(solution)/shard_map/z-1y0/ppermute | solution.py:39
  204.0 6.6 %outer_down.1 = bf16[2,512,2048]{2,1,0:T(8,128)(2,1)} custom-call(bf16[256,1024]{1,0:T(8,128)(2,1)S(1)} %copy-done.3, bf16[256,1024]{1,0:T(8,128)(2,1)S(1)} %copy-done.8, bf16[256,1024]{1,0:T(8,128)(2,1)S(1)} %copy-done.16, bf16[256,1024]{1,0:T(8,128)(2,1)S(1)} %copy-done.18, bf16[256,2048]{1,0:T(8,128)(2,1)S(1)} %copy-done.1, ...), custom_call_target="tpu_custom_call" | custom-call | flops 4294967296 | tf_op jit(solution)/shard_map/outer_down/pallas_call | solution.py:242
  210.7 6.6 %outer_up.1 = bf16[2,2048,512]{2,1,0:T(8,128)(2,1)} custom-call(bf16[256,2048]{1,0:T(8,128)(2,1)S(1)} %copy-done, bf16[256,2048]{1,0:T(8,128)(2,1)S(1)} %copy-done.5, bf16[256,2048]{1,0:T(8,128)(2,1)S(1)} %copy-done.10, bf16[256,2048]{1,0:T(8,128)(2,1)S(1)} %copy-done.13, bf16[256,1024]{1,0:T(8,128)(2,1)S(1)} %copy-done.2, bf16[256,1024]{1,0:T(8,128)(2,1)S(1)} %copy-done.7, ...), custom_call_target="tpu_custom_call" | custom-call | flops 4294967296 | tf_op jit(solution)/shard_map/outer_up/pallas_call | solution.py:242
  (183 shorter events, 54.5 us)
Async XLA Ops:
  3.3 23.8 %collective-permute-start.2 = (bf16[32,4352]{1,0:T(8,128)(2,1)}, bf16[32,4352]{1,0:T(8,128)(2,1)S(1)}, u32[]{:S(2)}, u32[]{:S(2)}) collective-permute-start(bf16[32,4352]{1,0:T(8,128)(2,1)} %get-tuple-element.67.refs_0_.refs_6_.refs_12_.refs_11_), channel_id=1, source_target_pairs={{0,4},{1,5},{2,6},{3,7},{4,0},{5,1},{6,2},{7,3},{8,12},{9,13},{10,... | collective-permute-start | bytes 835592 | tf_op jit(solution)/shard_map/z2y0/ppermute | solution.py:39
  7.4 21.6 %collective-permute-start.1 = (bf16[32,4352]{1,0:T(8,128)(2,1)}, bf16[32,4352]{1,0:T(8,128)(2,1)S(1)}, u32[]{:S(2)}, u32[]{:S(2)}) collective-permute-start(bf16[32,4352]{1,0:T(8,128)(2,1)} %get-tuple-element.67.refs_0_.refs_6_.refs_12_.refs_11_), channel_id=1, source_target_pairs={{0,2},{1,3},{2,4},{3,5},{4,6},{5,7},{6,0},{7,1},{8,10},{9,11},{10,... | collective-permute-start | bytes 835592 | tf_op jit(solution)/shard_map/z1y0/ppermute | solution.py:39
  9.0 20.0 %collective-permute-start = (bf16[32,4352]{1,0:T(8,128)(2,1)}, bf16[32,4352]{1,0:T(8,128)(2,1)S(1)}, u32[]{:S(2)}, u32[]{:S(2)}) collective-permute-start(bf16[32,4352]{1,0:T(8,128)(2,1)} %get-tuple-element.67.refs_0_.refs_6_.refs_12_.refs_11_), channel_id=1, source_target_pairs={{0,6},{1,7},{2,0},{3,1},{4,2},{5,3},{6,4},{7,5},{8,14},{9,15},{10,... | collective-permute-start | bytes 835592 | tf_op jit(solution)/shard_map/z3y0/ppermute | solution.py:39
  12.2 22.7 %collective-permute-start.5 = (bf16[64,2048]{1,0:T(8,128)(2,1)S(1)}, bf16[64,2048]{1,0:T(8,128)(2,1)S(1)}, u32[]{:S(2)}, u32[]{:S(2)}) collective-permute-start(bf16[64,2048]{1,0:T(8,128)(2,1)S(1)} %slice_bitcast_fusion.refs_0_), channel_id=1, source_target_pairs={{0,1},{1,0},{2,3},{3,2},{4,5},{5,4},{6,7},{7,6},{8,9},{9,8},{10,11... | collective-permute-start | bytes 786440 | tf_op jit(solution)/shard_map/z0y1/ppermute | solution.py:39
  13.8 25.0 %collective-permute-start.3 = (bf16[32,4352]{1,0:T(8,128)(2,1)}, bf16[32,4352]{1,0:T(8,128)(2,1)S(1)}, u32[]{:S(2)}, u32[]{:S(2)}) collective-permute-start(bf16[32,4352]{1,0:T(8,128)(2,1)} %get-tuple-element.67.refs_0_.refs_6_.refs_12_.refs_11_), channel_id=1, source_target_pairs={{0,1},{1,0},{2,3},{3,2},{4,5},{5,4},{6,7},{7,6},{8,9},{9,8},{10,11... | collective-permute-start | bytes 835592 | tf_op jit(solution)/shard_map/z0y1/ppermute | solution.py:39
  29.0 24.2 %collective-permute-start.10 = (bf16[32,4096]{1,0:T(8,128)(2,1)}, bf16[32,4096]{1,0:T(8,128)(2,1)S(1)}, u32[]{:S(2)}, u32[]{:S(2)}) collective-permute-start(bf16[32,4096]{1,0:T(8,128)(2,1)} %get-tuple-element.77.refs_0_.refs_6_), channel_id=1, source_target_pairs={{0,4},{1,5},{2,6},{3,7},{4,0},{5,1},{6,2},{7,3},{8,12},{9,13},{10,... | collective-permute-start | bytes 786440 | tf_op jit(solution)/shard_map/z2y0/ppermute | solution.py:39
  34.9 18.3 %collective-permute-start.9 = (bf16[32,4096]{1,0:T(8,128)(2,1)}, bf16[32,4096]{1,0:T(8,128)(2,1)S(1)}, u32[]{:S(2)}, u32[]{:S(2)}) collective-permute-start(bf16[32,4096]{1,0:T(8,128)(2,1)} %get-tuple-element.77.refs_0_.refs_6_), channel_id=1, source_target_pairs={{0,2},{1,3},{2,4},{3,5},{4,6},{5,7},{6,0},{7,1},{8,10},{9,11},{10,... | collective-permute-start | bytes 786440 | tf_op jit(solution)/shard_map/z1y0/ppermute | solution.py:39
  34.9 19.1 %collective-permute-start.8 = (bf16[32,4096]{1,0:T(8,128)(2,1)}, bf16[32,4096]{1,0:T(8,128)(2,1)S(1)}, u32[]{:S(2)}, u32[]{:S(2)}) collective-permute-start(bf16[32,4096]{1,0:T(8,128)(2,1)} %get-tuple-element.77.refs_0_.refs_6_), channel_id=1, source_target_pairs={{0,6},{1,7},{2,0},{3,1},{4,2},{5,3},{6,4},{7,5},{8,14},{9,15},{10,... | collective-permute-start | bytes 786440 | tf_op jit(solution)/shard_map/z3y0/ppermute | solution.py:39
  38.8 25.0 %collective-permute-start.6 = (bf16[96,4352]{1,0:T(8,128)(2,1)S(1)}, bf16[96,4352]{1,0:T(8,128)(2,1)}, u32[]{:S(2)}, u32[]{:S(2)}) collective-permute-start(bf16[96,4352]{1,0:T(8,128)(2,1)S(1)} %pad_maximum_fusion), channel_id=1, source_target_pairs={{0,1},{1,0},{2,3},{3,2},{4,5},{5,4},{6,7},{7,6},{8,9},{9,8},{10,11... | collective-permute-start | bytes 2506760 | tf_op jit(solution)/shard_map/z0y1/ppermute | solution.py:39
  54.1 24.2 %collective-permute-start.17 = (bf16[96,4096]{1,0:T(8,128)(2,1)S(1)}, bf16[96,4096]{1,0:T(8,128)(2,1)}, u32[]{:S(2)}, u32[]{:S(2)}) collective-permute-start(bf16[96,4096]{1,0:T(8,128)(2,1)S(1)} %pad_maximum_fusion.1), channel_id=1, source_target_pairs={{0,1},{1,0},{2,3},{3,2},{4,5},{5,4},{6,7},{7,6},{8,9},{9,8},{10,11... | collective-permute-start | bytes 2359304 | tf_op jit(solution)/shard_map/z0y1/ppermute | solution.py:39
  55.7 22.6 %collective-permute-start.13 = (bf16[64,2048]{1,0:T(8,128)(2,1)S(1)}, bf16[64,2048]{1,0:T(8,128)(2,1)}, u32[]{:S(2)}, u32[]{:S(2)}) collective-permute-start(bf16[64,2048]{1,0:T(8,128)(2,1)S(1)} %slice_bitcast_fusion.refs_0_), channel_id=1, source_target_pairs={{0,4},{1,5},{2,6},{3,7},{4,0},{5,1},{6,2},{7,3},{8,12},{9,13},{10,... | collective-permute-start | bytes 786440 | tf_op jit(solution)/shard_map/z2y0/ppermute | solution.py:39
  59.8 18.5 %collective-permute-start.12 = (bf16[64,2048]{1,0:T(8,128)(2,1)S(1)}, bf16[64,2048]{1,0:T(8,128)(2,1)}, u32[]{:S(2)}, u32[]{:S(2)}) collective-permute-start(bf16[64,2048]{1,0:T(8,128)(2,1)S(1)} %slice_bitcast_fusion.refs_0_), channel_id=1, source_target_pairs={{0,2},{1,3},{2,4},{3,5},{4,6},{5,7},{6,0},{7,1},{8,10},{9,11},{10,... | collective-permute-start | bytes 786440 | tf_op jit(solution)/shard_map/z1y0/ppermute | solution.py:39
  60.7 17.6 %collective-permute-start.11 = (bf16[64,2048]{1,0:T(8,128)(2,1)S(1)}, bf16[64,2048]{1,0:T(8,128)(2,1)}, u32[]{:S(2)}, u32[]{:S(2)}) collective-permute-start(bf16[64,2048]{1,0:T(8,128)(2,1)S(1)} %slice_bitcast_fusion.refs_0_), channel_id=1, source_target_pairs={{0,6},{1,7},{2,0},{3,1},{4,2},{5,3},{6,4},{7,5},{8,14},{9,15},{10,... | collective-permute-start | bytes 786440 | tf_op jit(solution)/shard_map/z3y0/ppermute | solution.py:39
  74.4 15.1 %collective-permute-start.7 = (bf16[128,2048]{1,0:T(8,128)(2,1)}, bf16[128,2048]{1,0:T(8,128)(2,1)S(1)}, u32[]{:S(2)}, u32[]{:S(2)}) collective-permute-start(bf16[128,2048]{1,0:T(8,128)(2,1)} %get-tuple-element.71), channel_id=1, source_target_pairs={{0,1},{1,0},{2,3},{3,2},{4,5},{5,4},{6,7},{7,6},{8,9},{9,8},{10,11... | collective-permute-start | bytes 1572872 | tf_op jit(solution)/shard_map/z0y-1/ppermute | solution.py:39
  90.3 20.2 %collective-permute-start.14 = (bf16[32,2048]{1,0:T(8,128)(2,1)S(1)}, bf16[32,2048]{1,0:T(8,128)(2,1)S(1)}, u32[]{:S(2)}, u32[]{:S(2)}) collective-permute-start(bf16[32,2048]{1,0:T(8,128)(2,1)S(1)} %get-tuple-element.74), channel_id=1, source_target_pairs={{0,2},{1,3},{2,4},{3,5},{4,6},{5,7},{6,0},{7,1},{8,10},{9,11},{10,... | collective-permute-start | bytes 393224 | tf_op jit(solution)/shard_map/z-3y0/ppermute | solution.py:39
  95.6 17.8 %collective-permute-start.15 = (bf16[32,2048]{1,0:T(8,128)(2,1)}, bf16[32,2048]{1,0:T(8,128)(2,1)S(1)}, u32[]{:S(2)}, u32[]{:S(2)}) collective-permute-start(bf16[32,2048]{1,0:T(8,128)(2,1)} %get-tuple-element.75), channel_id=1, source_target_pairs={{0,6},{1,7},{2,0},{3,1},{4,2},{5,3},{6,4},{7,5},{8,14},{9,15},{10,... | collective-permute-start | bytes 393224 | tf_op jit(solution)/shard_map/z-1y0/ppermute | solution.py:39
  95.6 17.8 %collective-permute-start.16 = (bf16[32,2048]{1,0:T(8,128)(2,1)S(1)}, bf16[32,2048]{1,0:T(8,128)(2,1)S(1)}, u32[]{:S(2)}, u32[]{:S(2)}) collective-permute-start(bf16[32,2048]{1,0:T(8,128)(2,1)S(1)} %get-tuple-element.76), channel_id=1, source_target_pairs={{0,4},{1,5},{2,6},{3,7},{4,0},{5,1},{6,2},{7,3},{8,12},{9,13},{10,... | collective-permute-start | bytes 393224 | tf_op jit(solution)/shard_map/z-2y0/ppermute | solution.py:39
  128.6 23.2 %collective-permute-start.23 = (bf16[192,2048]{1,0:T(8,128)(2,1)S(1)}, bf16[192,2048]{1,0:T(8,128)(2,1)S(1)}, u32[]{:S(2)}, u32[]{:S(2)}) collective-permute-start(bf16[192,2048]{1,0:T(8,128)(2,1)S(1)} %pad_maximum_fusion.2), channel_id=1, source_target_pairs={{0,1},{1,0},{2,3},{3,2},{4,5},{5,4},{6,7},{7,6},{8,9},{9,8},{10,11... | collective-permute-start | bytes 2359304 | tf_op jit(solution)/shard_map/z0y1/ppermute | solution.py:39
  133.6 26.7 %collective-permute-start.27 = (bf16[128,2048]{1,0:T(8,128)(2,1)S(1)}, bf16[128,2048]{1,0:T(8,128)(2,1)S(1)}, u32[]{:S(2)}, u32[]{:S(2)}) collective-permute-start(bf16[128,2048]{1,0:T(8,128)(2,1)S(1)} %pad_maximum_fusion.3), channel_id=1, source_target_pairs={{0,1},{1,0},{2,3},{3,2},{4,5},{5,4},{6,7},{7,6},{8,9},{9,8},{10,11... | collective-permute-start | bytes 1572872 | tf_op jit(solution)/shard_map/z0y1/ppermute | solution.py:39
  150.6 22.7 %collective-permute-start.36 = (bf16[128,2048]{1,0:T(8,128)(2,1)S(1)}, bf16[128,2048]{1,0:T(8,128)(2,1)}, u32[]{:S(2)}, u32[]{:S(2)}) collective-permute-start(bf16[128,2048]{1,0:T(8,128)(2,1)S(1)} %pad_maximum_fusion.4), channel_id=1, source_target_pairs={{0,1},{1,0},{2,3},{3,2},{4,5},{5,4},{6,7},{7,6},{8,9},{9,8},{10,11... | collective-permute-start | bytes 1572872 | tf_op jit(solution)/shard_map/z0y1/ppermute | solution.py:39
  184.2 14.5 %collective-permute-start.37 = (bf16[128,2048]{1,0:T(8,128)(2,1)}, bf16[128,2048]{1,0:T(8,128)(2,1)S(1)}, u32[]{:S(2)}, u32[]{:S(2)}) collective-permute-start(bf16[128,2048]{1,0:T(8,128)(2,1)} %get-tuple-element.93), channel_id=1, source_target_pairs={{0,1},{1,0},{2,3},{3,2},{4,5},{5,4},{6,7},{7,6},{8,9},{9,8},{10,11... | collective-permute-start | bytes 1572872 | tf_op jit(solution)/shard_map/z0y-1/ppermute | solution.py:39
  199.5 17.7 %collective-permute-start.38 = (bf16[32,2048]{1,0:T(8,128)(2,1)S(1)}, bf16[32,2048]{1,0:T(8,128)(2,1)S(1)}, u32[]{:S(2)}, u32[]{:S(2)}) collective-permute-start(bf16[32,2048]{1,0:T(8,128)(2,1)S(1)} %get-tuple-element.94), channel_id=1, source_target_pairs={{0,2},{1,3},{2,4},{3,5},{4,6},{5,7},{6,0},{7,1},{8,10},{9,11},{10,... | collective-permute-start | bytes 393224 | tf_op jit(solution)/shard_map/z-3y0/ppermute | solution.py:39
  199.6 17.7 %collective-permute-start.39 = (bf16[32,2048]{1,0:T(8,128)(2,1)S(1)}, bf16[32,2048]{1,0:T(8,128)(2,1)S(1)}, u32[]{:S(2)}, u32[]{:S(2)}) collective-permute-start(bf16[32,2048]{1,0:T(8,128)(2,1)S(1)} %get-tuple-element.95), channel_id=1, source_target_pairs={{0,6},{1,7},{2,0},{3,1},{4,2},{5,3},{6,4},{7,5},{8,14},{9,15},{10,... | collective-permute-start | bytes 393224 | tf_op jit(solution)/shard_map/z-1y0/ppermute | solution.py:39
  203.4 13.9 %collective-permute-start.40 = (bf16[32,2048]{1,0:T(8,128)(2,1)S(1)}, bf16[32,2048]{1,0:T(8,128)(2,1)S(1)}, u32[]{:S(2)}, u32[]{:S(2)}) collective-permute-start(bf16[32,2048]{1,0:T(8,128)(2,1)S(1)} %get-tuple-element.96), channel_id=1, source_target_pairs={{0,4},{1,5},{2,6},{3,7},{4,0},{5,1},{6,2},{7,3},{8,12},{9,13},{10,... | collective-permute-start | bytes 393224 | tf_op jit(solution)/shard_map/z-2y0/ppermute | solution.py:39
  (66 other events, 906.1 us)

commit v3 on v2

--- a/solution.py
+++ b/solution.py
@@ -387,11 +387,11 @@
     own_a, sums_a = grid.reduce_y(back_a)
     back_b = early_rows(1, after([b0] + zb + mix(yb, fb), zx))
     total_a = grid.reduce_z(own_a, sums_a, turn)
+    fx = grid.near(after(fuse(zx), back_b))
     own_b, sums_b = grid.reduce_y(back_b)
     early_a, sent_a = early_grad(0, total_a)
     move_down = lambda *x: [grid.move_down(x[0], k) for k in grid.along]
-    down_a = turn("z", move_down, sent_a)
-    fx = grid.near(fuse(zx))
+    down_a = turn("z", move_down, after(sent_a, fx))
     second_blocks = [second_in] + zx + mix(yx, fx)
     total_b = grid.reduce_z(own_b, sums_b, straight)
     fa = grid.near(fuse(down_a))

time: 221 us -> 216 us (0.977)
  starting transfers between devices: 86 us -> 80.1 us
    ppermute x33, starting transfers between devices: 68.8 us -> 61.6 us  [move(): return lax.ppermute(x, 'expert', self.pairs(dz, dy))]
  transfers between devices with their start and end apart: 41 -> 41, of which waited for: 13 -> 14; matrix products, arithmetic and copies ran while one was open for 2% -> 3% of each run, Pallas kernels for 28% -> 29%
where the time goes in v3:
time: 216 us; the launch traced here: 213 us
  starting transfers between devices  80.1 us (37%)
  Pallas kernels  64.7 us (30%)
  waiting for transfers between devices  56.3 us (26%)
  local copies, waits for them, and re-layouts  6.57 us (3%)
  other arithmetic  3.85 us (2%)
    ppermute x33, starting transfers between devices, move(): return lax.ppermute(x, 'expert', self.pairs(dz, dy))  61.6 us
    ppermute x33, waiting for transfers between devices, move(): return lax.ppermute(x, 'expert', self.pairs(dz, dy))  44.3 us
    pallas_call x4, Pallas kernels, on_core(): pl.pallas_call(kernel, in_specs=[pl.BlockSpec(memory_space=pltpu.SMEM)] *...  42.4 us
    pallas_call x3, Pallas kernels, outer(): pl.pallas_call(functools.partial(outer_kernel, len(lefts)), in_specs=[spe...  19.7 us
    ppermute x8, starting transfers between devices, move_down(): return lax.ppermute(x, ('section', 'expert'), pairs)  18.5 us
    ppermute x8, waiting for transfers between devices, move_down(): return lax.ppermute(x, ('section', 'expert'), pairs)  12 us
  transfers between devices with their start and end apart: 41, of which 14 were waited for; matrix products, arithmetic and copies ran while one was open for 3% of the time, Pallas kernels for 29%

profile of v3, /device:TPU:0, one launch (start us, length us, event | category | flops | bytes accessed | tf_op | source)
XLA Modules:
  0.0 213.3 jit_solution(13078647566524047551)
XLA Ops:
  3.3 4.1 %collective-permute-start.2 = (bf16[32,4352]{1,0:T(8,128)(2,1)}, bf16[32,4352]{1,0:T(8,128)(2,1)S(1)}, u32[]{:S(2)}, u32[]{:S(2)}) collective-permute-start(bf16[32,4352]{1,0:T(8,128)(2,1)} %get-tuple-element.69.refs_0_.refs_6_.refs_12_.refs_11_), channel_id=1, source_target_pairs={{0,4},{1,5},{2,6},{3,7},{4,0},{5,1},{6,2},{7,3},{8,12},{9,13},{10,... | collective-permute-start | bytes 835592 | tf_op jit(solution)/shard_map/z2y0/ppermute | solution.py:39
  14.3 12.8 %collective-permute-done.2.refs_3_.refs_9_.refs_15_.refs_14_ = bf16[32,4352]{1,0:T(8,128)(2,1)S(1)} collective-permute-done((bf16[32,4352]{1,0:T(8,128)(2,1)}, bf16[32,4352]{1,0:T(8,128)(2,1)S(1)}, u32[]{:S(2)}, u32[]{:S(2)}) %collective-permute-start.2) | collective-permute-done | bytes 278560 | tf_op jit(solution)/shard_map/z2y0/ppermute | solution.py:39
  29.1 4.9 %collective-permute-done.4.refs_4_.refs_10_ = bf16[32,4096]{1,0:T(8,128)(2,1)S(1)} collective-permute-done((bf16[32,4096]{1,0:T(8,128)(2,1)}, bf16[32,4096]{1,0:T(8,128)(2,1)S(1)}, u32[]{:S(2)}, u32[]{:S(2)}) %collective-permute-start.4) | collective-permute-done | bytes 262176 | tf_op jit(solution)/shard_map/z0y1/ppermute | solution.py:39
  36.5 3.8 %collective-permute-start.8 = (bf16[32,4096]{1,0:T(8,128)(2,1)S(1)}, bf16[32,4096]{1,0:T(8,128)(2,1)S(1)}, u32[]{:S(2)}, u32[]{:S(2)}) collective-permute-start(bf16[32,4096]{1,0:T(8,128)(2,1)S(1)} %copy-done.51), channel_id=1, source_target_pairs={{0,6},{1,7},{2,0},{3,1},{4,2},{5,3},{6,4},{7,5},{8,14},{9,15},{10,... | collective-permute-start | bytes 786440 | tf_op jit(solution)/shard_map/z3y0/ppermute | solution.py:39
  40.4 14.1 %collective-permute-done.10.refs_3_.refs_9_ = bf16[32,4096]{1,0:T(8,128)(2,1)S(1)} collective-permute-done((bf16[32,4096]{1,0:T(8,128)(2,1)S(1)}, bf16[32,4096]{1,0:T(8,128)(2,1)S(1)}, u32[]{:S(2)}, u32[]{:S(2)}) %collective-permute-start.10) | collective-permute-done | bytes 262176 | tf_op jit(solution)/shard_map/z2y0/ppermute | solution.py:39
  55.8 4.3 %collective-permute-start.13 = (bf16[64,2048]{1,0:T(8,128)(2,1)S(1)}, bf16[64,2048]{1,0:T(8,128)(2,1)S(1)}, u32[]{:S(2)}, u32[]{:S(2)}) collective-permute-start(bf16[64,2048]{1,0:T(8,128)(2,1)S(1)} %slice_bitcast_fusion.refs_0_), channel_id=1, source_target_pairs={{0,4},{1,5},{2,6},{3,7},{4,0},{5,1},{6,2},{7,3},{8,12},{9,13},{10,... | collective-permute-start | bytes 786440 | tf_op jit(solution)/shard_map/z2y0/ppermute | solution.py:39
  64.0 10.6 %expert_rows.4 = (bf16[256,2048]{1,0:T(8,128)(2,1)}, bf16[256,2048]{1,0:T(8,128)(2,1)}, bf16[256,1024]{1,0:T(8,128)(2,1)}, bf16[256,1024]{1,0:T(8,128)(2,1)}, bf...) custom-call(s32[1]{0:T(128)} %bitcast.1.me, ...), custom_call_target="tpu_custom_call" | custom-call | flops 5368709120 | tf_op jit(solution)/shard_map/expert_rows/pallas_call | solution.py:75
  78.6 10.7 %expert_rows.5 = (bf16[256,2048]{1,0:T(8,128)(2,1)}, bf16[256,2048]{1,0:T(8,128)(2,1)}, bf16[256,1024]{1,0:T(8,128)(2,1)}, bf16[256,1024]{1,0:T(8,128)(2,1)}, bf...) custom-call(s32[1]{0:T(128)} %bitcast.1.me, ...), custom_call_target="tpu_custom_call" | custom-call | flops 5368709120 | tf_op jit(solution)/shard_map/expert_rows/pallas_call | solution.py:75
  92.3 5.0 %collective-permute-start.14 = (bf16[32,2048]{1,0:T(8,128)(2,1)S(1)}, bf16[32,2048]{1,0:T(8,128)(2,1)S(1)}, u32[]{:S(2)}, u32[]{:S(2)}) collective-permute-start(bf16[32,2048]{1,0:T(8,128)(2,1)S(1)} %get-tuple-element.76), channel_id=1, source_target_pairs={{0,2},{1,3},{2,4},{3,5},{4,6},{5,7},{6,0},{7,1},{8,10},{9,11},{10,... | collective-permute-start | bytes 393224 | tf_op jit(solution)/shard_map/z-3y0/ppermute | solution.py:39
  97.2 3.9 %collective-permute-start.16 = (bf16[32,2048]{1,0:T(8,128)(2,1)}, bf16[32,2048]{1,0:T(8,128)(2,1)}, u32[]{:S(2)}, u32[]{:S(2)}) collective-permute-start(bf16[32,2048]{1,0:T(8,128)(2,1)} %get-tuple-element.78), channel_id=1, source_target_pairs={{0,4},{1,5},{2,6},{3,7},{4,0},{5,1},{6,2},{7,3},{8,12},{9,13},{10,... | collective-permute-start | bytes 393224 | tf_op jit(solution)/shard_map/z-2y0/ppermute | solution.py:39
  101.2 3.3 %collective-permute-done.18 = bf16[128,2048]{1,0:T(8,128)(2,1)S(1)} collective-permute-done((bf16[128,2048]{1,0:T(8,128)(2,1)}, bf16[128,2048]{1,0:T(8,128)(2,1)S(1)}, u32[]{:S(2)}, u32[]{:S(2)}) %collective-permute-start.18) | collective-permute-done | bytes 524320 | tf_op jit(solution)/shard_map/z0y-1/ppermute | solution.py:39
  105.4 4.9 %collective-permute-start.19 = (bf16[32,2048]{1,0:T(8,128)(2,1)}, bf16[32,2048]{1,0:T(8,128)(2,1)}, u32[]{:S(2)}, u32[]{:S(2)}) collective-permute-start(bf16[32,2048]{1,0:T(8,128)(2,1)} %get-tuple-element.156), channel_id=1, source_target_pairs={{0,2},{1,3},{2,4},{3,5},{4,6},{5,7},{6,0},{7,1},{8,10},{9,11},{10,... | collective-permute-start | bytes 393224 | tf_op jit(solution)/shard_map/z-3y0/ppermute | solution.py:39
  115.1 4.2 %collective-permute-done.21 = bf16[32,2048]{1,0:T(8,128)(2,1)} collective-permute-done((bf16[32,2048]{1,0:T(8,128)(2,1)}, bf16[32,2048]{1,0:T(8,128)(2,1)}, u32[]{:S(2)}, u32[]{:S(2)}) %collective-permute-start.21) | collective-permute-done | bytes 131104 | tf_op jit(solution)/shard_map/z-2y0/ppermute | solution.py:39
  120.8 5.9 %collective-permute-start.26 = (bf16[32,2048]{1,0:T(8,128)(2,1)S(1)}, bf16[32,2048]{1,0:T(8,128)(2,1)S(1)}, u32[]{:S(2)}, u32[]{:S(2)}) collective-permute-start(bf16[32,2048]{1,0:T(8,128)(2,1)S(1)} %get-tuple-element.89), channel_id=1, source_target_pairs={{0,28},{1,29},{2,30},{3,31},{4,24},{5,25},{6,26},{7,27},{8,4},{9,5... | collective-permute-start | bytes 393224 | tf_op jit(solution)/shard_map/down_z2/ppermute | solution.py:49
  133.4 3.8 %collective-permute-done.24.refs_7_ = bf16[32,2048]{1,0:T(8,128)(2,1)S(1)} collective-permute-done((bf16[32,2048]{1,0:T(8,128)(2,1)S(1)}, bf16[32,2048]{1,0:T(8,128)(2,1)S(1)}, u32[]{:S(2)}, u32[]{:S(2)}) %collective-permute-start.24) | collective-permute-done | bytes 131104 | tf_op jit(solution)/shard_map/down_z3/ppermute | solution.py:49
  139.1 3.1 %collective-permute-start.31 = (bf16[32,2048]{1,0:T(8,128)(2,1)S(1)}, bf16[32,2048]{1,0:T(8,128)(2,1)S(1)}, u32[]{:S(2)}, u32[]{:S(2)}) collective-permute-start(bf16[32,2048]{1,0:T(8,128)(2,1)S(1)} %get-tuple-element.92), channel_id=1, source_target_pairs={{0,26},{1,27},{2,28},{3,29},{4,30},{5,31},{6,24},{7,25},{8,2},{9,3... | collective-permute-start | bytes 393224 | tf_op jit(solution)/shard_map/down_z1/ppermute | solution.py:49
  143.0 3.0 %collective-permute-start.29 = (bf16[32,2048]{1,0:T(8,128)(2,1)S(1)}, bf16[32,2048]{1,0:T(8,128)(2,1)S(1)}, u32[]{:S(2)}, u32[]{:S(2)}) collective-permute-start(bf16[32,2048]{1,0:T(8,128)(2,1)S(1)} %get-tuple-element.92), channel_id=1, source_target_pairs={{0,24},{1,25},{2,26},{3,27},{4,28},{5,29},{6,30},{7,31},{8,0},{9,1... | collective-permute-start | bytes 393224 | tf_op jit(solution)/shard_map/down_z0/ppermute | solution.py:49
  146.1 4.7 %collective-permute-done.32.refs_9_ = bf16[32,2048]{1,0:T(8,128)(2,1)S(1)} collective-permute-done((bf16[32,2048]{1,0:T(8,128)(2,1)S(1)}, bf16[32,2048]{1,0:T(8,128)(2,1)S(1)}, u32[]{:S(2)}, u32[]{:S(2)}) %collective-permute-start.32) | collective-permute-done | bytes 131104 | tf_op jit(solution)/shard_map/down_z2/ppermute | solution.py:49
  154.3 10.4 %expert_rows.6 = (bf16[256,2048]{1,0:T(8,128)(2,1)}, bf16[256,2048]{1,0:T(8,128)(2,1)}, bf16[256,1024]{1,0:T(8,128)(2,1)}, bf16[256,1024]{1,0:T(8,128)(2,1)}, bf...) custom-call(s32[1]{0:T(128)} %bitcast.1.me, bf16[64,2048]{1,0:T(8,128)(2,1)} %copy-done.34, ...), custom_call_target="tpu_custom_call" | custom-call | flops 5368709120 | tf_op jit(solution)/shard_map/expert_rows/pallas_call | solution.py:75
  167.9 10.7 %expert_rows.7 = (bf16[256,2048]{1,0:T(8,128)(2,1)}, bf16[256,2048]{1,0:T(8,128)(2,1)}, bf16[256,1024]{1,0:T(8,128)(2,1)}, bf16[256,1024]{1,0:T(8,128)(2,1)}, bf...) custom-call(s32[1]{0:T(128)} %bitcast.1.me, bf16[64,2048]{1,0:T(8,128)(2,1)} %copy-done.34, ...), custom_call_target="tpu_custom_call" | custom-call | flops 5368709120 | tf_op jit(solution)/shard_map/expert_rows/pallas_call | solution.py:75
  186.2 6.6 %outer_gate.1 = bf16[2,2048,512]{2,1,0:T(8,128)(2,1)} custom-call(bf16[256,2048]{1,0:T(8,128)(2,1)S(1)} %copy-done, bf16[256,2048]{1,0:T(8,128)(2,1)S(1)} %copy-done.5, bf16[256,2048]{1,0:T(8,128)(2,1)S(1)} %copy-done.10, bf16[256,2048]{1,0:T(8,128)(2,1)S(1)} %copy-done.12, bf16[256,1024]{1,0:T(8,128)(2,1)S(1)} %copy-done.4, ...), custom_call_target="tpu_custom_call" | custom-call | flops 4294967296 | tf_op jit(solution)/shard_map/outer_gate/pallas_call | solution.py:242
  194.8 3.8 %collective-permute-start.39 = (bf16[32,2048]{1,0:T(8,128)(2,1)S(1)}, bf16[32,2048]{1,0:T(8,128)(2,1)S(1)}, u32[]{:S(2)}, u32[]{:S(2)}) collective-permute-start(bf16[32,2048]{1,0:T(8,128)(2,1)S(1)} %get-tuple-element.99), channel_id=1, source_target_pairs={{0,6},{1,7},{2,0},{3,1},{4,2},{5,3},{6,4},{7,5},{8,14},{9,15},{10,... | collective-permute-start | bytes 393224 | tf_op jit(solution)/shard_map/z-1y0/ppermute | solution.py:39
  198.8 6.6 %outer_down.1 = bf16[2,512,2048]{2,1,0:T(8,128)(2,1)} custom-call(bf16[256,1024]{1,0:T(8,128)(2,1)S(1)} %copy-done.3, bf16[256,1024]{1,0:T(8,128)(2,1)S(1)} %copy-done.8, bf16[256,1024]{1,0:T(8,128)(2,1)S(1)} %copy-done.16, bf16[256,1024]{1,0:T(8,128)(2,1)S(1)} %copy-done.18, bf16[256,2048]{1,0:T(8,128)(2,1)S(1)} %copy-done.1, ...), custom_call_target="tpu_custom_call" | custom-call | flops 4294967296 | tf_op jit(solution)/shard_map/outer_down/pallas_call | solution.py:242
  205.5 6.6 %outer_up.1 = bf16[2,2048,512]{2,1,0:T(8,128)(2,1)} custom-call(bf16[256,2048]{1,0:T(8,128)(2,1)S(1)} %copy-done, bf16[256,2048]{1,0:T(8,128)(2,1)S(1)} %copy-done.5, bf16[256,2048]{1,0:T(8,128)(2,1)S(1)} %copy-done.10, bf16[256,2048]{1,0:T(8,128)(2,1)S(1)} %copy-done.13, bf16[256,1024]{1,0:T(8,128)(2,1)S(1)} %copy-done.2, bf16[256,1024]{1,0:T(8,128)(2,1)S(1)} %copy-done.7, ...), custom_call_target="tpu_custom_call" | custom-call | flops 4294967296 | tf_op jit(solution)/shard_map/outer_up/pallas_call | solution.py:242
  (191 shorter events, 59.9 us)
Async XLA Ops:
  3.3 23.8 %collective-permute-start.2 = (bf16[32,4352]{1,0:T(8,128)(2,1)}, bf16[32,4352]{1,0:T(8,128)(2,1)S(1)}, u32[]{:S(2)}, u32[]{:S(2)}) collective-permute-start(bf16[32,4352]{1,0:T(8,128)(2,1)} %get-tuple-element.69.refs_0_.refs_6_.refs_12_.refs_11_), channel_id=1, source_target_pairs={{0,4},{1,5},{2,6},{3,7},{4,0},{5,1},{6,2},{7,3},{8,12},{9,13},{10,... | collective-permute-start | bytes 835592 | tf_op jit(solution)/shard_map/z2y0/ppermute | solution.py:39
  7.4 21.6 %collective-permute-start.1 = (bf16[32,4352]{1,0:T(8,128)(2,1)}, bf16[32,4352]{1,0:T(8,128)(2,1)S(1)}, u32[]{:S(2)}, u32[]{:S(2)}) collective-permute-start(bf16[32,4352]{1,0:T(8,128)(2,1)} %get-tuple-element.69.refs_0_.refs_6_.refs_12_.refs_11_), channel_id=1, source_target_pairs={{0,2},{1,3},{2,4},{3,5},{4,6},{5,7},{6,0},{7,1},{8,10},{9,11},{10,... | collective-permute-start | bytes 835592 | tf_op jit(solution)/shard_map/z1y0/ppermute | solution.py:39
  9.0 20.0 %collective-permute-start = (bf16[32,4352]{1,0:T(8,128)(2,1)}, bf16[32,4352]{1,0:T(8,128)(2,1)S(1)}, u32[]{:S(2)}, u32[]{:S(2)}) collective-permute-start(bf16[32,4352]{1,0:T(8,128)(2,1)} %get-tuple-element.69.refs_0_.refs_6_.refs_12_.refs_11_), channel_id=1, source_target_pairs={{0,6},{1,7},{2,0},{3,1},{4,2},{5,3},{6,4},{7,5},{8,14},{9,15},{10,... | collective-permute-start | bytes 835592 | tf_op jit(solution)/shard_map/z3y0/ppermute | solution.py:39
  11.2 22.7 %collective-permute-start.3 = (bf16[32,4352]{1,0:T(8,128)(2,1)}, bf16[32,4352]{1,0:T(8,128)(2,1)S(1)}, u32[]{:S(2)}, u32[]{:S(2)}) collective-permute-start(bf16[32,4352]{1,0:T(8,128)(2,1)} %get-tuple-element.69.refs_0_.refs_6_.refs_12_.refs_11_), channel_id=1, source_target_pairs={{0,1},{1,0},{2,3},{3,2},{4,5},{5,4},{6,7},{7,6},{8,9},{9,8},{10,11... | collective-permute-start | bytes 835592 | tf_op jit(solution)/shard_map/z0y1/ppermute | solution.py:39
  13.7 15.3 %collective-permute-start.5 = (bf16[64,2048]{1,0:T(8,128)(2,1)S(1)}, bf16[64,2048]{1,0:T(8,128)(2,1)S(1)}, u32[]{:S(2)}, u32[]{:S(2)}) collective-permute-start(bf16[64,2048]{1,0:T(8,128)(2,1)S(1)} %slice_bitcast_fusion.refs_0_), channel_id=1, source_target_pairs={{0,1},{1,0},{2,3},{3,2},{4,5},{5,4},{6,7},{7,6},{8,9},{9,8},{10,11... | collective-permute-start | bytes 786440 | tf_op jit(solution)/shard_map/z0y1/ppermute | solution.py:39
  34.0 30.1 %collective-permute-start.6 = (bf16[96,4352]{1,0:T(8,128)(2,1)S(1)}, bf16[96,4352]{1,0:T(8,128)(2,1)}, u32[]{:S(2)}, u32[]{:S(2)}) collective-permute-start(bf16[96,4352]{1,0:T(8,128)(2,1)S(1)} %pad_maximum_fusion), channel_id=1, source_target_pairs={{0,1},{1,0},{2,3},{3,2},{4,5},{5,4},{6,7},{7,6},{8,9},{9,8},{10,11... | collective-permute-start | bytes 2506760 | tf_op jit(solution)/shard_map/z0y1/ppermute | solution.py:39
  36.2 18.3 %collective-permute-start.10 = (bf16[32,4096]{1,0:T(8,128)(2,1)S(1)}, bf16[32,4096]{1,0:T(8,128)(2,1)S(1)}, u32[]{:S(2)}, u32[]{:S(2)}) collective-permute-start(bf16[32,4096]{1,0:T(8,128)(2,1)S(1)} %copy-done.51), channel_id=1, source_target_pairs={{0,4},{1,5},{2,6},{3,7},{4,0},{5,1},{6,2},{7,3},{8,12},{9,13},{10,... | collective-permute-start | bytes 786440 | tf_op jit(solution)/shard_map/z2y0/ppermute | solution.py:39
  36.5 17.9 %collective-permute-start.9 = (bf16[32,4096]{1,0:T(8,128)(2,1)S(1)}, bf16[32,4096]{1,0:T(8,128)(2,1)S(1)}, u32[]{:S(2)}, u32[]{:S(2)}) collective-permute-start(bf16[32,4096]{1,0:T(8,128)(2,1)S(1)} %copy-done.51), channel_id=1, source_target_pairs={{0,2},{1,3},{2,4},{3,5},{4,6},{5,7},{6,0},{7,1},{8,10},{9,11},{10,... | collective-permute-start | bytes 786440 | tf_op jit(solution)/shard_map/z1y0/ppermute | solution.py:39
  36.5 18.5 %collective-permute-start.8 = (bf16[32,4096]{1,0:T(8,128)(2,1)S(1)}, bf16[32,4096]{1,0:T(8,128)(2,1)S(1)}, u32[]{:S(2)}, u32[]{:S(2)}) collective-permute-start(bf16[32,4096]{1,0:T(8,128)(2,1)S(1)} %copy-done.51), channel_id=1, source_target_pairs={{0,6},{1,7},{2,0},{3,1},{4,2},{5,3},{6,4},{7,5},{8,14},{9,15},{10,... | collective-permute-start | bytes 786440 | tf_op jit(solution)/shard_map/z3y0/ppermute | solution.py:39
  55.1 23.4 %collective-permute-start.17 = (bf16[96,4096]{1,0:T(8,128)(2,1)S(1)}, bf16[96,4096]{1,0:T(8,128)(2,1)}, u32[]{:S(2)}, u32[]{:S(2)}) collective-permute-start(bf16[96,4096]{1,0:T(8,128)(2,1)S(1)} %pad_maximum_fusion.1), channel_id=1, source_target_pairs={{0,1},{1,0},{2,3},{3,2},{4,5},{5,4},{6,7},{7,6},{8,9},{9,8},{10,11... | collective-permute-start | bytes 2359304 | tf_op jit(solution)/shard_map/z0y1/ppermute | solution.py:39
  55.8 22.7 %collective-permute-start.13 = (bf16[64,2048]{1,0:T(8,128)(2,1)S(1)}, bf16[64,2048]{1,0:T(8,128)(2,1)S(1)}, u32[]{:S(2)}, u32[]{:S(2)}) collective-permute-start(bf16[64,2048]{1,0:T(8,128)(2,1)S(1)} %slice_bitcast_fusion.refs_0_), channel_id=1, source_target_pairs={{0,4},{1,5},{2,6},{3,7},{4,0},{5,1},{6,2},{7,3},{8,12},{9,13},{10,... | collective-permute-start | bytes 786440 | tf_op jit(solution)/shard_map/z2y0/ppermute | solution.py:39
  60.0 18.4 %collective-permute-start.12 = (bf16[64,2048]{1,0:T(8,128)(2,1)S(1)}, bf16[64,2048]{1,0:T(8,128)(2,1)S(1)}, u32[]{:S(2)}, u32[]{:S(2)}) collective-permute-start(bf16[64,2048]{1,0:T(8,128)(2,1)S(1)} %slice_bitcast_fusion.refs_0_), channel_id=1, source_target_pairs={{0,2},{1,3},{2,4},{3,5},{4,6},{5,7},{6,0},{7,1},{8,10},{9,11},{10,... | collective-permute-start | bytes 786440 | tf_op jit(solution)/shard_map/z1y0/ppermute | solution.py:39
  61.0 17.5 %collective-permute-start.11 = (bf16[64,2048]{1,0:T(8,128)(2,1)S(1)}, bf16[64,2048]{1,0:T(8,128)(2,1)S(1)}, u32[]{:S(2)}, u32[]{:S(2)}) collective-permute-start(bf16[64,2048]{1,0:T(8,128)(2,1)S(1)} %slice_bitcast_fusion.refs_0_), channel_id=1, source_target_pairs={{0,6},{1,7},{2,0},{3,1},{4,2},{5,3},{6,4},{7,5},{8,14},{9,15},{10,... | collective-permute-start | bytes 786440 | tf_op jit(solution)/shard_map/z3y0/ppermute | solution.py:39
  74.6 16.8 %collective-permute-start.7 = (bf16[128,2048]{1,0:T(8,128)(2,1)}, bf16[128,2048]{1,0:T(8,128)(2,1)S(1)}, u32[]{:S(2)}, u32[]{:S(2)}) collective-permute-start(bf16[128,2048]{1,0:T(8,128)(2,1)} %get-tuple-element.73), channel_id=1, source_target_pairs={{0,1},{1,0},{2,3},{3,2},{4,5},{5,4},{6,7},{7,6},{8,9},{9,8},{10,11... | collective-permute-start | bytes 1572872 | tf_op jit(solution)/shard_map/z0y-1/ppermute | solution.py:39
  89.3 15.1 %collective-permute-start.18 = (bf16[128,2048]{1,0:T(8,128)(2,1)}, bf16[128,2048]{1,0:T(8,128)(2,1)S(1)}, u32[]{:S(2)}, u32[]{:S(2)}) collective-permute-start(bf16[128,2048]{1,0:T(8,128)(2,1)} %get-tuple-element.86), channel_id=1, source_target_pairs={{0,1},{1,0},{2,3},{3,2},{4,5},{5,4},{6,7},{7,6},{8,9},{9,8},{10,11... | collective-permute-start | bytes 1572872 | tf_op jit(solution)/shard_map/z0y-1/ppermute | solution.py:39
  90.9 29.9 %collective-permute-start.22 = (bf16[192,2048]{1,0:T(8,128)(2,1)S(1)}, bf16[192,2048]{1,0:T(8,128)(2,1)}, u32[]{:S(2)}, u32[]{:S(2)}) collective-permute-start(bf16[192,2048]{1,0:T(8,128)(2,1)S(1)} %pad_maximum_fusion.2), channel_id=1, source_target_pairs={{0,1},{1,0},{2,3},{3,2},{4,5},{5,4},{6,7},{7,6},{8,9},{9,8},{10,11... | collective-permute-start | bytes 2359304 | tf_op jit(solution)/shard_map/z0y1/ppermute | solution.py:39
  92.3 18.0 %collective-permute-start.14 = (bf16[32,2048]{1,0:T(8,128)(2,1)S(1)}, bf16[32,2048]{1,0:T(8,128)(2,1)S(1)}, u32[]{:S(2)}, u32[]{:S(2)}) collective-permute-start(bf16[32,2048]{1,0:T(8,128)(2,1)S(1)} %get-tuple-element.76), channel_id=1, source_target_pairs={{0,2},{1,3},{2,4},{3,5},{4,6},{5,7},{6,0},{7,1},{8,10},{9,11},{10,... | collective-permute-start | bytes 393224 | tf_op jit(solution)/shard_map/z-3y0/ppermute | solution.py:39
  97.2 15.0 %collective-permute-start.15 = (bf16[32,2048]{1,0:T(8,128)(2,1)S(1)}, bf16[32,2048]{1,0:T(8,128)(2,1)}, u32[]{:S(2)}, u32[]{:S(2)}) collective-permute-start(bf16[32,2048]{1,0:T(8,128)(2,1)S(1)} %get-tuple-element.77), channel_id=1, source_target_pairs={{0,6},{1,7},{2,0},{3,1},{4,2},{5,3},{6,4},{7,5},{8,14},{9,15},{10,... | collective-permute-start | bytes 393224 | tf_op jit(solution)/shard_map/z-1y0/ppermute | solution.py:39
  97.2 17.9 %collective-permute-start.16 = (bf16[32,2048]{1,0:T(8,128)(2,1)}, bf16[32,2048]{1,0:T(8,128)(2,1)}, u32[]{:S(2)}, u32[]{:S(2)}) collective-permute-start(bf16[32,2048]{1,0:T(8,128)(2,1)} %get-tuple-element.78), channel_id=1, source_target_pairs={{0,4},{1,5},{2,6},{3,7},{4,0},{5,1},{6,2},{7,3},{8,12},{9,13},{10,... | collective-permute-start | bytes 393224 | tf_op jit(solution)/shard_map/z-2y0/ppermute | solution.py:39
  137.5 16.0 %collective-permute-start.27 = (bf16[128,2048]{1,0:T(8,128)(2,1)S(1)}, bf16[128,2048]{1,0:T(8,128)(2,1)S(1)}, u32[]{:S(2)}, u32[]{:S(2)}) collective-permute-start(bf16[128,2048]{1,0:T(8,128)(2,1)S(1)} %pad_maximum_fusion.3), channel_id=1, source_target_pairs={{0,1},{1,0},{2,3},{3,2},{4,5},{5,4},{6,7},{7,6},{8,9},{9,8},{10,11... | collective-permute-start | bytes 1572872 | tf_op jit(solution)/shard_map/z0y1/ppermute | solution.py:39
  152.7 14.5 %collective-permute-start.36 = (bf16[128,2048]{1,0:T(8,128)(2,1)S(1)}, bf16[128,2048]{1,0:T(8,128)(2,1)S(1)}, u32[]{:S(2)}, u32[]{:S(2)}) collective-permute-start(bf16[128,2048]{1,0:T(8,128)(2,1)S(1)} %pad_maximum_fusion.4), channel_id=1, source_target_pairs={{0,1},{1,0},{2,3},{3,2},{4,5},{5,4},{6,7},{7,6},{8,9},{9,8},{10,11... | collective-permute-start | bytes 1572872 | tf_op jit(solution)/shard_map/z0y1/ppermute | solution.py:39
  164.8 14.7 %collective-permute-start.28 = (bf16[128,2048]{1,0:T(8,128)(2,1)}, bf16[128,2048]{1,0:T(8,128)(2,1)S(1)}, u32[]{:S(2)}, u32[]{:S(2)}) collective-permute-start(bf16[128,2048]{1,0:T(8,128)(2,1)} %get-tuple-element.91), channel_id=1, source_target_pairs={{0,1},{1,0},{2,3},{3,2},{4,5},{5,4},{6,7},{7,6},{8,9},{9,8},{10,11... | collective-permute-start | bytes 1572872 | tf_op jit(solution)/shard_map/z0y-1/ppermute | solution.py:39
  194.8 17.2 %collective-permute-start.38 = (bf16[32,2048]{1,0:T(8,128)(2,1)S(1)}, bf16[32,2048]{1,0:T(8,128)(2,1)S(1)}, u32[]{:S(2)}, u32[]{:S(2)}) collective-permute-start(bf16[32,2048]{1,0:T(8,128)(2,1)S(1)} %get-tuple-element.98), channel_id=1, source_target_pairs={{0,2},{1,3},{2,4},{3,5},{4,6},{5,7},{6,0},{7,1},{8,10},{9,11},{10,... | collective-permute-start | bytes 393224 | tf_op jit(solution)/shard_map/z-3y0/ppermute | solution.py:39
  194.8 17.2 %collective-permute-start.39 = (bf16[32,2048]{1,0:T(8,128)(2,1)S(1)}, bf16[32,2048]{1,0:T(8,128)(2,1)S(1)}, u32[]{:S(2)}, u32[]{:S(2)}) collective-permute-start(bf16[32,2048]{1,0:T(8,128)(2,1)S(1)} %get-tuple-element.99), channel_id=1, source_target_pairs={{0,6},{1,7},{2,0},{3,1},{4,2},{5,3},{6,4},{7,5},{8,14},{9,15},{10,... | collective-permute-start | bytes 393224 | tf_op jit(solution)/shard_map/z-1y0/ppermute | solution.py:39
  (70 other events, 878.3 us)

commit v4 on v3

--- a/solution.py
+++ b/solution.py
@@ -9,7 +9,7 @@
 
 LANES = 128
 VMEM_BYTES = 60 * 1024 * 1024
-OUTER_VMEM_BYTES = 20 * 1024 * 1024
+OUTER_VMEM_BYTES = 24 * 1024 * 1024
 NT = (((1,), (1,)), ((), ()))
 TN = (((0,), (0,)), ((), ()))
 BF16 = jnp.bfloat16
@@ -24,7 +24,7 @@
     def __init__(self, count):
         self.ny = max(d for d in range(1, count + 1) if count % d == 0 and d * d <= count)
         self.nz = count // self.ny
-        self.far = sorted(range(1, self.nz), key=lambda k: (min(k, self.nz - k), -k))
+        self.far = sorted(range(1, self.nz), key=lambda k: (min(k, self.nz - k), k))
         self.along = [0] + self.far
 
     def pairs(self, dz, dy):
@@ -217,40 +217,43 @@
     )
 
 
-def outer_kernel(pieces, *refs):
-    lefts, rights = refs[:pieces], refs[pieces : 2 * pieces]
-    out, right = refs[2 * pieces :]
-    local, rows, columns = out.shape
-    start = 0
-    for ref in rights:
-        right[start : start + ref.shape[0], :] = ref[...]
-        start += ref.shape[0]
+def outer_kernel(pieces, count, *refs):
+    lefts, rights, (*outs, right) = refs[:pieces], refs[pieces : (1 + count) * pieces], refs[(1 + count) * pieces :]
+    local, rows, columns = outs[0].shape
+    wide = right.shape[1] // count
+    for i in range(count):
+        start = 0
+        for ref in rights[i * pieces : (i + 1) * pieces]:
+            right[start : start + ref.shape[0], i * wide : (i + 1) * wide] = ref[...]
+            start += ref.shape[0]
     for m in tiles(lefts[0].shape[1]):
         left = jnp.concatenate([ref[:, m] for ref in lefts], axis=0)
         product = dot(left, right[...], TN).astype(BF16)
         if lefts[0].shape[1] == rows:
-            for e in range(local):
-                out[e, m, :] = product[:, e * columns : (e + 1) * columns]
+            for i, out in enumerate(outs):
+                for e in range(local):
+                    at = i * wide + e * columns
+                    out[e, m, :] = product[:, at : at + columns]
         else:
             at = m.start % rows
-            out[m.start // rows, at : at + m.stop - m.start, :] = product
+            outs[0][m.start // rows, at : at + m.stop - m.start, :] = product
 
 
 def outer(lefts, rights, local, rows, columns, name):
-    tokens = sum(x.shape[0] for x in lefts)
+    tokens, count = sum(x.shape[0] for x in lefts), len(rights)
     spec = pl.BlockSpec(memory_space=pltpu.VMEM)
     return pl.pallas_call(
-        functools.partial(outer_kernel, len(lefts)),
-        in_specs=[spec] * (2 * len(lefts)),
-        out_specs=spec,
-        out_shape=jax.ShapeDtypeStruct((local, rows, columns), BF16),
-        scratch_shapes=[pltpu.VMEM((tokens, rights[0].shape[1]), BF16)],
+        functools.partial(outer_kernel, len(lefts), count),
+        in_specs=[spec] * ((1 + count) * len(lefts)),
+        out_specs=[spec] * count,
+        out_shape=[jax.ShapeDtypeStruct((local, rows, columns), BF16)] * count,
+        scratch_shapes=[pltpu.VMEM((tokens, count * rights[0][0].shape[1]), BF16)],
         compiler_params=pltpu.CompilerParams(vmem_limit_bytes=OUTER_VMEM_BYTES),
         cost_estimate=pl.CostEstimate(
-            flops=2 * tokens * local * rows * columns, bytes_accessed=0, transcendentals=0
+            flops=2 * count * tokens * local * rows * columns, bytes_accessed=0, transcendentals=0
         ),
         name=name,
-    )(*lefts, *rights)
+    )(*lefts, *sum(rights, []))
 
 
 def payload_kernel(experts, half, routes, gates, x_in, c_in, *refs):
@@ -396,19 +399,18 @@
     total_b = grid.reduce_z(own_b, sums_b, straight)
     fa = grid.near(fuse(down_a))
     early_b, sent_b = early_grad(1, total_b)
-    down_b = turn("z", move_down, sent_b)
+    down_b = move_down(sent_b)
     late_back_a = late_rows(0, down_a + fa)
     fb = grid.near(fuse(down_b))
     own_a, sums_a = grid.reduce_y(late_back_a)
     late_back_b = late_rows(1, down_b + fb)
-    total_a = grid.reduce_z(own_a, sums_a, turn)
+    total_a = grid.reduce_z(own_a, sums_a, straight)
     own_b, sums_b = grid.reduce_y(late_back_b)
-    total_b = grid.reduce_z(own_b, sums_b, turn)
+    total_b = grid.reduce_z(own_b, sums_b, straight)
     grad_late_a = (down_a[0].astype(F32) + total_a).astype(BF16)
     grad_late_b = (down_b[0].astype(F32) + total_b).astype(BF16)
-    grad_gate = outer(after(xs, late_back_b, sums_a), dgs, local, depth, width, "outer_gate")
-    grad_up = outer(after(xs, sums_b), dus, local, depth, width, "outer_up")
-    grad_down = outer(after(hs, sums_b), cs, local, width, depth, "outer_down")
+    (grad_down,) = outer(after(hs, late_back_a, late_back_b, sums_b), [cs], local, width, depth, "outer_down")
+    grad_gate, grad_up = outer(after(xs, sums_a, total_b), [dgs, dus], local, depth, width, "outer_inputs")
     grad_early = jnp.concatenate([early_a, early_b], axis=0)
     grad_late = jnp.concatenate([grad_late_a, grad_late_b], axis=0)
     return (grad_early[None], grad_late[None], grad_gate[None], grad_up[None], grad_down[None])

time: 216 us -> 206 us (0.954)
  starting transfers between devices: 80.1 us -> 72.7 us
  local copies, waits for them, and re-layouts: 6.57 us -> 4.32 us
    ppermute x8, starting transfers between devices: 18.5 us -> 9.43 us  [move_down(): return lax.ppermute(x, ('section', 'expert'), pairs)]
    ppermute x8, waiting for transfers between devices: 12 us -> 15.4 us  [move_down(): return lax.ppermute(x, ('section', 'expert'), pairs)]
    pallas_call x3 -> x2, Pallas kernels: 19.7 us -> 18.3 us  [outer(): pl.pallas_call(functools.partial(outer_kernel, len(lefts), count), in_spe...]
  transfers between devices with their start and end apart: 41 -> 41, of which waited for: 14 -> 13; matrix products, arithmetic and copies ran while one was open for 3% -> 2% of each run, Pallas kernels for 29% -> 30%
where the time goes in v4:
time: 206 us; the launch traced here: 204 us
  starting transfers between devices  72.7 us (35%)
  Pallas kernels  63.5 us (31%)
  waiting for transfers between devices  57.8 us (28%)
  local copies, waits for them, and re-layouts  4.32 us (2%)
  other arithmetic  3.64 us (2%)
    ppermute x33, starting transfers between devices, move(): return lax.ppermute(x, 'expert', self.pairs(dz, dy))  63.3 us
    pallas_call x4, Pallas kernels, on_core(): pl.pallas_call(kernel, in_specs=[pl.BlockSpec(memory_space=pltpu.SMEM)] *...  42.5 us
    ppermute x33, waiting for transfers between devices, move(): return lax.ppermute(x, 'expert', self.pairs(dz, dy))  42.3 us
    pallas_call x2, Pallas kernels, outer(): pl.pallas_call(functools.partial(outer_kernel, len(lefts), count), in_spe...  18.3 us
    ppermute x8, waiting for transfers between devices, move_down(): return lax.ppermute(x, ('section', 'expert'), pairs)  15.4 us
    ppermute x8, starting transfers between devices, move_down(): return lax.ppermute(x, ('section', 'expert'), pairs)  9.43 us
  transfers between devices with their start and end apart: 41, of which 13 were waited for; matrix products, arithmetic and copies ran while one was open for 2% of the time, Pallas kernels for 30%

profile of v4, /device:TPU:0, one launch (start us, length us, event | category | flops | bytes accessed | tf_op | source)
XLA Modules:
  0.0 203.7 jit_solution(11880152315986382460)
XLA Ops:
  0.6 2.6 %payloads.1 = (bf16[32,4352]{1,0:T(8,128)(2,1)}, bf16[32,4096]{1,0:T(8,128)(2,1)}) custom-call(s32[1,10,2,64]{3,2,1,0:T(2,128)} %bitcast.23, f32[1,10,2,64]{3,2,1,0:T(2,128)} %bitcast.24, bf16[1,2,64,2048]{3,2,1,0:T(8,128)(2,1)} %x_in.1, bf16[1,64,2048]{2,1,0:T(8,128)(2,1)} %c_in.1), custom_call_target="tpu_custom_call" | custom-call | tf_op jit(solution)/shard_map/payloads/pallas_call | solution.py:307
  3.3 4.1 %collective-permute-start.2 = (bf16[32,4352]{1,0:T(8,128)(2,1)}, bf16[32,4352]{1,0:T(8,128)(2,1)S(1)}, u32[]{:S(2)}, u32[]{:S(2)}) collective-permute-start(bf16[32,4352]{1,0:T(8,128)(2,1)} %get-tuple-element.60.refs_0_.refs_6_.refs_12_.refs_11_), channel_id=1, source_target_pairs={{0,4},{1,5},{2,6},{3,7},{4,0},{5,1},{6,2},{7,3},{8,12},{9,13},{10,... | collective-permute-start | bytes 835592 | tf_op jit(solution)/shard_map/z2y0/ppermute | solution.py:39
  12.5 9.5 %collective-permute-done.2.refs_3_.refs_9_.refs_15_.refs_14_ = bf16[32,4352]{1,0:T(8,128)(2,1)S(1)} collective-permute-done((bf16[32,4352]{1,0:T(8,128)(2,1)}, bf16[32,4352]{1,0:T(8,128)(2,1)S(1)}, u32[]{:S(2)}, u32[]{:S(2)}) %collective-permute-start.2) | collective-permute-done | bytes 278560 | tf_op jit(solution)/shard_map/z2y0/ppermute | solution.py:39
  22.0 7.0 %collective-permute-start.4 = (bf16[32,4096]{1,0:T(8,128)(2,1)}, bf16[32,4096]{1,0:T(8,128)(2,1)S(1)}, u32[]{:S(2)}, u32[]{:S(2)}) collective-permute-start(bf16[32,4096]{1,0:T(8,128)(2,1)} %get-tuple-element.70.refs_0_.refs_6_), channel_id=1, source_target_pairs={{0,1},{1,0},{2,3},{3,2},{4,5},{5,4},{6,7},{7,6},{8,9},{9,8},{10,11... | collective-permute-start | bytes 786440 | tf_op jit(solution)/shard_map/z0y1/ppermute | solution.py:39
  29.0 5.9 %collective-permute-start.10 = (bf16[32,4096]{1,0:T(8,128)(2,1)}, bf16[32,4096]{1,0:T(8,128)(2,1)S(1)}, u32[]{:S(2)}, u32[]{:S(2)}) collective-permute-start(bf16[32,4096]{1,0:T(8,128)(2,1)} %get-tuple-element.70.refs_0_.refs_6_), channel_id=1, source_target_pairs={{0,4},{1,5},{2,6},{3,7},{4,0},{5,1},{6,2},{7,3},{8,12},{9,13},{10,... | collective-permute-start | bytes 786440 | tf_op jit(solution)/shard_map/z2y0/ppermute | solution.py:39
  38.6 9.9 %collective-permute-done.10.refs_3_.refs_9_ = bf16[32,4096]{1,0:T(8,128)(2,1)S(1)} collective-permute-done((bf16[32,4096]{1,0:T(8,128)(2,1)}, bf16[32,4096]{1,0:T(8,128)(2,1)S(1)}, u32[]{:S(2)}, u32[]{:S(2)}) %collective-permute-start.10) | collective-permute-done | bytes 262176 | tf_op jit(solution)/shard_map/z2y0/ppermute | solution.py:39
  48.5 5.4 %collective-permute-done.9.refs_2_.refs_8_ = bf16[32,4096]{1,0:T(8,128)(2,1)S(1)} collective-permute-done((bf16[32,4096]{1,0:T(8,128)(2,1)}, bf16[32,4096]{1,0:T(8,128)(2,1)S(1)}, u32[]{:S(2)}, u32[]{:S(2)}) %collective-permute-start.9) | collective-permute-done | bytes 262176 | tf_op jit(solution)/shard_map/z3y0/ppermute | solution.py:39
  55.6 4.3 %collective-permute-start.13 = (bf16[64,2048]{1,0:T(8,128)(2,1)S(1)}, bf16[64,2048]{1,0:T(8,128)(2,1)S(1)}, u32[]{:S(2)}, u32[]{:S(2)}) collective-permute-start(bf16[64,2048]{1,0:T(8,128)(2,1)S(1)} %slice_bitcast_fusion.refs_0_), channel_id=1, source_target_pairs={{0,4},{1,5},{2,6},{3,7},{4,0},{5,1},{6,2},{7,3},{8,12},{9,13},{10,... | collective-permute-start | bytes 786440 | tf_op jit(solution)/shard_map/z2y0/ppermute | solution.py:39
  59.8 3.3 %collective-permute-start.12 = (bf16[64,2048]{1,0:T(8,128)(2,1)S(1)}, bf16[64,2048]{1,0:T(8,128)(2,1)S(1)}, u32[]{:S(2)}, u32[]{:S(2)}) collective-permute-start(bf16[64,2048]{1,0:T(8,128)(2,1)S(1)} %slice_bitcast_fusion.refs_0_), channel_id=1, source_target_pairs={{0,6},{1,7},{2,0},{3,1},{4,2},{5,3},{6,4},{7,5},{8,14},{9,15},{10,... | collective-permute-start | bytes 786440 | tf_op jit(solution)/shard_map/z3y0/ppermute | solution.py:39
  63.3 10.6 %expert_rows.4 = (bf16[256,2048]{1,0:T(8,128)(2,1)}, bf16[256,2048]{1,0:T(8,128)(2,1)}, bf16[256,1024]{1,0:T(8,128)(2,1)}, bf16[256,1024]{1,0:T(8,128)(2,1)}, bf...) custom-call(s32[1]{0:T(128)} %bitcast.1.me, ...), custom_call_target="tpu_custom_call" | custom-call | flops 5368709120 | tf_op jit(solution)/shard_map/expert_rows/pallas_call | solution.py:75
  74.6 5.7 %collective-permute-done.11.refs_1_ = bf16[64,2048]{1,0:T(8,128)(2,1)} collective-permute-done((bf16[64,2048]{1,0:T(8,128)(2,1)S(1)}, bf16[64,2048]{1,0:T(8,128)(2,1)}, u32[]{:S(2)}, u32[]{:S(2)}) %collective-permute-start.11) | collective-permute-done | bytes 262176 | tf_op jit(solution)/shard_map/z1y0/ppermute | solution.py:39
  80.3 10.5 %expert_rows.5 = (bf16[256,2048]{1,0:T(8,128)(2,1)}, bf16[256,2048]{1,0:T(8,128)(2,1)}, bf16[256,1024]{1,0:T(8,128)(2,1)}, bf16[256,1024]{1,0:T(8,128)(2,1)}, bf...) custom-call(s32[1]{0:T(128)} %bitcast.1.me, ...), custom_call_target="tpu_custom_call" | custom-call | flops 5368709120 | tf_op jit(solution)/shard_map/expert_rows/pallas_call | solution.py:75
  95.1 3.8 %collective-permute-start.16 = (bf16[32,2048]{1,0:T(8,128)(2,1)S(1)}, bf16[32,2048]{1,0:T(8,128)(2,1)S(1)}, u32[]{:S(2)}, u32[]{:S(2)}) collective-permute-start(bf16[32,2048]{1,0:T(8,128)(2,1)S(1)} %get-tuple-element.69), channel_id=1, source_target_pairs={{0,4},{1,5},{2,6},{3,7},{4,0},{5,1},{6,2},{7,3},{8,12},{9,13},{10,... | collective-permute-start | bytes 393224 | tf_op jit(solution)/shard_map/z-2y0/ppermute | solution.py:39
  98.9 4.6 %collective-permute-done.18 = bf16[128,2048]{1,0:T(8,128)(2,1)S(1)} collective-permute-done((bf16[128,2048]{1,0:T(8,128)(2,1)}, bf16[128,2048]{1,0:T(8,128)(2,1)S(1)}, u32[]{:S(2)}, u32[]{:S(2)}) %collective-permute-start.18) | collective-permute-done | bytes 524320 | tf_op jit(solution)/shard_map/z0y-1/ppermute | solution.py:39
  105.2 4.7 %collective-permute-start.21 = (bf16[32,2048]{1,0:T(8,128)(2,1)S(1)}, bf16[32,2048]{1,0:T(8,128)(2,1)S(1)}, u32[]{:S(2)}, u32[]{:S(2)}) collective-permute-start(bf16[32,2048]{1,0:T(8,128)(2,1)S(1)} %get-tuple-element.141), channel_id=1, source_target_pairs={{0,4},{1,5},{2,6},{3,7},{4,0},{5,1},{6,2},{7,3},{8,12},{9,13},{10,... | collective-permute-start | bytes 393224 | tf_op jit(solution)/shard_map/z-2y0/ppermute | solution.py:39
  113.9 6.9 %collective-permute-done.21 = bf16[32,2048]{1,0:T(8,128)(2,1)S(1)} collective-permute-done((bf16[32,2048]{1,0:T(8,128)(2,1)S(1)}, bf16[32,2048]{1,0:T(8,128)(2,1)S(1)}, u32[]{:S(2)}, u32[]{:S(2)}) %collective-permute-start.21) | collective-permute-done | bytes 131104 | tf_op jit(solution)/shard_map/z-2y0/ppermute | solution.py:39
  124.1 4.5 %collective-permute-done.35.refs_9_ = bf16[32,2048]{1,0:T(8,128)(2,1)S(1)} collective-permute-done((bf16[32,2048]{1,0:T(8,128)(2,1)S(1)}, bf16[32,2048]{1,0:T(8,128)(2,1)S(1)}, u32[]{:S(2)}, u32[]{:S(2)}) %collective-permute-start.35) | collective-permute-done | bytes 131104 | tf_op jit(solution)/shard_map/down_z2/ppermute | solution.py:49
  131.8 3.6 %collective-permute-start.26 = (bf16[32,2048]{1,0:T(8,128)(2,1)S(1)}, bf16[32,2048]{1,0:T(8,128)(2,1)S(1)}, u32[]{:S(2)}, u32[]{:S(2)}) collective-permute-start(bf16[32,2048]{1,0:T(8,128)(2,1)S(1)} %get-tuple-element.80), channel_id=1, source_target_pairs={{0,28},{1,29},{2,30},{3,31},{4,24},{5,25},{6,26},{7,27},{8,4},{9,5... | collective-permute-start | bytes 393224 | tf_op jit(solution)/shard_map/down_z2/ppermute | solution.py:49
  139.0 2.9 %collective-permute-done.25.refs_8_ = bf16[32,2048]{1,0:T(8,128)(2,1)S(1)} collective-permute-done((bf16[32,2048]{1,0:T(8,128)(2,1)S(1)}, bf16[32,2048]{1,0:T(8,128)(2,1)S(1)}, u32[]{:S(2)}, u32[]{:S(2)}) %collective-permute-start.25) | collective-permute-done | bytes 131104 | tf_op jit(solution)/shard_map/down_z3/ppermute | solution.py:49
  141.9 5.1 %collective-permute-done.24.refs_7_ = bf16[32,2048]{1,0:T(8,128)(2,1)S(1)} collective-permute-done((bf16[32,2048]{1,0:T(8,128)(2,1)S(1)}, bf16[32,2048]{1,0:T(8,128)(2,1)S(1)}, u32[]{:S(2)}, u32[]{:S(2)}) %collective-permute-start.24) | collective-permute-done | bytes 131104 | tf_op jit(solution)/shard_map/down_z1/ppermute | solution.py:49
  148.9 10.5 %expert_rows.7 = (bf16[256,2048]{1,0:T(8,128)(2,1)}, bf16[256,2048]{1,0:T(8,128)(2,1)}, bf16[256,1024]{1,0:T(8,128)(2,1)}, bf16[256,1024]{1,0:T(8,128)(2,1)}, bf...) custom-call(s32[1]{0:T(128)} %bitcast.1.me, bf16[64,2048]{1,0:T(8,128)(2,1)} %copy-done.33, ...), custom_call_target="tpu_custom_call" | custom-call | flops 5368709120 | tf_op jit(solution)/shard_map/expert_rows/pallas_call | solution.py:75
  161.3 10.9 %expert_rows.6 = (bf16[256,2048]{1,0:T(8,128)(2,1)}, bf16[256,2048]{1,0:T(8,128)(2,1)}, bf16[256,1024]{1,0:T(8,128)(2,1)}, bf16[256,1024]{1,0:T(8,128)(2,1)}, bf...) custom-call(s32[1]{0:T(128)} %bitcast.1.me, bf16[64,2048]{1,0:T(8,128)(2,1)} %copy-done.33, ...), custom_call_target="tpu_custom_call" | custom-call | flops 5368709120 | tf_op jit(solution)/shard_map/expert_rows/pallas_call | solution.py:75
  180.6 6.6 %outer_down.1 = bf16[2,512,2048]{2,1,0:T(8,128)(2,1)} custom-call(bf16[256,1024]{1,0:T(8,128)(2,1)S(1)} %copy-done.4, bf16[256,1024]{1,0:T(8,128)(2,1)S(1)} %copy-done.9, bf16[256,1024]{1,0:T(8,128)(2,1)S(1)} %copy-done.19, bf16[256,1024]{1,0:T(8,128)(2,1)S(1)} %copy-done.18, bf16[256,2048]{1,0:T(8,128)(2,1)S(1)} %copy-done.1, ...), custom_call_target="tpu_custom_call" | custom-call | flops 4294967296 | tf_op jit(solution)/shard_map/outer_down/pallas_call | solution.py:245
  190.7 11.7 %outer_inputs.1 = (bf16[2,2048,512]{2,1,0:T(8,128)(2,1)}, bf16[2,2048,512]{2,1,0:T(8,128)(2,1)}) custom-call(bf16[256,2048]{1,0:T(8,128)(2,1)S(1)} %copy-done, bf16[256,2048]{1,0:T(8,128)(2,1)S(1)} %copy-done.5, bf16[256,2048]{1,0:T(8,128)(2,1)S(1)} %copy-done.11, bf16[256,2048]{1,0:T(8,128)(2,1)S(1)} %copy-done.10, bf16[256,1024]{1,0:T(8,128)(2,1)S(1)} %copy-done.2, ...), custom_call_target="tpu_custom_call" | custom-call | flops 8589934592 | tf_op jit(solution)/shard_map/outer_inputs/pallas_call | solution.py:245
  (184 shorter events, 47.3 us)
Async XLA Ops:
  3.3 18.7 %collective-permute-start.2 = (bf16[32,4352]{1,0:T(8,128)(2,1)}, bf16[32,4352]{1,0:T(8,128)(2,1)S(1)}, u32[]{:S(2)}, u32[]{:S(2)}) collective-permute-start(bf16[32,4352]{1,0:T(8,128)(2,1)} %get-tuple-element.60.refs_0_.refs_6_.refs_12_.refs_11_), channel_id=1, source_target_pairs={{0,4},{1,5},{2,6},{3,7},{4,0},{5,1},{6,2},{7,3},{8,12},{9,13},{10,... | collective-permute-start | bytes 835592 | tf_op jit(solution)/shard_map/z2y0/ppermute | solution.py:39
  7.4 21.5 %collective-permute-start.1 = (bf16[32,4352]{1,0:T(8,128)(2,1)}, bf16[32,4352]{1,0:T(8,128)(2,1)S(1)}, u32[]{:S(2)}, u32[]{:S(2)}) collective-permute-start(bf16[32,4352]{1,0:T(8,128)(2,1)} %get-tuple-element.60.refs_0_.refs_6_.refs_12_.refs_11_), channel_id=1, source_target_pairs={{0,6},{1,7},{2,0},{3,1},{4,2},{5,3},{6,4},{7,5},{8,14},{9,15},{10,... | collective-permute-start | bytes 835592 | tf_op jit(solution)/shard_map/z3y0/ppermute | solution.py:39
  8.7 20.2 %collective-permute-start = (bf16[32,4352]{1,0:T(8,128)(2,1)}, bf16[32,4352]{1,0:T(8,128)(2,1)S(1)}, u32[]{:S(2)}, u32[]{:S(2)}) collective-permute-start(bf16[32,4352]{1,0:T(8,128)(2,1)} %get-tuple-element.60.refs_0_.refs_6_.refs_12_.refs_11_), channel_id=1, source_target_pairs={{0,2},{1,3},{2,4},{3,5},{4,6},{5,7},{6,0},{7,1},{8,10},{9,11},{10,... | collective-permute-start | bytes 835592 | tf_op jit(solution)/shard_map/z1y0/ppermute | solution.py:39
  10.4 25.0 %collective-permute-start.5 = (bf16[64,2048]{1,0:T(8,128)(2,1)S(1)}, bf16[64,2048]{1,0:T(8,128)(2,1)S(1)}, u32[]{:S(2)}, u32[]{:S(2)}) collective-permute-start(bf16[64,2048]{1,0:T(8,128)(2,1)S(1)} %slice_bitcast_fusion.refs_0_), channel_id=1, source_target_pairs={{0,1},{1,0},{2,3},{3,2},{4,5},{5,4},{6,7},{7,6},{8,9},{9,8},{10,11... | collective-permute-start | bytes 786440 | tf_op jit(solution)/shard_map/z0y1/ppermute | solution.py:39
  12.0 25.0 %collective-permute-start.3 = (bf16[32,4352]{1,0:T(8,128)(2,1)}, bf16[32,4352]{1,0:T(8,128)(2,1)S(1)}, u32[]{:S(2)}, u32[]{:S(2)}) collective-permute-start(bf16[32,4352]{1,0:T(8,128)(2,1)} %get-tuple-element.60.refs_0_.refs_6_.refs_12_.refs_11_), channel_id=1, source_target_pairs={{0,1},{1,0},{2,3},{3,2},{4,5},{5,4},{6,7},{7,6},{8,9},{9,8},{10,11... | collective-permute-start | bytes 835592 | tf_op jit(solution)/shard_map/z0y1/ppermute | solution.py:39
  22.0 15.0 %collective-permute-start.4 = (bf16[32,4096]{1,0:T(8,128)(2,1)}, bf16[32,4096]{1,0:T(8,128)(2,1)S(1)}, u32[]{:S(2)}, u32[]{:S(2)}) collective-permute-start(bf16[32,4096]{1,0:T(8,128)(2,1)} %get-tuple-element.70.refs_0_.refs_6_), channel_id=1, source_target_pairs={{0,1},{1,0},{2,3},{3,2},{4,5},{5,4},{6,7},{7,6},{8,9},{9,8},{10,11... | collective-permute-start | bytes 786440 | tf_op jit(solution)/shard_map/z0y1/ppermute | solution.py:39
  29.0 19.5 %collective-permute-start.10 = (bf16[32,4096]{1,0:T(8,128)(2,1)}, bf16[32,4096]{1,0:T(8,128)(2,1)S(1)}, u32[]{:S(2)}, u32[]{:S(2)}) collective-permute-start(bf16[32,4096]{1,0:T(8,128)(2,1)} %get-tuple-element.70.refs_0_.refs_6_), channel_id=1, source_target_pairs={{0,4},{1,5},{2,6},{3,7},{4,0},{5,1},{6,2},{7,3},{8,12},{9,13},{10,... | collective-permute-start | bytes 786440 | tf_op jit(solution)/shard_map/z2y0/ppermute | solution.py:39
  34.9 19.0 %collective-permute-start.9 = (bf16[32,4096]{1,0:T(8,128)(2,1)}, bf16[32,4096]{1,0:T(8,128)(2,1)S(1)}, u32[]{:S(2)}, u32[]{:S(2)}) collective-permute-start(bf16[32,4096]{1,0:T(8,128)(2,1)} %get-tuple-element.70.refs_0_.refs_6_), channel_id=1, source_target_pairs={{0,6},{1,7},{2,0},{3,1},{4,2},{5,3},{6,4},{7,5},{8,14},{9,15},{10,... | collective-permute-start | bytes 786440 | tf_op jit(solution)/shard_map/z3y0/ppermute | solution.py:39
  35.4 18.5 %collective-permute-start.8 = (bf16[32,4096]{1,0:T(8,128)(2,1)}, bf16[32,4096]{1,0:T(8,128)(2,1)S(1)}, u32[]{:S(2)}, u32[]{:S(2)}) collective-permute-start(bf16[32,4096]{1,0:T(8,128)(2,1)} %get-tuple-element.70.refs_0_.refs_6_), channel_id=1, source_target_pairs={{0,2},{1,3},{2,4},{3,5},{4,6},{5,7},{6,0},{7,1},{8,10},{9,11},{10,... | collective-permute-start | bytes 786440 | tf_op jit(solution)/shard_map/z1y0/ppermute | solution.py:39
  37.0 26.3 %collective-permute-start.6 = (bf16[96,4352]{1,0:T(8,128)(2,1)S(1)}, bf16[96,4352]{1,0:T(8,128)(2,1)}, u32[]{:S(2)}, u32[]{:S(2)}) collective-permute-start(bf16[96,4352]{1,0:T(8,128)(2,1)S(1)} %pad_maximum_fusion), channel_id=1, source_target_pairs={{0,1},{1,0},{2,3},{3,2},{4,5},{5,4},{6,7},{7,6},{8,9},{9,8},{10,11... | collective-permute-start | bytes 2506760 | tf_op jit(solution)/shard_map/z0y1/ppermute | solution.py:39
  54.0 26.3 %collective-permute-start.17 = (bf16[96,4096]{1,0:T(8,128)(2,1)S(1)}, bf16[96,4096]{1,0:T(8,128)(2,1)}, u32[]{:S(2)}, u32[]{:S(2)}) collective-permute-start(bf16[96,4096]{1,0:T(8,128)(2,1)S(1)} %pad_maximum_fusion.1), channel_id=1, source_target_pairs={{0,1},{1,0},{2,3},{3,2},{4,5},{5,4},{6,7},{7,6},{8,9},{9,8},{10,11... | collective-permute-start | bytes 2359304 | tf_op jit(solution)/shard_map/z0y1/ppermute | solution.py:39
  55.6 19.0 %collective-permute-start.13 = (bf16[64,2048]{1,0:T(8,128)(2,1)S(1)}, bf16[64,2048]{1,0:T(8,128)(2,1)S(1)}, u32[]{:S(2)}, u32[]{:S(2)}) collective-permute-start(bf16[64,2048]{1,0:T(8,128)(2,1)S(1)} %slice_bitcast_fusion.refs_0_), channel_id=1, source_target_pairs={{0,4},{1,5},{2,6},{3,7},{4,0},{5,1},{6,2},{7,3},{8,12},{9,13},{10,... | collective-permute-start | bytes 786440 | tf_op jit(solution)/shard_map/z2y0/ppermute | solution.py:39
  63.1 17.2 %collective-permute-start.11 = (bf16[64,2048]{1,0:T(8,128)(2,1)S(1)}, bf16[64,2048]{1,0:T(8,128)(2,1)}, u32[]{:S(2)}, u32[]{:S(2)}) collective-permute-start(bf16[64,2048]{1,0:T(8,128)(2,1)S(1)} %slice_bitcast_fusion.refs_0_), channel_id=1, source_target_pairs={{0,2},{1,3},{2,4},{3,5},{4,6},{5,7},{6,0},{7,1},{8,10},{9,11},{10,... | collective-permute-start | bytes 786440 | tf_op jit(solution)/shard_map/z1y0/ppermute | solution.py:39
  73.9 17.9 %collective-permute-start.7 = (bf16[128,2048]{1,0:T(8,128)(2,1)}, bf16[128,2048]{1,0:T(8,128)(2,1)S(1)}, u32[]{:S(2)}, u32[]{:S(2)}) collective-permute-start(bf16[128,2048]{1,0:T(8,128)(2,1)} %get-tuple-element.64), channel_id=1, source_target_pairs={{0,1},{1,0},{2,3},{3,2},{4,5},{5,4},{6,7},{7,6},{8,9},{9,8},{10,11... | collective-permute-start | bytes 1572872 | tf_op jit(solution)/shard_map/z0y-1/ppermute | solution.py:39
  92.0 18.0 %collective-permute-start.14 = (bf16[32,2048]{1,0:T(8,128)(2,1)S(1)}, bf16[32,2048]{1,0:T(8,128)(2,1)S(1)}, u32[]{:S(2)}, u32[]{:S(2)}) collective-permute-start(bf16[32,2048]{1,0:T(8,128)(2,1)S(1)} %get-tuple-element.67), channel_id=1, source_target_pairs={{0,6},{1,7},{2,0},{3,1},{4,2},{5,3},{6,4},{7,5},{8,14},{9,15},{10,... | collective-permute-start | bytes 393224 | tf_op jit(solution)/shard_map/z-1y0/ppermute | solution.py:39
  93.4 19.5 %collective-permute-start.15 = (bf16[32,2048]{1,0:T(8,128)(2,1)S(1)}, bf16[32,2048]{1,0:T(8,128)(2,1)S(1)}, u32[]{:S(2)}, u32[]{:S(2)}) collective-permute-start(bf16[32,2048]{1,0:T(8,128)(2,1)S(1)} %get-tuple-element.68), channel_id=1, source_target_pairs={{0,2},{1,3},{2,4},{3,5},{4,6},{5,7},{6,0},{7,1},{8,10},{9,11},{10,... | collective-permute-start | bytes 393224 | tf_op jit(solution)/shard_map/z-3y0/ppermute | solution.py:39
  95.1 18.8 %collective-permute-start.16 = (bf16[32,2048]{1,0:T(8,128)(2,1)S(1)}, bf16[32,2048]{1,0:T(8,128)(2,1)S(1)}, u32[]{:S(2)}, u32[]{:S(2)}) collective-permute-start(bf16[32,2048]{1,0:T(8,128)(2,1)S(1)} %get-tuple-element.69), channel_id=1, source_target_pairs={{0,4},{1,5},{2,6},{3,7},{4,0},{5,1},{6,2},{7,3},{8,12},{9,13},{10,... | collective-permute-start | bytes 393224 | tf_op jit(solution)/shard_map/z-2y0/ppermute | solution.py:39
  105.2 15.6 %collective-permute-start.21 = (bf16[32,2048]{1,0:T(8,128)(2,1)S(1)}, bf16[32,2048]{1,0:T(8,128)(2,1)S(1)}, u32[]{:S(2)}, u32[]{:S(2)}) collective-permute-start(bf16[32,2048]{1,0:T(8,128)(2,1)S(1)} %get-tuple-element.141), channel_id=1, source_target_pairs={{0,4},{1,5},{2,6},{3,7},{4,0},{5,1},{6,2},{7,3},{8,12},{9,13},{10,... | collective-permute-start | bytes 393224 | tf_op jit(solution)/shard_map/z-2y0/ppermute | solution.py:39
  112.9 18.9 %collective-permute-start.22 = (bf16[192,2048]{1,0:T(8,128)(2,1)S(1)}, bf16[192,2048]{1,0:T(8,128)(2,1)S(1)}, u32[]{:S(2)}, u32[]{:S(2)}) collective-permute-start(bf16[192,2048]{1,0:T(8,128)(2,1)S(1)} %pad_maximum_fusion.2), channel_id=1, source_target_pairs={{0,1},{1,0},{2,3},{3,2},{4,5},{5,4},{6,7},{7,6},{8,9},{9,8},{10,11... | collective-permute-start | bytes 2359304 | tf_op jit(solution)/shard_map/z0y1/ppermute | solution.py:39
  130.8 17.3 %collective-permute-start.36 = (bf16[128,2048]{1,0:T(8,128)(2,1)S(1)}, bf16[128,2048]{1,0:T(8,128)(2,1)S(1)}, u32[]{:S(2)}, u32[]{:S(2)}) collective-permute-start(bf16[128,2048]{1,0:T(8,128)(2,1)S(1)} %pad_maximum_fusion.4), channel_id=1, source_target_pairs={{0,1},{1,0},{2,3},{3,2},{4,5},{5,4},{6,7},{7,6},{8,9},{9,8},{10,11... | collective-permute-start | bytes 1572872 | tf_op jit(solution)/shard_map/z0y1/ppermute | solution.py:39
  172.3 14.9 %collective-permute-start.28 = (bf16[128,2048]{1,0:T(8,128)(2,1)}, bf16[128,2048]{1,0:T(8,128)(2,1)S(1)}, u32[]{:S(2)}, u32[]{:S(2)}) collective-permute-start(bf16[128,2048]{1,0:T(8,128)(2,1)} %get-tuple-element.82), channel_id=1, source_target_pairs={{0,1},{1,0},{2,3},{3,2},{4,5},{5,4},{6,7},{7,6},{8,9},{9,8},{10,11... | collective-permute-start | bytes 1572872 | tf_op jit(solution)/shard_map/z0y-1/ppermute | solution.py:39
  173.9 15.5 %collective-permute-start.38 = (bf16[32,2048]{1,0:T(8,128)(2,1)S(1)}, bf16[32,2048]{1,0:T(8,128)(2,1)S(1)}, u32[]{:S(2)}, u32[]{:S(2)}) collective-permute-start(bf16[32,2048]{1,0:T(8,128)(2,1)S(1)} %get-tuple-element.132), channel_id=1, source_target_pairs={{0,6},{1,7},{2,0},{3,1},{4,2},{5,3},{6,4},{7,5},{8,14},{9,15},{10,... | collective-permute-start | bytes 393224 | tf_op jit(solution)/shard_map/z-1y0/ppermute | solution.py:39
  174.6 15.9 %collective-permute-start.40 = (bf16[32,2048]{1,0:T(8,128)(2,1)S(1)}, bf16[32,2048]{1,0:T(8,128)(2,1)S(1)}, u32[]{:S(2)}, u32[]{:S(2)}) collective-permute-start(bf16[32,2048]{1,0:T(8,128)(2,1)S(1)} %get-tuple-element.133), channel_id=1, source_target_pairs={{0,4},{1,5},{2,6},{3,7},{4,0},{5,1},{6,2},{7,3},{8,12},{9,13},{10,... | collective-permute-start | bytes 393224 | tf_op jit(solution)/shard_map/z-2y0/ppermute | solution.py:39
  187.4 15.0 %collective-permute-start.29 = (bf16[32,2048]{1,0:T(8,128)(2,1)S(1)}, bf16[32,2048]{1,0:T(8,128)(2,1)S(1)}, u32[]{:S(2)}, u32[]{:S(2)}) collective-permute-start(bf16[32,2048]{1,0:T(8,128)(2,1)S(1)} %get-tuple-element.129), channel_id=1, source_target_pairs={{0,6},{1,7},{2,0},{3,1},{4,2},{5,3},{6,4},{7,5},{8,14},{9,15},{10,... | collective-permute-start | bytes 393224 | tf_op jit(solution)/shard_map/z-1y0/ppermute | solution.py:39
  (67 other events, 892.7 us)

commit v5 on v4

--- a/solution.py
+++ b/solution.py
@@ -113,7 +113,7 @@
     x_hbm, c_hbm = take(2)
     values_hbm, outs = take(3), take(count)
     weights, values = take(3), take(3)
-    x, c, g, gate, up, back, total_out, x_sem, c_sem, g_sem, w_sem, v_sem, out_sem = refs
+    x, c, g, gate, up, total_out, x_sem, c_sem, g_sem, w_sem, v_sem, out_sem = refs
     gate_w, up_w, down_w = weights
     grad_gate, grad_up, hidden = values
     local, depth, width = gate_w.shape
@@ -175,14 +175,13 @@
         if e == local - 1:
             for i in range(3):
                 write(values[i], values_hbm[i], v_sem.at[i])
-        for d in tiles(depth):
-            total = dot(grad_gate[:, columns], gate_w[e, d, :], NT)
-            total = total + dot(grad_up[:, columns], up_w[e, d, :], NT)
-            if e:
-                total = total + back[:, d]
-            if e < local - 1:
-                back[:, d] = total
-                continue
+        for d in tiles(depth) if e == local - 1 else ():
+            total = None
+            for part in range(local):
+                columns = slice(part * width, (part + 1) * width)
+                for grad, weight_of in ((grad_gate, gate_w), (grad_up, up_w)):
+                    term = dot(grad[:, columns], weight_of[part, d, :], NT)
+                    total = term if total is None else total + term
             total_out[:, d] = total.astype(BF16)
             if d.stop in (depth // 2, depth):
                 side = slice(d.stop - depth // 2, d.stop)
@@ -210,7 +209,7 @@
         + [pltpu.VMEM((tokens, depth), BF16)] * 2
         + [pltpu.VMEM((tokens, lanes), BF16)]
         + [pltpu.VMEM((tokens, width), F32)] * 2
-        + [pltpu.VMEM((tokens, depth), F32), pltpu.VMEM((tokens, depth), BF16)]
+        + [pltpu.VMEM((tokens, depth), BF16)]
         + [pltpu.SemaphoreType.DMA((tokens // place[0],)) for place in places]
         + [pltpu.SemaphoreType.DMA((3 * local,)), pltpu.SemaphoreType.DMA((5,))]
         + [pltpu.SemaphoreType.DMA((count, 2))],
@@ -379,16 +378,16 @@
     straight = lambda link, move, *x: move(*x)
     a, b = halves
     along_z = lambda x: grid.along_z(x)[1:]
-    ya, yb, yx = grid.near(a0), grid.near(b0), grid.near(second_in)
+    ya, yx = grid.near(a0), grid.near(second_in)
     za = turn("z", along_z, a0)
-    fa = grid.near(after(fuse(za), ya, yb, yx))
+    fa = grid.near(after(fuse(za), ya, yx))
     zb = turn("z", along_z, b0)
     gate_blocks = [a0] + za + mix(ya, fa)
-    fb = grid.near(fuse(zb))
+    fb = grid.near(fuse([b0] + zb))
     zx = turn("z", along_z, second_in)
     back_a = early_rows(0, gate_blocks)
     own_a, sums_a = grid.reduce_y(back_a)
-    back_b = early_rows(1, after([b0] + zb + mix(yb, fb), zx))
+    back_b = early_rows(1, after([b0] + zb + fb, zx))
     total_a = grid.reduce_z(own_a, sums_a, turn)
     fx = grid.near(after(fuse(zx), back_b))
     own_b, sums_b = grid.reduce_y(back_b)

time: 206 us -> 206 us (level)
  waiting for transfers between devices: 57.8 us -> 63.7 us
  starting transfers between devices: 72.7 us -> 67 us
    ppermute x33 -> x32, waiting for transfers between devices: 42.3 us -> 48.2 us  [move(): return lax.ppermute(x, 'expert', self.pairs(dz, dy))]
    ppermute x33 -> x32, starting transfers between devices: 63.3 us -> 57.7 us  [move(): return lax.ppermute(x, 'expert', self.pairs(dz, dy))]
  transfers between devices with their start and end apart: 41 -> 40, of which waited for: 13 -> 16; matrix products, arithmetic and copies ran while one was open for 2% -> 2% of each run, Pallas kernels for 30% -> 30%
where the time goes in v5:
time: 206 us; the launch traced here: 204 us
  starting transfers between devices  67 us (33%)
  waiting for transfers between devices  63.7 us (31%)
  Pallas kernels  63.4 us (31%)
  local copies, waits for them, and re-layouts  4.31 us (2%)
  other arithmetic  3.72 us (2%)
    ppermute x32, starting transfers between devices, move(): return lax.ppermute(x, 'expert', self.pairs(dz, dy))  57.7 us
    ppermute x32, waiting for transfers between devices, move(): return lax.ppermute(x, 'expert', self.pairs(dz, dy))  48.2 us
    pallas_call x4, Pallas kernels, on_core(): pl.pallas_call(kernel, in_specs=[pl.BlockSpec(memory_space=pltpu.SMEM)] *...  42.5 us
    pallas_call x2, Pallas kernels, outer(): pl.pallas_call(functools.partial(outer_kernel, len(lefts), count), in_spe...  18.3 us
    ppermute x8, waiting for transfers between devices, move_down(): return lax.ppermute(x, ('section', 'expert'), pairs)  15.4 us
    ppermute x8, starting transfers between devices, move_down(): return lax.ppermute(x, ('section', 'expert'), pairs)  9.34 us
  transfers between devices with their start and end apart: 40, of which 16 were waited for; matrix products, arithmetic and copies ran while one was open for 2% of the time, Pallas kernels for 30%

profile of v5, /device:TPU:0, one launch (start us, length us, event | category | flops | bytes accessed | tf_op | source)
XLA Modules:
  0.0 203.9 jit_solution(2219654002987224627)
XLA Ops:
  0.6 2.6 %payloads.1 = (bf16[32,4352]{1,0:T(8,128)(2,1)}, bf16[32,4096]{1,0:T(8,128)(2,1)}) custom-call(s32[1,10,2,64]{3,2,1,0:T(2,128)} %bitcast.23, f32[1,10,2,64]{3,2,1,0:T(2,128)} %bitcast.24, bf16[1,2,64,2048]{3,2,1,0:T(8,128)(2,1)} %x_in.1, bf16[1,64,2048]{2,1,0:T(8,128)(2,1)} %c_in.1), custom_call_target="tpu_custom_call" | custom-call | tf_op jit(solution)/shard_map/payloads/pallas_call | solution.py:306
  3.3 4.1 %collective-permute-start.2 = (bf16[32,4352]{1,0:T(8,128)(2,1)}, bf16[32,4352]{1,0:T(8,128)(2,1)S(1)}, u32[]{:S(2)}, u32[]{:S(2)}) collective-permute-start(bf16[32,4352]{1,0:T(8,128)(2,1)} %get-tuple-element.59.refs_0_.refs_6_.refs_12_.refs_10_.refs_11_), channel_id=1, source_target_pairs={{0,4},{1,5},{2,6},{3,7},{4,0},{5,1},{6,2},{7,3},{8,12},{9,13},{10,... | collective-permute-start | bytes 835592 | tf_op jit(solution)/shard_map/z2y0/ppermute | solution.py:39
  12.5 9.5 %collective-permute-done.2.refs_3_.refs_9_.refs_15_.refs_13_.refs_14_ = bf16[32,4352]{1,0:T(8,128)(2,1)S(1)} collective-permute-done((bf16[32,4352]{1,0:T(8,128)(2,1)}, bf16[32,4352]{1,0:T(8,128)(2,1)S(1)}, u32[]{:S(2)}, u32[]{:S(2)}) %collective-permute-start.2) | collective-permute-done | bytes 278560 | tf_op jit(solution)/shard_map/z2y0/ppermute | solution.py:39
  22.0 5.4 %collective-permute-done.refs_1_.refs_7_.refs_13_.refs_11_.refs_12_ = bf16[32,4352]{1,0:T(8,128)(2,1)S(1)} collective-permute-done((bf16[32,4352]{1,0:T(8,128)(2,1)}, bf16[32,4352]{1,0:T(8,128)(2,1)S(1)}, u32[]{:S(2)}, u32[]{:S(2)}) %collective-permute-start) | collective-permute-done | bytes 278560 | tf_op jit(solution)/shard_map/z1y0/ppermute | solution.py:39
  27.4 7.4 %collective-permute-start.9 = (bf16[32,4096]{1,0:T(8,128)(2,1)}, bf16[32,4096]{1,0:T(8,128)(2,1)S(1)}, u32[]{:S(2)}, u32[]{:S(2)}) collective-permute-start(bf16[32,4096]{1,0:T(8,128)(2,1)} %get-tuple-element.69.refs_0_.refs_5_), channel_id=1, source_target_pairs={{0,4},{1,5},{2,6},{3,7},{4,0},{5,1},{6,2},{7,3},{8,12},{9,13},{10,... | collective-permute-start | bytes 786440 | tf_op jit(solution)/shard_map/z2y0/ppermute | solution.py:39
  38.6 9.9 %collective-permute-done.9.refs_3_.refs_8_ = bf16[32,4096]{1,0:T(8,128)(2,1)S(1)} collective-permute-done((bf16[32,4096]{1,0:T(8,128)(2,1)}, bf16[32,4096]{1,0:T(8,128)(2,1)S(1)}, u32[]{:S(2)}, u32[]{:S(2)}) %collective-permute-start.9) | collective-permute-done | bytes 262176 | tf_op jit(solution)/shard_map/z2y0/ppermute | solution.py:39
  48.5 5.4 %collective-permute-done.8.refs_2_.refs_7_ = bf16[32,4096]{1,0:T(8,128)(2,1)S(1)} collective-permute-done((bf16[32,4096]{1,0:T(8,128)(2,1)}, bf16[32,4096]{1,0:T(8,128)(2,1)S(1)}, u32[]{:S(2)}, u32[]{:S(2)}) %collective-permute-start.8) | collective-permute-done | bytes 262176 | tf_op jit(solution)/shard_map/z3y0/ppermute | solution.py:39
  55.6 4.3 %collective-permute-start.12 = (bf16[64,2048]{1,0:T(8,128)(2,1)S(1)}, bf16[64,2048]{1,0:T(8,128)(2,1)S(1)}, u32[]{:S(2)}, u32[]{:S(2)}) collective-permute-start(bf16[64,2048]{1,0:T(8,128)(2,1)S(1)} %slice_bitcast_fusion.refs_0_), channel_id=1, source_target_pairs={{0,4},{1,5},{2,6},{3,7},{4,0},{5,1},{6,2},{7,3},{8,12},{9,13},{10,... | collective-permute-start | bytes 786440 | tf_op jit(solution)/shard_map/z2y0/ppermute | solution.py:39
  59.9 3.3 %collective-permute-start.11 = (bf16[64,2048]{1,0:T(8,128)(2,1)S(1)}, bf16[64,2048]{1,0:T(8,128)(2,1)}, u32[]{:S(2)}, u32[]{:S(2)}) collective-permute-start(bf16[64,2048]{1,0:T(8,128)(2,1)S(1)} %slice_bitcast_fusion.refs_0_), channel_id=1, source_target_pairs={{0,6},{1,7},{2,0},{3,1},{4,2},{5,3},{6,4},{7,5},{8,14},{9,15},{10,... | collective-permute-start | bytes 786440 | tf_op jit(solution)/shard_map/z3y0/ppermute | solution.py:39
  63.4 10.5 %expert_rows.4 = (bf16[256,2048]{1,0:T(8,128)(2,1)}, bf16[256,2048]{1,0:T(8,128)(2,1)}, bf16[256,1024]{1,0:T(8,128)(2,1)}, bf16[256,1024]{1,0:T(8,128)(2,1)}, bf...) custom-call(s32[1]{0:T(128)} %bitcast.1.me, ...), custom_call_target="tpu_custom_call" | custom-call | flops 5368709120 | tf_op jit(solution)/shard_map/expert_rows/pallas_call | solution.py:75
  74.6 5.8 %collective-permute-done.10.refs_1_ = bf16[64,2048]{1,0:T(8,128)(2,1)} collective-permute-done((bf16[64,2048]{1,0:T(8,128)(2,1)S(1)}, bf16[64,2048]{1,0:T(8,128)(2,1)}, u32[]{:S(2)}, u32[]{:S(2)}) %collective-permute-start.10) | collective-permute-done | bytes 262176 | tf_op jit(solution)/shard_map/z1y0/ppermute | solution.py:39
  80.9 10.5 %expert_rows.5 = (bf16[256,2048]{1,0:T(8,128)(2,1)}, bf16[256,2048]{1,0:T(8,128)(2,1)}, bf16[256,1024]{1,0:T(8,128)(2,1)}, bf16[256,1024]{1,0:T(8,128)(2,1)}, bf...) custom-call(s32[1]{0:T(128)} %bitcast.1.me, ...), custom_call_target="tpu_custom_call" | custom-call | flops 5368709120 | tf_op jit(solution)/shard_map/expert_rows/pallas_call | solution.py:75
  93.2 2.7 %collective-permute-start.13 = (bf16[32,2048]{1,0:T(8,128)(2,1)S(1)}, bf16[32,2048]{1,0:T(8,128)(2,1)S(1)}, u32[]{:S(2)}, u32[]{:S(2)}) collective-permute-start(bf16[32,2048]{1,0:T(8,128)(2,1)S(1)} %get-tuple-element.66), channel_id=1, source_target_pairs={{0,6},{1,7},{2,0},{3,1},{4,2},{5,3},{6,4},{7,5},{8,14},{9,15},{10,... | collective-permute-start | bytes 393224 | tf_op jit(solution)/shard_map/z-1y0/ppermute | solution.py:39
  99.2 4.4 %collective-permute-done.17 = bf16[128,2048]{1,0:T(8,128)(2,1)S(1)} collective-permute-done((bf16[128,2048]{1,0:T(8,128)(2,1)}, bf16[128,2048]{1,0:T(8,128)(2,1)S(1)}, u32[]{:S(2)}, u32[]{:S(2)}) %collective-permute-start.17) | collective-permute-done | bytes 524320 | tf_op jit(solution)/shard_map/z0y-1/ppermute | solution.py:39
  105.1 4.8 %collective-permute-start.20 = (bf16[32,2048]{1,0:T(8,128)(2,1)S(1)}, bf16[32,2048]{1,0:T(8,128)(2,1)S(1)}, u32[]{:S(2)}, u32[]{:S(2)}) collective-permute-start(bf16[32,2048]{1,0:T(8,128)(2,1)S(1)} %get-tuple-element.139), channel_id=1, source_target_pairs={{0,4},{1,5},{2,6},{3,7},{4,0},{5,1},{6,2},{7,3},{8,12},{9,13},{10,... | collective-permute-start | bytes 393224 | tf_op jit(solution)/shard_map/z-2y0/ppermute | solution.py:39
  113.9 6.9 %collective-permute-done.20 = bf16[32,2048]{1,0:T(8,128)(2,1)S(1)} collective-permute-done((bf16[32,2048]{1,0:T(8,128)(2,1)S(1)}, bf16[32,2048]{1,0:T(8,128)(2,1)S(1)}, u32[]{:S(2)}, u32[]{:S(2)}) %collective-permute-start.20) | collective-permute-done | bytes 131104 | tf_op jit(solution)/shard_map/z-2y0/ppermute | solution.py:39
  124.1 4.2 %collective-permute-done.34.refs_9_ = bf16[32,2048]{1,0:T(8,128)(2,1)S(1)} collective-permute-done((bf16[32,2048]{1,0:T(8,128)(2,1)S(1)}, bf16[32,2048]{1,0:T(8,128)(2,1)S(1)}, u32[]{:S(2)}, u32[]{:S(2)}) %collective-permute-start.34) | collective-permute-done | bytes 131104 | tf_op jit(solution)/shard_map/down_z2/ppermute | solution.py:49
  132.0 3.5 %collective-permute-start.25 = (bf16[32,2048]{1,0:T(8,128)(2,1)S(1)}, bf16[32,2048]{1,0:T(8,128)(2,1)S(1)}, u32[]{:S(2)}, u32[]{:S(2)}) collective-permute-start(bf16[32,2048]{1,0:T(8,128)(2,1)S(1)} %get-tuple-element.78), channel_id=1, source_target_pairs={{0,28},{1,29},{2,30},{3,31},{4,24},{5,25},{6,26},{7,27},{8,4},{9,5... | collective-permute-start | bytes 393224 | tf_op jit(solution)/shard_map/down_z2/ppermute | solution.py:49
  139.2 2.9 %collective-permute-done.24.refs_8_ = bf16[32,2048]{1,0:T(8,128)(2,1)S(1)} collective-permute-done((bf16[32,2048]{1,0:T(8,128)(2,1)S(1)}, bf16[32,2048]{1,0:T(8,128)(2,1)S(1)}, u32[]{:S(2)}, u32[]{:S(2)}) %collective-permute-start.24) | collective-permute-done | bytes 131104 | tf_op jit(solution)/shard_map/down_z3/ppermute | solution.py:49
  142.0 4.8 %collective-permute-done.23.refs_7_ = bf16[32,2048]{1,0:T(8,128)(2,1)S(1)} collective-permute-done((bf16[32,2048]{1,0:T(8,128)(2,1)S(1)}, bf16[32,2048]{1,0:T(8,128)(2,1)S(1)}, u32[]{:S(2)}, u32[]{:S(2)}) %collective-permute-start.23) | collective-permute-done | bytes 131104 | tf_op jit(solution)/shard_map/down_z1/ppermute | solution.py:49
  149.0 10.5 %expert_rows.7 = (bf16[256,2048]{1,0:T(8,128)(2,1)}, bf16[256,2048]{1,0:T(8,128)(2,1)}, bf16[256,1024]{1,0:T(8,128)(2,1)}, bf16[256,1024]{1,0:T(8,128)(2,1)}, bf...) custom-call(s32[1]{0:T(128)} %bitcast.1.me, bf16[64,2048]{1,0:T(8,128)(2,1)} %copy-done.33, ...), custom_call_target="tpu_custom_call" | custom-call | flops 5368709120 | tf_op jit(solution)/shard_map/expert_rows/pallas_call | solution.py:75
  161.3 10.9 %expert_rows.6 = (bf16[256,2048]{1,0:T(8,128)(2,1)}, bf16[256,2048]{1,0:T(8,128)(2,1)}, bf16[256,1024]{1,0:T(8,128)(2,1)}, bf16[256,1024]{1,0:T(8,128)(2,1)}, bf...) custom-call(s32[1]{0:T(128)} %bitcast.1.me, bf16[64,2048]{1,0:T(8,128)(2,1)} %copy-done.33, ...), custom_call_target="tpu_custom_call" | custom-call | flops 5368709120 | tf_op jit(solution)/shard_map/expert_rows/pallas_call | solution.py:75
  180.7 6.6 %outer_down.1 = bf16[2,512,2048]{2,1,0:T(8,128)(2,1)} custom-call(bf16[256,1024]{1,0:T(8,128)(2,1)S(1)} %copy-done.4, bf16[256,1024]{1,0:T(8,128)(2,1)S(1)} %copy-done.9, bf16[256,1024]{1,0:T(8,128)(2,1)S(1)} %copy-done.19, bf16[256,1024]{1,0:T(8,128)(2,1)S(1)} %copy-done.18, bf16[256,2048]{1,0:T(8,128)(2,1)S(1)} %copy-done.1, ...), custom_call_target="tpu_custom_call" | custom-call | flops 4294967296 | tf_op jit(solution)/shard_map/outer_down/pallas_call | solution.py:244
  190.8 11.7 %outer_inputs.1 = (bf16[2,2048,512]{2,1,0:T(8,128)(2,1)}, bf16[2,2048,512]{2,1,0:T(8,128)(2,1)}) custom-call(bf16[256,2048]{1,0:T(8,128)(2,1)S(1)} %copy-done, bf16[256,2048]{1,0:T(8,128)(2,1)S(1)} %copy-done.5, bf16[256,2048]{1,0:T(8,128)(2,1)S(1)} %copy-done.11, bf16[256,2048]{1,0:T(8,128)(2,1)S(1)} %copy-done.10, bf16[256,1024]{1,0:T(8,128)(2,1)S(1)} %copy-done.2, ...), custom_call_target="tpu_custom_call" | custom-call | flops 8589934592 | tf_op jit(solution)/shard_map/outer_inputs/pallas_call | solution.py:244
  (180 shorter events, 49.5 us)
Async XLA Ops:
  3.3 18.7 %collective-permute-start.2 = (bf16[32,4352]{1,0:T(8,128)(2,1)}, bf16[32,4352]{1,0:T(8,128)(2,1)S(1)}, u32[]{:S(2)}, u32[]{:S(2)}) collective-permute-start(bf16[32,4352]{1,0:T(8,128)(2,1)} %get-tuple-element.59.refs_0_.refs_6_.refs_12_.refs_10_.refs_11_), channel_id=1, source_target_pairs={{0,4},{1,5},{2,6},{3,7},{4,0},{5,1},{6,2},{7,3},{8,12},{9,13},{10,... | collective-permute-start | bytes 835592 | tf_op jit(solution)/shard_map/z2y0/ppermute | solution.py:39
  7.4 14.6 %collective-permute-start.1 = (bf16[32,4352]{1,0:T(8,128)(2,1)}, bf16[32,4352]{1,0:T(8,128)(2,1)S(1)}, u32[]{:S(2)}, u32[]{:S(2)}) collective-permute-start(bf16[32,4352]{1,0:T(8,128)(2,1)} %get-tuple-element.59.refs_0_.refs_6_.refs_12_.refs_10_.refs_11_), channel_id=1, source_target_pairs={{0,6},{1,7},{2,0},{3,1},{4,2},{5,3},{6,4},{7,5},{8,14},{9,15},{10,... | collective-permute-start | bytes 835592 | tf_op jit(solution)/shard_map/z3y0/ppermute | solution.py:39
  8.7 18.7 %collective-permute-start = (bf16[32,4352]{1,0:T(8,128)(2,1)}, bf16[32,4352]{1,0:T(8,128)(2,1)S(1)}, u32[]{:S(2)}, u32[]{:S(2)}) collective-permute-start(bf16[32,4352]{1,0:T(8,128)(2,1)} %get-tuple-element.59.refs_0_.refs_6_.refs_12_.refs_10_.refs_11_), channel_id=1, source_target_pairs={{0,2},{1,3},{2,4},{3,5},{4,6},{5,7},{6,0},{7,1},{8,10},{9,11},{10,... | collective-permute-start | bytes 835592 | tf_op jit(solution)/shard_map/z1y0/ppermute | solution.py:39
  9.4 27.5 %collective-permute-start.3 = (bf16[32,4352]{1,0:T(8,128)(2,1)}, bf16[32,4352]{1,0:T(8,128)(2,1)S(1)}, u32[]{:S(2)}, u32[]{:S(2)}) collective-permute-start(bf16[32,4352]{1,0:T(8,128)(2,1)} %get-tuple-element.59.refs_0_.refs_6_.refs_12_.refs_10_.refs_11_), channel_id=1, source_target_pairs={{0,1},{1,0},{2,3},{3,2},{4,5},{5,4},{6,7},{7,6},{8,9},{9,8},{10,11... | collective-permute-start | bytes 835592 | tf_op jit(solution)/shard_map/z0y1/ppermute | solution.py:39
  11.9 25.0 %collective-permute-start.4 = (bf16[64,2048]{1,0:T(8,128)(2,1)S(1)}, bf16[64,2048]{1,0:T(8,128)(2,1)S(1)}, u32[]{:S(2)}, u32[]{:S(2)}) collective-permute-start(bf16[64,2048]{1,0:T(8,128)(2,1)S(1)} %slice_bitcast_fusion.refs_0_), channel_id=1, source_target_pairs={{0,1},{1,0},{2,3},{3,2},{4,5},{5,4},{6,7},{7,6},{8,9},{9,8},{10,11... | collective-permute-start | bytes 786440 | tf_op jit(solution)/shard_map/z0y1/ppermute | solution.py:39
  27.4 21.1 %collective-permute-start.9 = (bf16[32,4096]{1,0:T(8,128)(2,1)}, bf16[32,4096]{1,0:T(8,128)(2,1)S(1)}, u32[]{:S(2)}, u32[]{:S(2)}) collective-permute-start(bf16[32,4096]{1,0:T(8,128)(2,1)} %get-tuple-element.69.refs_0_.refs_5_), channel_id=1, source_target_pairs={{0,4},{1,5},{2,6},{3,7},{4,0},{5,1},{6,2},{7,3},{8,12},{9,13},{10,... | collective-permute-start | bytes 786440 | tf_op jit(solution)/shard_map/z2y0/ppermute | solution.py:39
  34.9 19.0 %collective-permute-start.8 = (bf16[32,4096]{1,0:T(8,128)(2,1)}, bf16[32,4096]{1,0:T(8,128)(2,1)S(1)}, u32[]{:S(2)}, u32[]{:S(2)}) collective-permute-start(bf16[32,4096]{1,0:T(8,128)(2,1)} %get-tuple-element.69.refs_0_.refs_5_), channel_id=1, source_target_pairs={{0,6},{1,7},{2,0},{3,1},{4,2},{5,3},{6,4},{7,5},{8,14},{9,15},{10,... | collective-permute-start | bytes 786440 | tf_op jit(solution)/shard_map/z3y0/ppermute | solution.py:39
  35.4 18.5 %collective-permute-start.7 = (bf16[32,4096]{1,0:T(8,128)(2,1)}, bf16[32,4096]{1,0:T(8,128)(2,1)S(1)}, u32[]{:S(2)}, u32[]{:S(2)}) collective-permute-start(bf16[32,4096]{1,0:T(8,128)(2,1)} %get-tuple-element.69.refs_0_.refs_5_), channel_id=1, source_target_pairs={{0,2},{1,3},{2,4},{3,5},{4,6},{5,7},{6,0},{7,1},{8,10},{9,11},{10,... | collective-permute-start | bytes 786440 | tf_op jit(solution)/shard_map/z1y0/ppermute | solution.py:39
  37.0 26.3 %collective-permute-start.5 = (bf16[96,4352]{1,0:T(8,128)(2,1)S(1)}, bf16[96,4352]{1,0:T(8,128)(2,1)}, u32[]{:S(2)}, u32[]{:S(2)}) collective-permute-start(bf16[96,4352]{1,0:T(8,128)(2,1)S(1)} %pad_maximum_fusion.1), channel_id=1, source_target_pairs={{0,1},{1,0},{2,3},{3,2},{4,5},{5,4},{6,7},{7,6},{8,9},{9,8},{10,11... | collective-permute-start | bytes 2506760 | tf_op jit(solution)/shard_map/z0y1/ppermute | solution.py:39
  54.0 26.9 %collective-permute-start.16 = (bf16[128,4096]{1,0:T(8,128)(2,1)S(1)}, bf16[128,4096]{1,0:T(8,128)(2,1)}, u32[]{:S(2)}, u32[]{:S(2)}) collective-permute-start(bf16[128,4096]{1,0:T(8,128)(2,1)S(1)} %pad_maximum_fusion), channel_id=1, source_target_pairs={{0,1},{1,0},{2,3},{3,2},{4,5},{5,4},{6,7},{7,6},{8,9},{9,8},{10,11... | collective-permute-start | bytes 3145736 | tf_op jit(solution)/shard_map/z0y1/ppermute | solution.py:39
  55.6 19.0 %collective-permute-start.12 = (bf16[64,2048]{1,0:T(8,128)(2,1)S(1)}, bf16[64,2048]{1,0:T(8,128)(2,1)S(1)}, u32[]{:S(2)}, u32[]{:S(2)}) collective-permute-start(bf16[64,2048]{1,0:T(8,128)(2,1)S(1)} %slice_bitcast_fusion.refs_0_), channel_id=1, source_target_pairs={{0,4},{1,5},{2,6},{3,7},{4,0},{5,1},{6,2},{7,3},{8,12},{9,13},{10,... | collective-permute-start | bytes 786440 | tf_op jit(solution)/shard_map/z2y0/ppermute | solution.py:39
  59.9 14.7 %collective-permute-start.11 = (bf16[64,2048]{1,0:T(8,128)(2,1)S(1)}, bf16[64,2048]{1,0:T(8,128)(2,1)}, u32[]{:S(2)}, u32[]{:S(2)}) collective-permute-start(bf16[64,2048]{1,0:T(8,128)(2,1)S(1)} %slice_bitcast_fusion.refs_0_), channel_id=1, source_target_pairs={{0,6},{1,7},{2,0},{3,1},{4,2},{5,3},{6,4},{7,5},{8,14},{9,15},{10,... | collective-permute-start | bytes 786440 | tf_op jit(solution)/shard_map/z3y0/ppermute | solution.py:39
  63.1 17.2 %collective-permute-start.10 = (bf16[64,2048]{1,0:T(8,128)(2,1)S(1)}, bf16[64,2048]{1,0:T(8,128)(2,1)}, u32[]{:S(2)}, u32[]{:S(2)}) collective-permute-start(bf16[64,2048]{1,0:T(8,128)(2,1)S(1)} %slice_bitcast_fusion.refs_0_), channel_id=1, source_target_pairs={{0,2},{1,3},{2,4},{3,5},{4,6},{5,7},{6,0},{7,1},{8,10},{9,11},{10,... | collective-permute-start | bytes 786440 | tf_op jit(solution)/shard_map/z1y0/ppermute | solution.py:39
  73.9 19.1 %collective-permute-start.6 = (bf16[128,2048]{1,0:T(8,128)(2,1)}, bf16[128,2048]{1,0:T(8,128)(2,1)S(1)}, u32[]{:S(2)}, u32[]{:S(2)}) collective-permute-start(bf16[128,2048]{1,0:T(8,128)(2,1)} %get-tuple-element.62), channel_id=1, source_target_pairs={{0,1},{1,0},{2,3},{3,2},{4,5},{5,4},{6,7},{7,6},{8,9},{9,8},{10,11... | collective-permute-start | bytes 1572872 | tf_op jit(solution)/shard_map/z0y-1/ppermute | solution.py:39
  93.2 16.7 %collective-permute-start.13 = (bf16[32,2048]{1,0:T(8,128)(2,1)S(1)}, bf16[32,2048]{1,0:T(8,128)(2,1)S(1)}, u32[]{:S(2)}, u32[]{:S(2)}) collective-permute-start(bf16[32,2048]{1,0:T(8,128)(2,1)S(1)} %get-tuple-element.66), channel_id=1, source_target_pairs={{0,6},{1,7},{2,0},{3,1},{4,2},{5,3},{6,4},{7,5},{8,14},{9,15},{10,... | collective-permute-start | bytes 393224 | tf_op jit(solution)/shard_map/z-1y0/ppermute | solution.py:39
  95.9 17.1 %collective-permute-start.14 = (bf16[32,2048]{1,0:T(8,128)(2,1)S(1)}, bf16[32,2048]{1,0:T(8,128)(2,1)S(1)}, u32[]{:S(2)}, u32[]{:S(2)}) collective-permute-start(bf16[32,2048]{1,0:T(8,128)(2,1)S(1)} %get-tuple-element.67), channel_id=1, source_target_pairs={{0,2},{1,3},{2,4},{3,5},{4,6},{5,7},{6,0},{7,1},{8,10},{9,11},{10,... | collective-permute-start | bytes 393224 | tf_op jit(solution)/shard_map/z-3y0/ppermute | solution.py:39
  97.8 16.1 %collective-permute-start.15 = (bf16[32,2048]{1,0:T(8,128)(2,1)S(1)}, bf16[32,2048]{1,0:T(8,128)(2,1)S(1)}, u32[]{:S(2)}, u32[]{:S(2)}) collective-permute-start(bf16[32,2048]{1,0:T(8,128)(2,1)S(1)} %get-tuple-element.68), channel_id=1, source_target_pairs={{0,4},{1,5},{2,6},{3,7},{4,0},{5,1},{6,2},{7,3},{8,12},{9,13},{10,... | collective-permute-start | bytes 393224 | tf_op jit(solution)/shard_map/z-2y0/ppermute | solution.py:39
  105.1 15.7 %collective-permute-start.20 = (bf16[32,2048]{1,0:T(8,128)(2,1)S(1)}, bf16[32,2048]{1,0:T(8,128)(2,1)S(1)}, u32[]{:S(2)}, u32[]{:S(2)}) collective-permute-start(bf16[32,2048]{1,0:T(8,128)(2,1)S(1)} %get-tuple-element.139), channel_id=1, source_target_pairs={{0,4},{1,5},{2,6},{3,7},{4,0},{5,1},{6,2},{7,3},{8,12},{9,13},{10,... | collective-permute-start | bytes 393224 | tf_op jit(solution)/shard_map/z-2y0/ppermute | solution.py:39
  113.0 19.0 %collective-permute-start.21 = (bf16[192,2048]{1,0:T(8,128)(2,1)S(1)}, bf16[192,2048]{1,0:T(8,128)(2,1)S(1)}, u32[]{:S(2)}, u32[]{:S(2)}) collective-permute-start(bf16[192,2048]{1,0:T(8,128)(2,1)S(1)} %pad_maximum_fusion.2), channel_id=1, source_target_pairs={{0,1},{1,0},{2,3},{3,2},{4,5},{5,4},{6,7},{7,6},{8,9},{9,8},{10,11... | collective-permute-start | bytes 2359304 | tf_op jit(solution)/shard_map/z0y1/ppermute | solution.py:39
  131.1 17.1 %collective-permute-start.35 = (bf16[128,2048]{1,0:T(8,128)(2,1)S(1)}, bf16[128,2048]{1,0:T(8,128)(2,1)S(1)}, u32[]{:S(2)}, u32[]{:S(2)}) collective-permute-start(bf16[128,2048]{1,0:T(8,128)(2,1)S(1)} %pad_maximum_fusion.4), channel_id=1, source_target_pairs={{0,1},{1,0},{2,3},{3,2},{4,5},{5,4},{6,7},{7,6},{8,9},{9,8},{10,11... | collective-permute-start | bytes 1572872 | tf_op jit(solution)/shard_map/z0y1/ppermute | solution.py:39
  172.2 15.1 %collective-permute-start.27 = (bf16[128,2048]{1,0:T(8,128)(2,1)}, bf16[128,2048]{1,0:T(8,128)(2,1)S(1)}, u32[]{:S(2)}, u32[]{:S(2)}) collective-permute-start(bf16[128,2048]{1,0:T(8,128)(2,1)} %get-tuple-element.80), channel_id=1, source_target_pairs={{0,1},{1,0},{2,3},{3,2},{4,5},{5,4},{6,7},{7,6},{8,9},{9,8},{10,11... | collective-permute-start | bytes 1572872 | tf_op jit(solution)/shard_map/z0y-1/ppermute | solution.py:39
  173.9 15.6 %collective-permute-start.37 = (bf16[32,2048]{1,0:T(8,128)(2,1)S(1)}, bf16[32,2048]{1,0:T(8,128)(2,1)S(1)}, u32[]{:S(2)}, u32[]{:S(2)}) collective-permute-start(bf16[32,2048]{1,0:T(8,128)(2,1)S(1)} %get-tuple-element.130), channel_id=1, source_target_pairs={{0,6},{1,7},{2,0},{3,1},{4,2},{5,3},{6,4},{7,5},{8,14},{9,15},{10,... | collective-permute-start | bytes 393224 | tf_op jit(solution)/shard_map/z-1y0/ppermute | solution.py:39
  174.7 16.0 %collective-permute-start.39 = (bf16[32,2048]{1,0:T(8,128)(2,1)S(1)}, bf16[32,2048]{1,0:T(8,128)(2,1)S(1)}, u32[]{:S(2)}, u32[]{:S(2)}) collective-permute-start(bf16[32,2048]{1,0:T(8,128)(2,1)S(1)} %get-tuple-element.131), channel_id=1, source_target_pairs={{0,4},{1,5},{2,6},{3,7},{4,0},{5,1},{6,2},{7,3},{8,12},{9,13},{10,... | collective-permute-start | bytes 393224 | tf_op jit(solution)/shard_map/z-2y0/ppermute | solution.py:39
  187.6 15.0 %collective-permute-start.28 = (bf16[32,2048]{1,0:T(8,128)(2,1)S(1)}, bf16[32,2048]{1,0:T(8,128)(2,1)S(1)}, u32[]{:S(2)}, u32[]{:S(2)}) collective-permute-start(bf16[32,2048]{1,0:T(8,128)(2,1)S(1)} %get-tuple-element.127), channel_id=1, source_target_pairs={{0,6},{1,7},{2,0},{3,1},{4,2},{5,3},{6,4},{7,5},{8,14},{9,15},{10,... | collective-permute-start | bytes 393224 | tf_op jit(solution)/shard_map/z-1y0/ppermute | solution.py:39
  (65 other events, 887.6 us)
